TPU v7x, 256 devices: a whole 4x4x8 slice. The times are simulated.
256 devices in a mesh: dp: 4 (over y), tensor: 4 (over x), latent: 16 (over z, core).
Axes of the slice: x: 4, y: 4, z: 8, core: 2. Of those that a mesh axis runs over, the one named last changes fastest.
Arguments:
- resid: bfloat16 [1024, 3584], P('dp', ('tensor', 'latent')), may hold values from -6 to 6
- out_grad: bfloat16 [1024, 3584], P('dp', ('tensor', 'latent')), may hold values from -6 to 6
- norm_gain: float32 [3584], replicated, may hold values from 0.25 to 1.75
- w_gate: bfloat16 [3584, 14336], P('dp', ('tensor', 'latent')), may hold values from -0.09375 to 0.09375
- w_up: bfloat16 [3584, 14336], P('dp', ('tensor', 'latent')), may hold values from -0.09375 to 0.09375
- w_down_t: bfloat16 [3584, 14336], P('dp', ('tensor', 'latent')), may hold values from -0.046875 to 0.046875
- decoder: bfloat16 [65536, 3584], P('latent', 'tensor'), may hold values from -0.09375 to 0.09375
- dec_bias: float32 [3584], replicated, may hold values from -5 to 5
- block_ids: int32 [8, 32], P('dp'), may hold values from 0 to 511, as said below
- counts: int32 [8], P('dp'), may hold values from 1 to 32, as said below
- latent_acts: bfloat16 [1024, 4096], P(('dp', 'tensor', 'latent')), may hold values from 0.099609375 to 4
Outputs:
- scores: bfloat16 [1024, 4096], P(('dp', 'tensor', 'latent'))
- error_score: float32 [1024], P(('dp', 'tensor', 'latent'))
Inputs may be any that keep to these rules, and one draw needn't show every extreme that they name: `block_ids`: within a row the ids are distinct; no latent index (id // 32) owns more than 8 of a row's 32 ids, and in every row one owns exactly 8. Slots k < counts[b] are live; 32 is reached in some row of every draw.
All inputs are finite; a program needn't handle non-finite values.
Results may differ from a plain program's by a relative error of at most 0.017.
Values may be sent and summed in bfloat16 or wider, within the bound.
No kernel may reach another device: no remote copies, remote signals or barrier semaphores. Data moves between devices by JAX's collectives and lax.ppermute only.
A program may use at most 64 MiB of HBM per device.

v0:
```python
import math

import jax
import jax.numpy as jnp
from jax import lax
from jax.sharding import PartitionSpec as P

LATENT_BLOCK = 128


def gelu_parts(gate):
    coeff = math.sqrt(2.0 / math.pi)
    inner = coeff * (gate + 0.044715 * gate * gate * gate)
    hyper = jnp.tanh(inner)
    act = 0.5 * gate * (1.0 + hyper)
    slope = 0.5 * (1.0 + hyper) + 0.5 * gate * (1.0 - hyper * hyper) * coeff * (
        1.0 + 3.0 * 0.044715 * gate * gate
    )
    return (act, slope)


def norm_backward(grad_norm, x_hat, root_mean, upstream, norm_gain):
    grad_scaled = grad_norm * norm_gain
    center = jnp.mean(grad_scaled * x_hat, axis=-1, keepdims=True)
    return upstream.astype(jnp.float32) + (grad_scaled - x_hat * center) / root_mean


def on_device(
    resid,
    out_grad,
    norm_gain,
    w_gate,
    w_up,
    w_down_t,
    decoder,
    dec_bias,
    block_ids,
    counts,
    latent_acts,
):
    gate_full, up_full, down_full = (
        lax.all_gather(w_gate, "dp", axis=0, tiled=True),
        lax.all_gather(w_up, "dp", axis=0, tiled=True),
        lax.all_gather(w_down_t, "dp", axis=0, tiled=True),
    )
    x_all, grad_out = (
        lax.all_gather(resid, ("tensor", "latent"), axis=1, tiled=True),
        lax.all_gather(out_grad, ("tensor", "latent"), axis=1, tiled=True),
    )
    x_float = x_all.astype(jnp.float32)
    root_mean = jnp.sqrt(jnp.mean(x_float * x_float, axis=-1, keepdims=True) + 1e-06)
    x_hat = x_float / root_mean
    normed = (x_hat * norm_gain).astype(jnp.bfloat16)
    gate = jnp.dot(normed, gate_full, preferred_element_type=jnp.float32)
    up_value = jnp.dot(normed, up_full, preferred_element_type=jnp.float32)
    grad_a = jnp.dot(grad_out, down_full, preferred_element_type=jnp.float32)
    act, slope = gelu_parts(gate)
    grad_up = (grad_a * act).astype(jnp.bfloat16)
    grad_gate = (grad_a * up_value * slope).astype(jnp.bfloat16)
    group_size = lax.axis_size(("tensor", "latent"))
    tokens_all = x_all.shape[0]
    row_count = tokens_all // group_size
    first_row = lax.axis_index(("tensor", "latent")) * row_count
    dec_cols = decoder.shape[1]
    col_start = lax.axis_index("tensor") * dec_cols
    contract = (((1,), (1,)), ((), ()))

    def own_rows(array):
        return lax.dynamic_slice_in_dim(array, first_row, row_count, 0)

    grad_norm = lax.psum(
        lax.dot_general(grad_gate, gate_full, contract, preferred_element_type=jnp.float32)
        + lax.dot_general(grad_up, up_full, contract, preferred_element_type=jnp.float32),
        ("tensor", "latent"),
    )
    grad_x = norm_backward(grad_norm, x_hat, root_mean, grad_out, norm_gain)
    grad_mine = own_rows(grad_x)
    grad_cols = lax.dynamic_slice_in_dim(grad_x.astype(jnp.bfloat16), col_start, dec_cols, 1)
    block_count = block_ids.shape[0]
    slot_count = block_ids.shape[1]
    block_rows = tokens_all // block_count
    local_blocks = decoder.shape[0] // LATENT_BLOCK
    my_latent = lax.axis_index("latent")
    owner_index = block_ids // local_blocks
    owned = owner_index == my_latent
    local_ids = block_ids % local_blocks
    row_block = (first_row + jnp.arange(row_count, dtype=jnp.int32)) // block_rows
    products = lax.dot_general(grad_cols, decoder, contract, preferred_element_type=jnp.float32)
    products = products.reshape(block_count, block_rows, local_blocks, LATENT_BLOCK)
    select = (
        owned[:, :, None] & (local_ids[:, :, None] == jnp.arange(local_blocks, dtype=jnp.int32))
    ).astype(jnp.float32)
    partial_terms = jnp.einsum("bkm,btmj->btkj", select, products)
    partial_flat = partial_terms.reshape(tokens_all, slot_count * LATENT_BLOCK)
    summed = lax.psum_scatter(partial_flat, ("tensor", "latent"), scatter_dimension=0, tiled=True)
    live_slots = (
        jnp.arange(slot_count, dtype=jnp.int32)[None, :] < counts[row_block][:, None]
    ).astype(jnp.float32)
    live_cols = jnp.repeat(live_slots, LATENT_BLOCK, axis=1)
    score_full = summed * latent_acts.astype(jnp.float32) * live_cols
    x_mine = own_rows(x_float)
    error_score = (
        jnp.sum(grad_mine * (x_mine - dec_bias), axis=-1) - jnp.sum(score_full, axis=-1)
    ) / math.sqrt(x_all.shape[1])
    return (score_full.astype(jnp.bfloat16), error_score)


def solution(mesh):
    return jax.shard_map(
        on_device,
        mesh=mesh,
        in_specs=(
            P("dp", ("tensor", "latent")),
            P("dp", ("tensor", "latent")),
            P(),
            P("dp", ("tensor", "latent")),
            P("dp", ("tensor", "latent")),
            P("dp", ("tensor", "latent")),
            P("latent", "tensor"),
            P(),
            P("dp", None),
            P("dp"),
            P(("dp", "tensor", "latent"), None),
        ),
        out_specs=(P(("dp", "tensor", "latent"), None), P(("dp", "tensor", "latent"))),
        check_vma=False,
    )
```

profile of v0, /device:TPU:1, one launch (start us, length us, event | category | flops | bytes accessed | tf_op | source)
XLA Modules:
  0.0 685.8 jit_solution(1836352508827180140)
XLA Ops:
  7.2 0.0 copy-start
  7.2 0.0 all-gather.10.cloned.1.call-start
  7.2 0.7 all-gather.10.cloned.1.call-update
  7.9 0.0 all-gather.8.cloned.1.call-start
  8.0 0.7 all-gather.8.cloned.1.call-update
  8.7 0.0 all-gather.6.cloned.1.call-start
  8.7 0.7 all-gather.6.cloned.1.call-update
  9.4 0.0 all-gather.14.cloned.1.call-start
  9.4 0.5 all-gather.14.cloned.1.call-update
  10.0 0.0 all-gather.12.cloned.1.call-start
  10.0 0.5 all-gather.12.cloned.1.call-update
  10.6 0.0 all-reduce.4.cloned.1.call-start
  10.6 81.4 %all-gather.10.cloned.1.call-done = bf16[256,3584]{0,1:T(8,128)(2,1)} async-done(((bf16[256,56]{0,1:T(8,128)(2,1)}), bf16[256,3584]{0,1:T(8,128)(2,1)}) %all-gather.10.cloned.1.call-update) | async-done | bytes 1835024 | tf_op jit(solution)/shard_map/all_gather | solution.py:47
  92.0 2.8 copy.18
  94.8 0.0 copy-start.5
  94.8 0.4 multiply_reduce_fusion.1
  95.2 25.3 %all-gather.8.cloned.1.call-done = bf16[3584,224]{0,1:T(8,128)(2,1)} async-done(((bf16[896,224]{0,1:T(8,128)(2,1)}), bf16[3584,224]{0,1:T(8,128)(2,1)}) %all-gather.8.cloned.1.call-update) | async-done | bytes 1605648 | tf_op jit(solution)/shard_map/all_gather | solution.py:44
  120.5 80.1 %all-gather.6.cloned.1.call-done = bf16[256,3584]{0,1:T(8,128)(2,1)} async-done(((bf16[256,56]{0,1:T(8,128)(2,1)}), bf16[256,3584]{0,1:T(8,128)(2,1)}) %all-gather.6.cloned.1.call-update) | async-done | bytes 1835024 | tf_op jit(solution)/shard_map/all_gather | solution.py:48
  200.6 3.3 fusion.49
  203.9 25.1 %all-gather.14.cloned.1.call-done = bf16[3584,224]{0,1:T(8,128)(2,1)} async-done(((bf16[896,224]{0,1:T(8,128)(2,1)}), bf16[3584,224]{0,1:T(8,128)(2,1)}) %all-gather.14.cloned.1.call-update) | async-done | bytes 1605648 | tf_op jit(solution)/shard_map/all_gather | solution.py:42
  229.0 2.9 fusion.5
  231.9 28.1 %all-gather.12.cloned.1.call-done = bf16[3584,224]{0,1:T(8,128)(2,1)} async-done(((bf16[896,224]{0,1:T(8,128)(2,1)}), bf16[3584,224]{0,1:T(8,128)(2,1)}) %all-gather.12.cloned.1.call-update) | async-done | bytes 1605648 | tf_op jit(solution)/shard_map/all_gather | solution.py:43
  260.0 6.4 fusion.4
  266.4 4.9 convolution_add_fusion
  271.3 0.0 all-reduce.4.cloned.1.call-update
  271.3 0.2 all-reduce.6.cloned.1.call-start
  271.5 0.4 copy-done.8
  272.0 3.8 copy.17
  275.8 188.0 %all-reduce.4.cloned.1.call-done = f32[256,3584]{1,0:T(8,128)} async-done(((f32[256,3584]{1,0:T(8,128)}), f32[256,3584]{1,0:T(8,128)}) %all-reduce.4.cloned.1.call-update) | async-done | bytes 3670032 | tf_op jit(solution)/shard_map/psum | solution.py:71
  463.8 3.0 multiply_reduce_fusion
  466.8 0.1 copy-done.1
  466.9 0.6 copy-done.2
  467.5 1.2 divide_add_fusion
  468.7 6.8 convolution_bitcast_fusion
  475.5 0.5 copy.20
  476.0 0.8 fusion
  476.8 5.8 copy.29
  482.5 0.0 all-reduce.6.cloned.1.call-update
  482.6 0.6 copy-done.9
  483.2 0.6 dynamic-slice
  484.5 0.6 gather_fusion
  485.1 0.1 fusion.34
  485.2 0.1 broadcast_bitcast_fusion
  485.3 0.4 convert_element_type.29
  485.7 1.1 multiply_reduce_fusion.2
  486.8 190.0 %all-reduce.6.cloned.1.call-done = f32[256,4096]{1,0:T(8,128)} async-done(((f32[256,4096]{1,0:T(8,128)}), f32[256,4096]{1,0:T(8,128)}) %all-reduce.6.cloned.1.call-update) | async-done | bytes 4194320
  676.8 1.7 fusion.47
  678.5 0.5 subtract_multiply_fusion
  (20 shorter events, 0.1 us)
Async XLA Ops:
  7.2 477.3 %copy-start = (s32[2]{0:T(128)S(1)}, s32[2]{0:T(128)}, u32[]{:S(2)}) copy-start(s32[2]{0:T(128)} %param.20) | copy-start | bytes 28
  7.2 84.8 %all-gather.10.cloned.1.call-start = ((), (), s32[]{:S(2)}) async-start(), calls=%async_computation.2 | async-start | bytes 1863680 | tf_op jit(solution)/shard_map/all_gather | solution.py:47
  7.9 112.6 %all-gather.8.cloned.1.call-start = ((), (), s32[]{:S(2)}) async-start(), calls=%async_computation.1 | async-start | bytes 2007040 | tf_op jit(solution)/shard_map/all_gather | solution.py:44
  8.7 192.0 %all-gather.6.cloned.1.call-start = ((), (), s32[]{:S(2)}) async-start(), calls=%async_computation | async-start | bytes 1863680 | tf_op jit(solution)/shard_map/all_gather | solution.py:48
  9.4 219.6 %all-gather.14.cloned.1.call-start = ((), (), s32[]{:S(2)}) async-start(), calls=%async_computation.4 | async-start | bytes 2007040 | tf_op jit(solution)/shard_map/all_gather | solution.py:42
  10.0 250.0 %all-gather.12.cloned.1.call-start = ((), (), s32[]{:S(2)}) async-start(), calls=%async_computation.3 | async-start | bytes 2007040 | tf_op jit(solution)/shard_map/all_gather | solution.py:43
  10.6 453.2 %all-reduce.4.cloned.1.call-start = ((), (), s32[]{:S(2)}) async-start(), calls=%async_computation.5 | async-start | bytes 7340032 | tf_op jit(solution)/shard_map/psum | solution.py:71
  94.8 134.2 %copy-start.5 = (f32[3584]{0:T(1024)S(1)}, f32[3584]{0:T(1024)}, u32[]{:S(2)}) copy-start(f32[3584]{0:T(1024)} %param.13) | copy-start | bytes 43012
  260.0 6.4 copy-start.4
  271.3 0.7 copy-start.8
  271.3 405.5 %all-reduce.6.cloned.1.call-start = ((), (), s32[]{:S(2)}) async-start(), calls=%async_computation.6 | async-start | bytes 8388608
  463.8 3.1 copy-start.1
  463.8 3.7 copy-start.2
  468.7 6.8 copy-start.3
  482.5 0.7 copy-start.9
  482.5 3.2 copy-start.7
  482.6 194.2 %copy-start.6 = (bf16[4,4096]{1,0:T(4,128)(2,1)S(1)}, bf16[4,4096]{1,0:T(4,128)(2,1)}, u32[]{:S(2)}) copy-start(bf16[4,4096]{1,0:T(4,128)(2,1)} %param.21) | copy-start | bytes 98308
Sparse Core Ops, SparseCore 0:
  10.7 81.2 all-gather.9
  93.8 26.6 all-gather.7
  123.2 77.3 all-gather.5
  202.3 26.6 all-gather.13
  230.7 29.2 all-gather.11
  271.4 192.3 all-reduce.3
  482.7 194.0 all-reduce.5
where the time goes:
time: 687 us; the launch traced here: 686 us
  waiting for transfers between devices  621 us (90%)
  matrix products  25 us (4%)
  local copies, waits for them, and re-layouts  15.9 us (2%)
  between operations  14.9 us (2%)
  other arithmetic  8.42 us (1%)
    unnamed x8, waiting for transfers between devices  193 us
    psum x1, waiting for transfers between devices, on_device(): lax.psum(lax.dot_general(grad_gate, gate_full, contract, preferred_elemen...  188 us
    all_gather x1, waiting for transfers between devices, on_device(): lax.all_gather(resid, ('tensor', 'latent'), axis=1, tiled=True)  81.4 us
    all_gather x1, waiting for transfers between devices, on_device(): lax.all_gather(out_grad, ('tensor', 'latent'), axis=1, tiled=True)  80.1 us
    all_gather x1, waiting for transfers between devices, on_device(): lax.all_gather(w_up, 'dp', axis=0, tiled=True)  28.1 us
    all_gather x1, waiting for transfers between devices, on_device(): lax.all_gather(w_down_t, 'dp', axis=0, tiled=True)  25.3 us
    all_gather x1, waiting for transfers between devices, on_device(): lax.all_gather(w_gate, 'dp', axis=0, tiled=True)  25.1 us
  transfers between devices with their start and end apart: 7, of which 7 were waited for; matrix products, arithmetic and copies ran while one was open for 2% of the time, Pallas kernels for 0%

commit v1 on v0

v1 whole, which is shorter than its diff:
```python
import functools
import math

import jax
import jax.numpy as jnp
from jax import lax
from jax.experimental import pallas as pl
from jax.experimental.pallas import tpu as pltpu
from jax.sharding import PartitionSpec as P

BLOCK = 128
N_DP, N_T, N_L, N_Z = 4, 4, 16, 8
TOK = 256
D = 3584
CHUNK = D // N_T
PIECE = CHUNK // N_L
HID = 224
HALF = CHUNK // 2
CAP = 8
SLOTS = 32
SENT = HALF + 16
COLS = CAP * BLOCK
WIDE = COLS + BLOCK
OWN_TOK = TOK // N_T
EPS = 1e-06
F32, BF16 = jnp.float32, jnp.bfloat16

VMEM = pl.BlockSpec(memory_space=pltpu.VMEM)
SMEM = pl.BlockSpec(memory_space=pltpu.SMEM)
ANY = pl.BlockSpec(memory_space=pl.ANY)


def shape(dims, dtype):
    return jax.ShapeDtypeStruct(dims, dtype)


def call(kernel, name, in_specs, outs, scratch=(), limit=48):
    return pl.pallas_call(
        kernel,
        name=name,
        in_specs=in_specs,
        out_specs=jax.tree.map(lambda _: VMEM, outs),
        out_shape=outs,
        scratch_shapes=list(scratch),
        compiler_params=pltpu.CompilerParams(vmem_limit_bytes=limit * 2**20),
    )


def shift(x, axis, size, by):
    return lax.ppermute(x, axis, [(i, (i + by) % size) for i in range(size)])


def swap_core(x):
    return lax.ppermute(x, "latent", [(i, i ^ 1) for i in range(N_L)])


def split(row):
    high = row.astype(BF16).astype(F32)
    return high, row - high


def rows_of(high, low, count):
    index = lax.broadcasted_iota(jnp.int32, (count, high.shape[1]), 0)
    return jnp.where(index == 0, high, jnp.where(index == 1, low, 0.0))


def mlp_kernel(idx, *refs):
    own, other = refs[0:4], refs[4:8]
    gain = refs[8]
    weights = [refs[9 + 5 * i : 14 + 5 * i] for i in range(3)]
    keep, send, cen_out, root_out = refs[24:28]
    x_scr, g_scr, xn_scr, gb_scr, part, out_scr = refs[28:]
    dp, tensor, z, core = idx[0], idx[1], idx[2], idx[3]
    square = jnp.zeros((PIECE, TOK), F32)
    for pieces, side in ((own, core), (other, 1 - core)):
        for e in range(N_T):
            base = lax.rem(tensor - e + N_T, N_T) * CHUNK + side * PIECE
            for d in range(N_Z):
                at = pl.multiple_of(base + lax.rem(z - d + N_Z, N_Z) * 2 * PIECE, 8)
                x = pieces[e][d, 0].astype(F32)
                square += x * x
                x_scr[pl.ds(at, PIECE), :] = x
                g_scr[pl.ds(at, PIECE), :] = pieces[e][d, 1].astype(F32)
    mean = jnp.sum(square, axis=0, keepdims=True) * (1.0 / D)
    root = jnp.sqrt(mean + EPS)
    root_out[...] = root
    inv = 1.0 / root
    step = 448
    for i in range(D // step):
        at = pl.ds(i * step, step)
        xn_scr[at, :] = (x_scr[at, :] * inv * gain[at, :]).astype(BF16)
        gb_scr[at, :] = g_scr[at, :].astype(BF16)

    chunks = (dp, lax.rem(dp + N_DP - 1, N_DP), lax.rem(dp + 1, N_DP), lax.rem(dp + 2, N_DP))
    places = (
        (chunks[0], 0, CHUNK),
        (chunks[1], 0, CHUNK),
        (chunks[2], 0, CHUNK),
        (chunks[3], 0, HALF),
        (chunks[3], HALF, HALF),
    )
    gate = up = grad_a = jnp.zeros((HID, TOK), F32)
    contract = (((0,), (0,)), ((), ()))
    for j, (chunk, offset, size) in enumerate(places):
        at = pl.ds(pl.multiple_of(chunk * CHUNK + offset, 16), size)
        xn, gb = xn_scr[at, :], gb_scr[at, :]
        gate += lax.dot_general(weights[0][j][...], xn, contract, preferred_element_type=F32)
        up += lax.dot_general(weights[1][j][...], xn, contract, preferred_element_type=F32)
        grad_a += lax.dot_general(weights[2][j][...], gb, contract, preferred_element_type=F32)
    coeff = math.sqrt(2.0 / math.pi)
    cube = 0.044715 * gate * gate
    hyper = jnp.tanh(coeff * (gate + cube * gate))
    half = 0.5 * (1.0 + hyper)
    act = gate * half
    slope = half + 0.5 * gate * (1.0 - hyper * hyper) * coeff * (1.0 + 3.0 * cube)
    grad_up = (grad_a * act).astype(BF16)
    grad_gate = (grad_a * up * slope).astype(BF16)
    center = jnp.sum(
        grad_gate.astype(F32) * gate + grad_up.astype(F32) * up, axis=0, keepdims=True
    )
    cen_out[...] = center
    high, low = split(center)
    out_scr[pl.ds(HALF, 16), :] = rows_of(high, low, 16)
    for k in range(4):
        for j in ((k,) if k < 3 else (3, 4)):
            offset = HALF if j == 4 else 0
            part[pl.ds(offset, weights[0][j].shape[0]), :] = jnp.dot(
                weights[0][j][...], grad_gate, preferred_element_type=F32
            ) + jnp.dot(weights[1][j][...], grad_up, preferred_element_type=F32)
        for s in range(N_Z):
            mine = pl.multiple_of(s * 2 * PIECE + core * PIECE, 8)
            theirs = pl.multiple_of(s * 2 * PIECE + (1 - core) * PIECE, 8)
            keep[chunks[k], pl.ds(s * PIECE, PIECE), :] = part[pl.ds(mine, PIECE), :]
            out_scr[pl.ds(s * PIECE, PIECE), :] = part[pl.ds(theirs, PIECE), :]
        send[chunks[k]] = out_scr[...].astype(BF16)


def core_sum_kernel(idx, keep, got, cen, own, s1, s2, s3, cen_out, scr):
    tensor = idx[1]
    tail = got[0].astype(F32)[HALF:, :]
    center = cen[...] + tail[0:1, :] + tail[1:2, :]
    cen_out[...] = center
    high, low = split(center)
    scr[pl.ds(HALF, 16), :] = rows_of(high, low, 16)
    own[...] = keep[tensor] + got[tensor].astype(F32)[:HALF, :]
    for e, out in ((1, s1), (2, s2), (3, s3)):
        to = lax.rem(tensor + e, N_T)
        scr[pl.ds(0, HALF), :] = keep[to] + got[to].astype(F32)[:HALF, :]
        out[...] = scr[...].astype(BF16)


def tensor_sum_kernel(idx, own, r1, r2, r3, cen, *refs):
    mine, sends, cen_out, scr, row = refs[0], refs[1:8], refs[8], refs[9], refs[10]
    z = idx[2]
    total = own[...]
    center = cen[...]
    for r in (r1, r2, r3):
        v = r[...].astype(F32)
        total = total + v[:HALF, :]
        center = center + v[HALF : HALF + 1, :] + v[HALF + 1 : HALF + 2, :]
    cen_out[...] = center
    scr[...] = total
    high, low = split(center)
    row[pl.ds(PIECE, 8), :] = rows_of(high, low, 8)
    mine[...] = scr[pl.ds(pl.multiple_of(z * PIECE, 8), PIECE), :]
    for d in range(1, N_Z):
        at = pl.multiple_of(lax.rem(z + d, N_Z) * PIECE, 8)
        row[pl.ds(0, PIECE), :] = scr[pl.ds(at, PIECE), :]
        sends[d - 1][...] = row[...].astype(BF16)


def grad_kernel(mine, *refs):
    got, (cen, root, gain, bias, x_ref, g_ref, cast, err) = refs[:7], refs[7:]
    total = mine[...]
    center = cen[...]
    for r in got:
        v = r[...].astype(F32)
        total = total + v[:PIECE, :]
        center = center + v[PIECE : PIECE + 1, :] + v[PIECE + 1 : PIECE + 2, :]
    center = center * (1.0 / D)
    x = x_ref[...].astype(F32)
    inv = 1.0 / root[...]
    grad_x = g_ref[...].astype(F32) + (total * gain[...] - x * inv * center) * inv
    cast[...] = grad_x.astype(BF16)
    err[...] = jnp.sum(grad_x * (x - bias[...]), axis=0, keepdims=True)


def decode_kernel(idx, ids, grad, err, decoder, own, s1, s2, s3, dec, wide, sems):
    tensor = idx[1]
    copies = []
    for b in range(2):
        for r in range(CAP):
            rows = pl.ds(pl.multiple_of(ids[b, r] * BLOCK, BLOCK), BLOCK)
            copy = pltpu.make_async_copy(
                decoder.at[rows], dec.at[b, pl.ds(r * BLOCK, BLOCK)], sems.at[b, r]
            )
            copy.start()
            copies.append(copy)
    tall = jnp.broadcast_to(err[...], (BLOCK, TOK)).T
    high, low = split(tall)
    lane = lax.broadcasted_iota(jnp.int32, (TOK, BLOCK), 1)
    wide[:, COLS:] = jnp.where(lane == 0, high, jnp.where(lane == 1, low, 0.0))
    for b in range(2):
        tokens = grad[:, b * BLOCK : (b + 1) * BLOCK]
        for r in range(CAP):
            copies[b * CAP + r].wait()
        wide[b * BLOCK : (b + 1) * BLOCK, :COLS] = lax.dot_general(
            tokens, dec[b], (((0,), (1,)), ((), ())), preferred_element_type=F32
        )
    own[...] = wide[pl.ds(pl.multiple_of(tensor * OWN_TOK, OWN_TOK), OWN_TOK), :]
    for e, out in ((1, s1), (2, s2), (3, s3)):
        to = lax.rem(tensor + e, N_T)
        rows = pl.ds(pl.multiple_of(to * OWN_TOK, OWN_TOK), OWN_TOK)
        out[...] = wide[rows, :].astype(BF16)


def product_sum_kernel(own, r1, r2, r3, out):
    total = own[...]
    for r in (r1, r2, r3):
        total = total + r[...].astype(F32)
    out[:, :COLS] = total[:, :COLS].astype(BF16)
    high, low = split(total[:, COLS : COLS + 1] + total[:, COLS + 1 : COLS + 2])
    lane = lax.broadcasted_iota(jnp.int32, (OWN_TOK, BLOCK), 1)
    out[:, COLS:] = jnp.where(lane == 0, high, jnp.where(lane == 1, low, 0.0)).astype(BF16)


def score_kernel(slots, got, acts, scores, err, scr):
    scr[...] = got[...].astype(F32)
    total = jnp.zeros((4, BLOCK), F32)
    for k in range(SLOTS):
        at = pl.ds(pl.multiple_of(slots[1, k] * BLOCK, BLOCK), BLOCK)
        live = slots[2, k].astype(F32)
        value = scr[slots[0, k], :, at] * (acts[:, k * BLOCK : (k + 1) * BLOCK].astype(F32) * live)
        total += value
        scores[:, k * BLOCK : (k + 1) * BLOCK] = value.astype(BF16)
    extra = jnp.sum(scr[:, :, COLS:], axis=0)
    err[...] = jnp.sum(extra - total, axis=-1, keepdims=True) * (1.0 / math.sqrt(D))


def on_device(
    resid,
    out_grad,
    norm_gain,
    w_gate,
    w_up,
    w_down_t,
    decoder,
    dec_bias,
    block_ids,
    counts,
    latent_acts,
):
    dp, tensor, latent = (lax.axis_index(a) for a in ("dp", "tensor", "latent"))
    idx = jnp.stack([dp, tensor, latent // 2, latent % 2]).astype(jnp.int32)

    with jax.named_scope("weight_rows"):
        pieces = []
        for w in (w_gate, w_up, w_down_t):
            below = shift(w, "dp", N_DP, 1)
            above = shift(w, "dp", N_DP, -1)
            far_low = shift(below[:HALF], "dp", N_DP, 1)
            far_high = shift(above[HALF:], "dp", N_DP, -1)
            pieces += [w, below, above, far_low, far_high]

    with jax.named_scope("token_features"):
        x_own, g_own = resid.T, out_grad.T
        mine = jnp.stack([x_own, g_own])
        column = jnp.stack([mine] + [shift(mine, "latent", N_L, 2 * d) for d in range(1, N_Z)])
        own = [column] + [shift(column, "tensor", N_T, e) for e in range(1, N_T)]
        other = [swap_core(a) for a in own]

    with jax.named_scope("mlp"):
        keep, send, cen, root = call(
            mlp_kernel,
            "mlp",
            [SMEM] + [VMEM] * 24,
            (
                shape((N_T, HALF, TOK), F32),
                shape((N_T, SENT, TOK), BF16),
                shape((1, TOK), F32),
                shape((1, TOK), F32),
            ),
            [
                pltpu.VMEM((D, TOK), F32),
                pltpu.VMEM((D, TOK), F32),
                pltpu.VMEM((D, TOK), BF16),
                pltpu.VMEM((D, TOK), BF16),
                pltpu.VMEM((CHUNK, TOK), F32),
                pltpu.VMEM((SENT, TOK), F32),
            ],
        )(idx, *own, *other, norm_gain[:, None], *pieces)

    with jax.named_scope("hidden_sums"):
        got = swap_core(send)
        row = shape((1, TOK), F32)
        chunk, s1, s2, s3, cen = call(
            core_sum_kernel,
            "core_sum",
            [SMEM] + [VMEM] * 3,
            (shape((HALF, TOK), F32),) + (shape((SENT, TOK), BF16),) * 3 + (row,),
            [pltpu.VMEM((SENT, TOK), F32)],
        )(idx, keep, got, cen)
        got = [shift(s, "tensor", N_T, e) for e, s in ((1, s1), (2, s2), (3, s3))]
        *sends, cen = call(
            tensor_sum_kernel,
            "tensor_sum",
            [SMEM] + [VMEM] * 5,
            (shape((PIECE, TOK), F32),) + (shape((PIECE + 8, TOK), BF16),) * 7 + (row,),
            [pltpu.VMEM((HALF, TOK), F32), pltpu.VMEM((PIECE + 8, TOK), F32)],
        )(idx, chunk, *got, cen)
        got = [shift(s, "latent", N_L, 2 * (i + 1)) for i, s in enumerate(sends[1:])]
        first = (tensor * N_L + latent) * PIECE
        gain_own = lax.dynamic_slice_in_dim(norm_gain, first, PIECE, 0)[:, None]
        bias_own = lax.dynamic_slice_in_dim(dec_bias, first, PIECE, 0)[:, None]
        cast, err = call(
            grad_kernel, "grad", [VMEM] * 14, (shape((PIECE, TOK), BF16), row)
        )(sends[0], *got, cen, root, gain_own, bias_own, x_own, g_own)

    with jax.named_scope("decode"):
        grads = lax.all_gather(cast, "latent", axis=0, tiled=True)
        owner = block_ids // SLOTS
        same = owner[:, :, None] == owner[:, None, :]
        before = jnp.tril(jnp.ones((SLOTS, SLOTS), bool), -1)
        rank = jnp.sum(same & before, axis=2, dtype=jnp.int32)
        takes = (owner == latent)[:, :, None] & (rank[:, :, None] == jnp.arange(CAP))
        local = jnp.sum(jnp.where(takes, (block_ids % SLOTS)[:, :, None], 0), axis=1)
        token_block = tensor // 2
        live = jnp.arange(SLOTS, dtype=jnp.int32) < counts[token_block]
        slots = jnp.stack([owner[token_block], rank[token_block], live.astype(jnp.int32)])
        own, s1, s2, s3 = call(
            decode_kernel,
            "decode",
            [SMEM, SMEM, VMEM, VMEM, ANY],
            (shape((OWN_TOK, WIDE), F32),) + (shape((OWN_TOK, WIDE), BF16),) * 3,
            [
                pltpu.VMEM((2, COLS, CHUNK), BF16),
                pltpu.VMEM((TOK, WIDE), F32),
                pltpu.SemaphoreType.DMA((2, CAP)),
            ],
        )(idx, local.astype(jnp.int32), grads, err, decoder)
        got = [shift(s, "tensor", N_T, e) for e, s in ((1, s1), (2, s2), (3, s3))]
        total = call(
            product_sum_kernel, "product_sum", [VMEM] * 4, shape((OWN_TOK, WIDE), BF16)
        )(own, *got)

    with jax.named_scope("scores"):
        got = lax.all_to_all(total.reshape(N_L, 4, WIDE), "latent", 0, 0, tiled=True)
        scores, err = call(
            score_kernel,
            "score",
            [SMEM, VMEM, VMEM],
            (shape((4, SLOTS * BLOCK), BF16), shape((4, 1), F32)),
            [pltpu.VMEM((N_L, 4, WIDE), F32)],
        )(slots, got, latent_acts)
    return scores, err.reshape(4)


def solution(mesh):
    return jax.shard_map(
        on_device,
        mesh=mesh,
        in_specs=(
            P("dp", ("tensor", "latent")),
            P("dp", ("tensor", "latent")),
            P(),
            P("dp", ("tensor", "latent")),
            P("dp", ("tensor", "latent")),
            P("dp", ("tensor", "latent")),
            P("latent", "tensor"),
            P(),
            P("dp", None),
            P("dp"),
            P(("dp", "tensor", "latent"), None),
        ),
        out_specs=(P(("dp", "tensor", "latent"), None), P(("dp", "tensor", "latent"))),
        check_vma=False,
    )
```

time: 687 us -> 186 us (0.27)
  waiting for transfers between devices: 621 us -> 55.2 us
  starting transfers between devices: 0.45 us -> 73.9 us
  matrix products: 25 us -> 0 us
  blocking collectives: 0 us -> 21.2 us
  Pallas kernels: 0 us -> 17 us
  between operations: 14.9 us -> 0.97 us
    all_gather x5 -> x0, waiting for transfers between devices: 240 us -> none  [the longest x1 81.4 us: on_device(): lax.all_gather(resid, ('tensor', 'latent'), axis=1, tiled=True)]
    unnamed x8 -> x0, waiting for transfers between devices: 193 us -> none
    psum x1 -> x0, waiting for transfers between devices: 188 us -> none  [on_device(): lax.psum(lax.dot_general(grad_gate, gate_full, contract, preferred_elemen...]
    ppermute x0 -> x40, starting transfers between devices: none -> 68 us  [the longest x35 56.7 us: shift(): return lax.ppermute(x, axis, [(i, (i + by) % size) for i in range(size)])]
    ppermute x0 -> x40, waiting for transfers between devices: none -> 46.6 us  [the longest x35 44.3 us: shift(): return lax.ppermute(x, axis, [(i, (i + by) % size) for i in range(size)])]
    dot_general x6 -> x0, matrix products: 25 us -> none  [the longest x1 6.79 us: on_device(): lax.dot_general(grad_cols, decoder, contract, preferred_element_type=jnp....]
    all_gather x0 -> x1, blocking collectives: none -> 21.2 us  [on_device(): grads = lax.all_gather(cast, 'latent', axis=0, tiled=True)]
    pallas_call x0 -> x7, Pallas kernels: none -> 17 us  [the longest x1 9.54 us: on_device(): call(mlp_kernel, 'mlp', [SMEM] + [VMEM] * 24, (shape((N_T, HALF, TOK), F3...]
  transfers between devices with their start and end apart: 7 -> 41, of which waited for: 7 -> 14; matrix products, arithmetic and copies ran while one was open for 2% -> 5% of each run, Pallas kernels for 0% -> 0%
where the time goes in v1:
time: 186 us
  starting transfers between devices  73.9 us (40%)
  waiting for transfers between devices  55.2 us (30%)
  blocking collectives  21.2 us (11%)
  Pallas kernels  17 us (9%)
  local copies, waits for them, and re-layouts  14.8 us (8%)
  other arithmetic  2.62 us (1%)
    ppermute x35, starting transfers between devices, shift(): return lax.ppermute(x, axis, [(i, (i + by) % size) for i in range(size)])  56.7 us
    ppermute x35, waiting for transfers between devices, shift(): return lax.ppermute(x, axis, [(i, (i + by) % size) for i in range(size)])  44.3 us
    all_gather x1, blocking collectives, on_device(): grads = lax.all_gather(cast, 'latent', axis=0, tiled=True)  21.2 us
    ppermute x5, starting transfers between devices, swap_core(): return lax.ppermute(x, 'latent', [(i, i ^ 1) for i in range(N_L)])  11.3 us
    unnamed x51, local copies, waits for them, and re-layouts  9.93 us
    pallas_call x1, Pallas kernels, on_device(): call(mlp_kernel, 'mlp', [SMEM] + [VMEM] * 24, (shape((N_T, HALF, TOK), F3...  9.54 us
    all_to_all x1, waiting for transfers between devices, on_device(): lax.all_to_all(total.reshape(N_L, 4, WIDE), 'latent', 0, 0, tiled=True)  8.63 us
    all_to_all x1, starting transfers between devices, on_device(): lax.all_to_all(total.reshape(N_L, 4, WIDE), 'latent', 0, 0, tiled=True)  5.93 us
  transfers between devices with their start and end apart: 41, of which 14 were waited for; matrix products, arithmetic and copies ran while one was open for 5% of the time, Pallas kernels for 0%

profile of v1, /device:TPU:1, one launch (start us, length us, event | category | flops | bytes accessed | tf_op | source)
XLA Modules:
  0.0 185.8 jit_solution(10094893056268480336)
XLA Ops:
  1.5 2.5 %collective-permute-start = (bf16[2,56,256]{2,1,0:T(8,128)(2,1)S(1)}, bf16[2,56,256]{2,1,0:T(8,128)(2,1)S(1)}, u32[]{:S(2)}, u32[]{:S(2)}) collective-permute-start(bf16[2,56,256]{2,1,0:T(8,128)(2,1)S(1)} %pad_maximum_fusion), channel_id=1, source_target_pairs={{0,2},{1,3},{2,4},{3,5},{4,6},{5,7},{6,8},{7,9},{8,10},{9,11},{10,... | collective-permute-start | bytes 172040 | tf_op jit(solution)/shard_map/token_features/ppermute | solution.py:50
  4.0 3.0 %collective-permute-start.1 = (bf16[2,56,256]{2,1,0:T(8,128)(2,1)S(1)}, bf16[2,56,256]{2,1,0:T(8,128)(2,1)S(1)}, u32[]{:S(2)}, u32[]{:S(2)}) collective-permute-start(bf16[2,56,256]{2,1,0:T(8,128)(2,1)S(1)} %pad_maximum_fusion), channel_id=1, source_target_pairs={{0,4},{1,5},{2,6},{3,7},{4,8},{5,9},{6,10},{7,11},{8,12},{9,13},{1... | collective-permute-start | bytes 172040 | tf_op jit(solution)/shard_map/token_features/ppermute | solution.py:50
  7.0 3.8 %collective-permute-start.2 = (bf16[2,56,256]{2,1,0:T(8,128)(2,1)S(1)}, bf16[2,56,256]{2,1,0:T(8,128)(2,1)S(1)}, u32[]{:S(2)}, u32[]{:S(2)}) collective-permute-start(bf16[2,56,256]{2,1,0:T(8,128)(2,1)S(1)} %pad_maximum_fusion), channel_id=1, source_target_pairs={{0,6},{1,7},{2,8},{3,9},{4,10},{5,11},{6,12},{7,13},{8,14},{9,15},... | collective-permute-start | bytes 172040 | tf_op jit(solution)/shard_map/token_features/ppermute | solution.py:50
  11.2 4.5 %collective-permute-start.4 = (bf16[2,56,256]{2,1,0:T(8,128)(2,1)S(1)}, bf16[2,56,256]{2,1,0:T(8,128)(2,1)S(1)}, u32[]{:S(2)}, u32[]{:S(2)}) collective-permute-start(bf16[2,56,256]{2,1,0:T(8,128)(2,1)S(1)} %pad_maximum_fusion), channel_id=1, source_target_pairs={{0,10},{1,11},{2,12},{3,13},{4,14},{5,15},{6,0},{7,1},{8,2},{9,3},... | collective-permute-start | bytes 172040 | tf_op jit(solution)/shard_map/token_features/ppermute | solution.py:50
  15.6 1.2 copy.43.refs_9_
  16.9 1.2 copy.44.refs_14_
  19.2 2.5 %collective-permute-start.5 = (bf16[2,56,256]{2,1,0:T(8,128)(2,1)S(1)}, bf16[2,56,256]{2,1,0:T(8,128)(2,1)S(1)}, u32[]{:S(2)}, u32[]{:S(2)}) collective-permute-start(bf16[2,56,256]{2,1,0:T(8,128)(2,1)S(1)} %pad_maximum_fusion), channel_id=1, source_target_pairs={{0,12},{1,13},{2,14},{3,15},{4,0},{5,1},{6,2},{7,3},{8,4},{9,5},{1... | collective-permute-start | bytes 172040 | tf_op jit(solution)/shard_map/token_features/ppermute | solution.py:50
  22.5 1.4 collective-permute-start.14
  23.8 1.5 collective-permute-start.15
  25.5 2.7 %collective-permute-start.19 = (bf16[896,224]{1,0:T(8,128)(2,1)S(1)}, bf16[896,224]{1,0:T(8,128)(2,1)S(1)}, u32[]{:S(2)}, u32[]{:S(2)}) collective-permute-start(bf16[896,224]{1,0:T(8,128)(2,1)S(1)} %copy.44.refs_14_), channel_id=1, source_target_pairs={{0,192},{64,0},{128,64},{192,128},{1,193},{65,1},{129,65},{193,129... | collective-permute-start | bytes 1204232 | tf_op jit(solution)/shard_map/weight_rows/ppermute | solution.py:50
  28.3 5.0 %collective-permute-done.14.refs_10_ = bf16[896,224]{1,0:T(8,128)(2,1)S(1)} collective-permute-done((bf16[896,224]{1,0:T(8,128)(2,1)S(1)}, bf16[896,224]{1,0:T(8,128)(2,1)S(1)}, u32[]{:S(2)}, u32[]{:S(2)}) %collective-permute-start.14) | collective-permute-done | bytes 401440 | tf_op jit(solution)/shard_map/weight_rows/ppermute | solution.py:50
  33.2 1.2 collective-permute-start.7
  34.5 1.4 collective-permute-start.23
  35.9 7.2 %collective-permute-done.18.refs_15_ = bf16[896,224]{1,0:T(8,128)(2,1)S(1)} collective-permute-done((bf16[896,224]{1,0:T(8,128)(2,1)S(1)}, bf16[896,224]{1,0:T(8,128)(2,1)S(1)}, u32[]{:S(2)}, u32[]{:S(2)}) %collective-permute-start.18) | collective-permute-done | bytes 401440 | tf_op jit(solution)/shard_map/weight_rows/ppermute | solution.py:50
  43.1 2.7 %collective-permute-start.8 = (bf16[8,2,56,256]{3,2,1,0:T(8,128)(2,1)S(1)}, bf16[8,2,56,256]{3,2,1,0:T(8,128)(2,1)S(1)}, u32[]{:S(2)}, u32[]{:S(2)}) collective-permute-start(bf16[8,2,56,256]{3,2,1,0:T(8,128)(2,1)S(1)} %bitcast_dynamic-update-slice_fusion.refs_0_), channel_id=1, source_target_pairs={{0,32},{16,48},{32,0},{48,16},{1,33},{17,49},{33,1},{49,17},{2,34}... | collective-permute-start | bytes 1376264 | tf_op jit(solution)/shard_map/token_features/ppermute | solution.py:50
  45.8 1.1 collective-permute-start.9
  46.9 6.0 %collective-permute-done.22.refs_20_ = bf16[896,224]{1,0:T(8,128)(2,1)S(1)} collective-permute-done((bf16[896,224]{1,0:T(8,128)(2,1)}, bf16[896,224]{1,0:T(8,128)(2,1)S(1)}, u32[]{:S(2)}, u32[]{:S(2)}) %collective-permute-start.22) | collective-permute-done | bytes 401440 | tf_op jit(solution)/shard_map/weight_rows/ppermute | solution.py:50
  52.9 3.5 %collective-permute-start.10 = (bf16[8,2,56,256]{3,2,1,0:T(8,128)(2,1)S(1)}, bf16[8,2,56,256]{3,2,1,0:T(8,128)(2,1)S(1)}, u32[]{:S(2)}, u32[]{:S(2)}) collective-permute-start(bf16[8,2,56,256]{3,2,1,0:T(8,128)(2,1)S(1)} %bitcast_dynamic-update-slice_fusion.refs_0_), channel_id=1, source_target_pairs={{0,1},{1,0},{2,3},{3,2},{4,5},{5,4},{6,7},{7,6},{8,9},{9,8},{10,11... | collective-permute-start | bytes 1376264 | tf_op jit(solution)/shard_map/token_features/ppermute | solution.py:54
  56.6 2.6 %collective-permute-start.17 = (bf16[448,224]{1,0:T(8,128)(2,1)S(1)}, bf16[448,224]{1,0:T(8,128)(2,1)S(1)}, u32[]{:S(2)}, u32[]{:S(2)}) collective-permute-start(bf16[448,224]{1,0:T(8,128)(2,1)S(1)} %slice.25), channel_id=1, source_target_pairs={{0,192},{64,0},{128,64},{192,128},{1,193},{65,1},{129,65},{193,129... | collective-permute-start | bytes 602120 | tf_op jit(solution)/shard_map/weight_rows/ppermute | solution.py:50
  59.2 1.1 collective-permute-start.11
  60.3 2.8 %collective-permute-done.9.refs_3_ = bf16[8,2,56,256]{3,2,1,0:T(8,128)(2,1)S(1)} collective-permute-done((bf16[8,2,56,256]{3,2,1,0:T(8,128)(2,1)S(1)}, bf16[8,2,56,256]{3,2,1,0:T(8,128)(2,1)S(1)}, u32[]{:S(2)}, u32[]{:S(2)}) %collective-permute-start.9) | collective-permute-done | bytes 458784 | tf_op jit(solution)/shard_map/token_features/ppermute | solution.py:50
  63.1 4.4 %collective-permute-start.12 = (bf16[8,2,56,256]{3,2,1,0:T(8,128)(2,1)S(1)}, bf16[8,2,56,256]{3,2,1,0:T(8,128)(2,1)}, u32[]{:S(2)}, u32[]{:S(2)}) collective-permute-start(bf16[8,2,56,256]{3,2,1,0:T(8,128)(2,1)S(1)} %collective-permute-done.8.refs_2_), channel_id=1, source_target_pairs={{0,1},{1,0},{2,3},{3,2},{4,5},{5,4},{6,7},{7,6},{8,9},{9,8},{10,11... | collective-permute-start | bytes 1376264 | tf_op jit(solution)/shard_map/token_features/ppermute | solution.py:54
  68.4 2.7 %collective-permute-start.21 = (bf16[448,224]{1,0:T(8,128)(2,1)S(1)}, bf16[448,224]{1,0:T(8,128)(2,1)S(1)}, u32[]{:S(2)}, u32[]{:S(2)}) collective-permute-start(bf16[448,224]{1,0:T(8,128)(2,1)S(1)} %slice.27), channel_id=1, source_target_pairs={{0,192},{64,0},{128,64},{192,128},{1,193},{65,1},{129,65},{193,129... | collective-permute-start | bytes 602120 | tf_op jit(solution)/shard_map/weight_rows/ppermute | solution.py:50
  72.4 3.1 %collective-permute-done.20.refs_17_ = bf16[448,224]{1,0:T(8,128)(2,1)S(1)} collective-permute-done((bf16[448,224]{1,0:T(8,128)(2,1)S(1)}, bf16[448,224]{1,0:T(8,128)(2,1)S(1)}, u32[]{:S(2)}, u32[]{:S(2)}) %collective-permute-start.20) | collective-permute-done | bytes 200736 | tf_op jit(solution)/shard_map/weight_rows/ppermute | solution.py:50
  76.9 2.7 %collective-permute-start.25 = (bf16[448,224]{1,0:T(8,128)(2,1)}, bf16[448,224]{1,0:T(8,128)(2,1)}, u32[]{:S(2)}, u32[]{:S(2)}) collective-permute-start(bf16[448,224]{1,0:T(8,128)(2,1)} %slice.29), channel_id=1, source_target_pairs={{0,192},{64,0},{128,64},{192,128},{1,193},{65,1},{129,65},{193,129... | collective-permute-start | bytes 602120 | tf_op jit(solution)/shard_map/weight_rows/ppermute | solution.py:50
  79.6 1.8 broadcast_in_dim.36.refs_8_
  81.5 2.0 %collective-permute-done.24.refs_22_ = bf16[448,224]{1,0:T(8,128)(2,1)} collective-permute-done((bf16[448,224]{1,0:T(8,128)(2,1)}, bf16[448,224]{1,0:T(8,128)(2,1)}, u32[]{:S(2)}, u32[]{:S(2)}) %collective-permute-start.24) | collective-permute-done | bytes 200736 | tf_op jit(solution)/shard_map/weight_rows/ppermute | solution.py:50
  86.3 9.5 %mlp.1 = (f32[4,448,256]{2,1,0:T(8,128)}, bf16[4,464,256]{2,1,0:T(8,128)(2,1)}, f32[1,256]{1,0:T(1,128)S(1)}, f32[1,256]{1,0:T(1,128)S(1)}) custom-call(s32[4]{0:T(128)S(1)} %pad_add_fusion.1.idx, bf16[8,2,56,256]{3,2,1,0:T(8,128)(2,1)S(1)} %bitcast_dynamic-update-slice_fusion.refs_0_, bf16[8,2,56,256]{3,2,1,0:T(8,128)(2,1)S(1)} %collective-permute-done.7.refs_1_, ...), custom_call_target="tpu_custom_call" | custom-call | tf_op jit(solution)/shard_map/mlp/mlp/pallas_call | solution.py:273
  95.9 2.3 %collective-permute-start.26 = (bf16[4,464,256]{2,1,0:T(8,128)(2,1)}, bf16[4,464,256]{2,1,0:T(8,128)(2,1)S(1)}, u32[]{:S(2)}, u32[]{:S(2)}) collective-permute-start(bf16[4,464,256]{2,1,0:T(8,128)(2,1)} %get-tuple-element.29), channel_id=1, source_target_pairs={{0,1},{1,0},{2,3},{3,2},{4,5},{5,4},{6,7},{7,6},{8,9},{9,8},{10,11... | collective-permute-start | bytes 2850824 | tf_op jit(solution)/shard_map/hidden_sums/ppermute | solution.py:54
  98.3 2.3 %collective-permute-done.26.got = bf16[4,464,256]{2,1,0:T(8,128)(2,1)S(1)} collective-permute-done((bf16[4,464,256]{2,1,0:T(8,128)(2,1)}, bf16[4,464,256]{2,1,0:T(8,128)(2,1)S(1)}, u32[]{:S(2)}, u32[]{:S(2)}) %collective-permute-start.26) | collective-permute-done | bytes 950304 | tf_op jit(solution)/shard_map/hidden_sums/ppermute | solution.py:54
  100.5 1.5 copy-done.1
  103.9 2.5 %collective-permute-start.28 = (bf16[464,256]{1,0:T(8,128)(2,1)S(1)}, bf16[464,256]{1,0:T(8,128)(2,1)S(1)}, u32[]{:S(2)}, u32[]{:S(2)}) collective-permute-start(bf16[464,256]{1,0:T(8,128)(2,1)S(1)} %get-tuple-element.33), channel_id=1, source_target_pairs={{0,32},{16,48},{32,0},{48,16},{1,33},{17,49},{33,1},{49,17},{2,34}... | collective-permute-start | bytes 712712 | tf_op jit(solution)/shard_map/hidden_sums/ppermute | solution.py:50
  107.0 4.1 %collective-permute-done.27.r1 = bf16[464,256]{1,0:T(8,128)(2,1)S(1)} collective-permute-done((bf16[464,256]{1,0:T(8,128)(2,1)S(1)}, bf16[464,256]{1,0:T(8,128)(2,1)S(1)}, u32[]{:S(2)}, u32[]{:S(2)}) %collective-permute-start.27) | collective-permute-done | bytes 237600 | tf_op jit(solution)/shard_map/hidden_sums/ppermute | solution.py:50
  111.0 5.9 %collective-permute-done.28.r2 = bf16[464,256]{1,0:T(8,128)(2,1)S(1)} collective-permute-done((bf16[464,256]{1,0:T(8,128)(2,1)S(1)}, bf16[464,256]{1,0:T(8,128)(2,1)S(1)}, u32[]{:S(2)}, u32[]{:S(2)}) %collective-permute-start.28) | collective-permute-done | bytes 237600 | tf_op jit(solution)/shard_map/hidden_sums/ppermute | solution.py:50
  118.5 1.9 %collective-permute-start.32 = (bf16[64,256]{1,0:T(8,128)(2,1)S(1)}, bf16[64,256]{1,0:T(8,128)(2,1)S(1)}, u32[]{:S(2)}, u32[]{:S(2)}) collective-permute-start(bf16[64,256]{1,0:T(8,128)(2,1)S(1)} %get-tuple-element.39), channel_id=1, source_target_pairs={{0,6},{1,7},{2,8},{3,9},{4,10},{5,11},{6,12},{7,13},{8,14},{9,15},... | collective-permute-start | bytes 98312 | tf_op jit(solution)/shard_map/hidden_sums/ppermute | solution.py:50
  120.5 3.5 %collective-permute-start.33 = (bf16[64,256]{1,0:T(8,128)(2,1)S(1)}, bf16[64,256]{1,0:T(8,128)(2,1)S(1)}, u32[]{:S(2)}, u32[]{:S(2)}) collective-permute-start(bf16[64,256]{1,0:T(8,128)(2,1)S(1)} %get-tuple-element.40), channel_id=1, source_target_pairs={{0,8},{1,9},{2,10},{3,11},{4,12},{5,13},{6,14},{7,15},{8,0},{9,1},... | collective-permute-start | bytes 98312 | tf_op jit(solution)/shard_map/hidden_sums/ppermute | solution.py:50
  124.0 1.8 collective-permute-start.34
  125.9 1.9 %collective-permute-start.35 = (bf16[64,256]{1,0:T(8,128)(2,1)S(1)}, bf16[64,256]{1,0:T(8,128)(2,1)S(1)}, u32[]{:S(2)}, u32[]{:S(2)}) collective-permute-start(bf16[64,256]{1,0:T(8,128)(2,1)S(1)} %get-tuple-element.42), channel_id=1, source_target_pairs={{0,12},{1,13},{2,14},{3,15},{4,0},{5,1},{6,2},{7,3},{8,4},{9,5},{1... | collective-permute-start | bytes 98312 | tf_op jit(solution)/shard_map/hidden_sums/ppermute | solution.py:50
  127.8 1.3 collective-permute-start.36
  129.4 1.3 collective-permute-done.35.refs_5_
  131.5 21.2 %all_gather.3.grad = bf16[896,256]{1,0:T(8,128)(2,1)S(1)} all-gather(bf16[56,256]{1,0:T(8,128)(2,1)S(1)} %get-tuple-element.46), channel_id=1, replica_groups=mesh['dp'=4,'tensor'=4,'latent'=16] {'latent'}, dimensions={0}, use_global_device_ids=true | all-gather | bytes 487424 | tf_op jit(solution)/shard_map/decode/all_gather | solution.py:320
  152.7 4.4 %decode.1 = (f32[64,1152]{1,0:T(8,128)S(1)}, bf16[64,1152]{1,0:T(8,128)(2,1)S(1)}, bf16[64,1152]{1,0:T(8,128)(2,1)S(1)}, bf16[64,1152]{1,0:T(8,128)(2,1)S(1)}) custom-call(s32[4]{0:T(128)S(1)} %pad_add_fusion.1.idx, s32[2,8]{1,0:T(2,128)S(1)} %select_reduce_fusion.ids, bf16[896,256]{1,0:T(8,128)(2,1)S(1)} %all_gather.3.grad, ...), custom_call_target="tpu_custom_call" | custom-call | tf_op jit(solution)/shard_map/decode/decode/pallas_call | solution.py:330
  158.1 2.5 %collective-permute-start.38 = (bf16[64,1152]{1,0:T(8,128)(2,1)S(1)}, bf16[64,1152]{1,0:T(8,128)(2,1)S(1)}, u32[]{:S(2)}, u32[]{:S(2)}) collective-permute-start(bf16[64,1152]{1,0:T(8,128)(2,1)S(1)} %get-tuple-element.50), channel_id=1, source_target_pairs={{0,32},{16,48},{32,0},{48,16},{1,33},{17,49},{33,1},{49,17},{2,34}... | collective-permute-start | bytes 442376 | tf_op jit(solution)/shard_map/decode/ppermute | solution.py:50
  161.4 2.4 %collective-permute-done.37.r1 = bf16[64,1152]{1,0:T(8,128)(2,1)S(1)} collective-permute-done((bf16[64,1152]{1,0:T(8,128)(2,1)S(1)}, bf16[64,1152]{1,0:T(8,128)(2,1)S(1)}, u32[]{:S(2)}, u32[]{:S(2)}) %collective-permute-start.37) | collective-permute-done | bytes 147488 | tf_op jit(solution)/shard_map/decode/ppermute | solution.py:50
  163.8 3.8 %collective-permute-done.38.r2 = bf16[64,1152]{1,0:T(8,128)(2,1)S(1)} collective-permute-done((bf16[64,1152]{1,0:T(8,128)(2,1)S(1)}, bf16[64,1152]{1,0:T(8,128)(2,1)S(1)}, u32[]{:S(2)}, u32[]{:S(2)}) %collective-permute-start.38) | collective-permute-done | bytes 147488 | tf_op jit(solution)/shard_map/decode/ppermute | solution.py:50
  168.6 5.9 %all-to-all-start = ((bf16[16,4,1152]{2,1,0:T(4,128)(2,1)}), bf16[16,4,1152]{2,1,0:T(4,128)(2,1)S(1)}, u32[]{:S(2)}, u32[]{:S(2)}) async-start(bf16[16,4,1152]{2,1,0:T(4,128)(2,1)} %reshape.38), calls=%async_computation | async-start | bytes 294912 | tf_op jit(solution)/shard_map/scores/all_to_all | solution.py:347
  175.2 8.6 %all-to-all-done.got = bf16[16,4,1152]{2,1,0:T(4,128)(2,1)S(1)} async-done(((bf16[16,4,1152]{2,1,0:T(4,128)(2,1)}), bf16[16,4,1152]{2,1,0:T(4,128)(2,1)S(1)}, u32[]{:S(2)}, u32[]{:S(2)}) %all-to-all-start) | async-done | bytes 147488 | tf_op jit(solution)/shard_map/scores/all_to_all | solution.py:347
  183.9 1.3 score.1
  (120 shorter events, 19.4 us)
Async XLA Ops:
  0.6 128.5 %copy-start = (f32[3584]{0:T(1024)S(1)}, f32[3584]{0:T(1024)}, u32[]{:S(2)}) copy-start(f32[3584]{0:T(1024)} %param.18) | copy-start | bytes 43012
  1.5 17.7 %collective-permute-start = (bf16[2,56,256]{2,1,0:T(8,128)(2,1)S(1)}, bf16[2,56,256]{2,1,0:T(8,128)(2,1)S(1)}, u32[]{:S(2)}, u32[]{:S(2)}) collective-permute-start(bf16[2,56,256]{2,1,0:T(8,128)(2,1)S(1)} %pad_maximum_fusion), channel_id=1, source_target_pairs={{0,2},{1,3},{2,4},{3,5},{4,6},{5,7},{6,8},{7,9},{8,10},{9,11},{10,... | collective-permute-start | bytes 172040 | tf_op jit(solution)/shard_map/token_features/ppermute | solution.py:50
  4.0 17.7 %collective-permute-start.1 = (bf16[2,56,256]{2,1,0:T(8,128)(2,1)S(1)}, bf16[2,56,256]{2,1,0:T(8,128)(2,1)S(1)}, u32[]{:S(2)}, u32[]{:S(2)}) collective-permute-start(bf16[2,56,256]{2,1,0:T(8,128)(2,1)S(1)} %pad_maximum_fusion), channel_id=1, source_target_pairs={{0,4},{1,5},{2,6},{3,7},{4,8},{5,9},{6,10},{7,11},{8,12},{9,13},{1... | collective-permute-start | bytes 172040 | tf_op jit(solution)/shard_map/token_features/ppermute | solution.py:50
  7.0 15.5 %collective-permute-start.2 = (bf16[2,56,256]{2,1,0:T(8,128)(2,1)S(1)}, bf16[2,56,256]{2,1,0:T(8,128)(2,1)S(1)}, u32[]{:S(2)}, u32[]{:S(2)}) collective-permute-start(bf16[2,56,256]{2,1,0:T(8,128)(2,1)S(1)} %pad_maximum_fusion), channel_id=1, source_target_pairs={{0,6},{1,7},{2,8},{3,9},{4,10},{5,11},{6,12},{7,13},{8,14},{9,15},... | collective-permute-start | bytes 172040 | tf_op jit(solution)/shard_map/token_features/ppermute | solution.py:50
  10.7 13.1 %collective-permute-start.3 = (bf16[2,56,256]{2,1,0:T(8,128)(2,1)S(1)}, bf16[2,56,256]{2,1,0:T(8,128)(2,1)S(1)}, u32[]{:S(2)}, u32[]{:S(2)}) collective-permute-start(bf16[2,56,256]{2,1,0:T(8,128)(2,1)S(1)} %pad_maximum_fusion), channel_id=1, source_target_pairs={{0,8},{1,9},{2,10},{3,11},{4,12},{5,13},{6,14},{7,15},{8,0},{9,1},... | collective-permute-start | bytes 172040 | tf_op jit(solution)/shard_map/token_features/ppermute | solution.py:50
  11.2 14.2 %collective-permute-start.4 = (bf16[2,56,256]{2,1,0:T(8,128)(2,1)S(1)}, bf16[2,56,256]{2,1,0:T(8,128)(2,1)S(1)}, u32[]{:S(2)}, u32[]{:S(2)}) collective-permute-start(bf16[2,56,256]{2,1,0:T(8,128)(2,1)S(1)} %pad_maximum_fusion), channel_id=1, source_target_pairs={{0,10},{1,11},{2,12},{3,13},{4,14},{5,15},{6,0},{7,1},{8,2},{9,3},... | collective-permute-start | bytes 172040 | tf_op jit(solution)/shard_map/token_features/ppermute | solution.py:50
  18.1 27.8 %copy-start.11 = (bf16[896,224]{1,0:T(8,128)(2,1)}, bf16[896,224]{1,0:T(8,128)(2,1)S(1)}, u32[]{:S(2)}) copy-start(bf16[896,224]{1,0:T(8,128)(2,1)S(1)} %copy.44.refs_14_) | copy-start | bytes 1204228
  19.1 60.5 %copy-start.18 = (f32[3584]{0:T(1024)S(1)}, f32[3584]{0:T(1024)}, u32[]{:S(2)}) copy-start(f32[3584]{0:T(1024)} %param.13) | copy-start | bytes 43012
  19.2 6.3 %collective-permute-start.5 = (bf16[2,56,256]{2,1,0:T(8,128)(2,1)S(1)}, bf16[2,56,256]{2,1,0:T(8,128)(2,1)S(1)}, u32[]{:S(2)}, u32[]{:S(2)}) collective-permute-start(bf16[2,56,256]{2,1,0:T(8,128)(2,1)S(1)} %pad_maximum_fusion), channel_id=1, source_target_pairs={{0,12},{1,13},{2,14},{3,15},{4,0},{5,1},{6,2},{7,3},{8,4},{9,5},{1... | collective-permute-start | bytes 172040 | tf_op jit(solution)/shard_map/token_features/ppermute | solution.py:50
  21.6 6.6 %collective-permute-start.6 = (bf16[2,56,256]{2,1,0:T(8,128)(2,1)S(1)}, bf16[2,56,256]{2,1,0:T(8,128)(2,1)S(1)}, u32[]{:S(2)}, u32[]{:S(2)}) collective-permute-start(bf16[2,56,256]{2,1,0:T(8,128)(2,1)S(1)} %pad_maximum_fusion), channel_id=1, source_target_pairs={{0,14},{1,15},{2,0},{3,1},{4,2},{5,3},{6,4},{7,5},{8,6},{9,7},{10,... | collective-permute-start | bytes 172040 | tf_op jit(solution)/shard_map/token_features/ppermute | solution.py:50
  22.5 10.8 %collective-permute-start.14 = (bf16[896,224]{1,0:T(8,128)(2,1)S(1)}, bf16[896,224]{1,0:T(8,128)(2,1)S(1)}, u32[]{:S(2)}, u32[]{:S(2)}) collective-permute-start(bf16[896,224]{1,0:T(8,128)(2,1)S(1)} %copy.43.refs_9_), channel_id=1, source_target_pairs={{0,64},{64,128},{128,192},{192,0},{1,65},{65,129},{129,193},{193,1... | collective-permute-start | bytes 1204232 | tf_op jit(solution)/shard_map/weight_rows/ppermute | solution.py:50
  23.8 10.6 %collective-permute-start.15 = (bf16[896,224]{1,0:T(8,128)(2,1)S(1)}, bf16[896,224]{1,0:T(8,128)(2,1)S(1)}, u32[]{:S(2)}, u32[]{:S(2)}) collective-permute-start(bf16[896,224]{1,0:T(8,128)(2,1)S(1)} %copy.43.refs_9_), channel_id=1, source_target_pairs={{0,192},{64,0},{128,64},{192,128},{1,193},{65,1},{129,65},{193,129... | collective-permute-start | bytes 1204232 | tf_op jit(solution)/shard_map/weight_rows/ppermute | solution.py:50
  25.4 17.7 %collective-permute-start.18 = (bf16[896,224]{1,0:T(8,128)(2,1)S(1)}, bf16[896,224]{1,0:T(8,128)(2,1)S(1)}, u32[]{:S(2)}, u32[]{:S(2)}) collective-permute-start(bf16[896,224]{1,0:T(8,128)(2,1)S(1)} %copy.44.refs_14_), channel_id=1, source_target_pairs={{0,64},{64,128},{128,192},{192,0},{1,65},{65,129},{129,193},{193,1... | collective-permute-start | bytes 1204232 | tf_op jit(solution)/shard_map/weight_rows/ppermute | solution.py:50
  25.5 20.3 %collective-permute-start.19 = (bf16[896,224]{1,0:T(8,128)(2,1)S(1)}, bf16[896,224]{1,0:T(8,128)(2,1)S(1)}, u32[]{:S(2)}, u32[]{:S(2)}) collective-permute-start(bf16[896,224]{1,0:T(8,128)(2,1)S(1)} %copy.44.refs_14_), channel_id=1, source_target_pairs={{0,192},{64,0},{128,64},{192,128},{1,193},{65,1},{129,65},{193,129... | collective-permute-start | bytes 1204232 | tf_op jit(solution)/shard_map/weight_rows/ppermute | solution.py:50
  28.2 24.7 %collective-permute-start.22 = (bf16[896,224]{1,0:T(8,128)(2,1)}, bf16[896,224]{1,0:T(8,128)(2,1)S(1)}, u32[]{:S(2)}, u32[]{:S(2)}) collective-permute-start(bf16[896,224]{1,0:T(8,128)(2,1)} %copy.45.refs_19_), channel_id=1, source_target_pairs={{0,64},{64,128},{128,192},{192,0},{1,65},{65,129},{129,193},{193,1... | collective-permute-start | bytes 1204232 | tf_op jit(solution)/shard_map/weight_rows/ppermute | solution.py:50
  33.2 23.3 %collective-permute-start.7 = (bf16[8,2,56,256]{3,2,1,0:T(8,128)(2,1)S(1)}, bf16[8,2,56,256]{3,2,1,0:T(8,128)(2,1)S(1)}, u32[]{:S(2)}, u32[]{:S(2)}) collective-permute-start(bf16[8,2,56,256]{3,2,1,0:T(8,128)(2,1)S(1)} %bitcast_dynamic-update-slice_fusion.refs_0_), channel_id=1, source_target_pairs={{0,16},{16,32},{32,48},{48,0},{1,17},{17,33},{33,49},{49,1},{2,18}... | collective-permute-start | bytes 1376264 | tf_op jit(solution)/shard_map/token_features/ppermute | solution.py:50
  34.5 22.0 %collective-permute-start.23 = (bf16[896,224]{1,0:T(8,128)(2,1)}, bf16[896,224]{1,0:T(8,128)(2,1)S(1)}, u32[]{:S(2)}, u32[]{:S(2)}) collective-permute-start(bf16[896,224]{1,0:T(8,128)(2,1)} %copy.45.refs_19_), channel_id=1, source_target_pairs={{0,192},{64,0},{128,64},{192,128},{1,193},{65,1},{129,65},{193,129... | collective-permute-start | bytes 1204232 | tf_op jit(solution)/shard_map/weight_rows/ppermute | solution.py:50
  43.1 33.2 %copy-start.13 = (bf16[896,224]{1,0:T(8,128)(2,1)}, bf16[896,224]{1,0:T(8,128)(2,1)S(1)}, u32[]{:S(2)}) copy-start(bf16[896,224]{1,0:T(8,128)(2,1)S(1)} %collective-permute-done.18.refs_15_) | copy-start | bytes 1204228
  43.1 16.2 %collective-permute-start.8 = (bf16[8,2,56,256]{3,2,1,0:T(8,128)(2,1)S(1)}, bf16[8,2,56,256]{3,2,1,0:T(8,128)(2,1)S(1)}, u32[]{:S(2)}, u32[]{:S(2)}) collective-permute-start(bf16[8,2,56,256]{3,2,1,0:T(8,128)(2,1)S(1)} %bitcast_dynamic-update-slice_fusion.refs_0_), channel_id=1, source_target_pairs={{0,32},{16,48},{32,0},{48,16},{1,33},{17,49},{33,1},{49,17},{2,34}... | collective-permute-start | bytes 1376264 | tf_op jit(solution)/shard_map/token_features/ppermute | solution.py:50
  45.8 33.8 %copy-start.14 = (bf16[896,224]{1,0:T(8,128)(2,1)}, bf16[896,224]{1,0:T(8,128)(2,1)S(1)}, u32[]{:S(2)}) copy-start(bf16[896,224]{1,0:T(8,128)(2,1)S(1)} %collective-permute-done.19.refs_16_) | copy-start | bytes 1204228
  45.8 17.3 %collective-permute-start.9 = (bf16[8,2,56,256]{3,2,1,0:T(8,128)(2,1)S(1)}, bf16[8,2,56,256]{3,2,1,0:T(8,128)(2,1)S(1)}, u32[]{:S(2)}, u32[]{:S(2)}) collective-permute-start(bf16[8,2,56,256]{3,2,1,0:T(8,128)(2,1)S(1)} %bitcast_dynamic-update-slice_fusion.refs_0_), channel_id=1, source_target_pairs={{0,48},{16,0},{32,16},{48,32},{1,49},{17,1},{33,17},{49,33},{2,50}... | collective-permute-start | bytes 1376264 | tf_op jit(solution)/shard_map/token_features/ppermute | solution.py:50
  52.9 26.7 %copy-start.15 = (bf16[896,224]{1,0:T(8,128)(2,1)}, bf16[896,224]{1,0:T(8,128)(2,1)S(1)}, u32[]{:S(2)}) copy-start(bf16[896,224]{1,0:T(8,128)(2,1)S(1)} %collective-permute-done.22.refs_20_) | copy-start | bytes 1204228
  52.9 14.6 %collective-permute-start.10 = (bf16[8,2,56,256]{3,2,1,0:T(8,128)(2,1)S(1)}, bf16[8,2,56,256]{3,2,1,0:T(8,128)(2,1)S(1)}, u32[]{:S(2)}, u32[]{:S(2)}) collective-permute-start(bf16[8,2,56,256]{3,2,1,0:T(8,128)(2,1)S(1)} %bitcast_dynamic-update-slice_fusion.refs_0_), channel_id=1, source_target_pairs={{0,1},{1,0},{2,3},{3,2},{4,5},{5,4},{6,7},{7,6},{8,9},{9,8},{10,11... | collective-permute-start | bytes 1376264 | tf_op jit(solution)/shard_map/token_features/ppermute | solution.py:54
  56.5 11.1 %collective-permute-start.16 = (bf16[448,224]{1,0:T(8,128)(2,1)S(1)}, bf16[448,224]{1,0:T(8,128)(2,1)S(1)}, u32[]{:S(2)}, u32[]{:S(2)}) collective-permute-start(bf16[448,224]{1,0:T(8,128)(2,1)S(1)} %slice.24), channel_id=1, source_target_pairs={{0,64},{64,128},{128,192},{192,0},{1,65},{65,129},{129,193},{193,1... | collective-permute-start | bytes 602120 | tf_op jit(solution)/shard_map/weight_rows/ppermute | solution.py:50
  56.6 11.1 %collective-permute-start.17 = (bf16[448,224]{1,0:T(8,128)(2,1)S(1)}, bf16[448,224]{1,0:T(8,128)(2,1)S(1)}, u32[]{:S(2)}, u32[]{:S(2)}) collective-permute-start(bf16[448,224]{1,0:T(8,128)(2,1)S(1)} %slice.25), channel_id=1, source_target_pairs={{0,192},{64,0},{128,64},{192,128},{1,193},{65,1},{129,65},{193,129... | collective-permute-start | bytes 602120 | tf_op jit(solution)/shard_map/weight_rows/ppermute | solution.py:50
  59.2 24.3 %collective-permute-start.11 = (bf16[8,2,56,256]{3,2,1,0:T(8,128)(2,1)S(1)}, bf16[8,2,56,256]{3,2,1,0:T(8,128)(2,1)}, u32[]{:S(2)}, u32[]{:S(2)}) collective-permute-start(bf16[8,2,56,256]{3,2,1,0:T(8,128)(2,1)S(1)} %collective-permute-done.7.refs_1_), channel_id=1, source_target_pairs={{0,1},{1,0},{2,3},{3,2},{4,5},{5,4},{6,7},{7,6},{8,9},{9,8},{10,11... | collective-permute-start | bytes 1376264 | tf_op jit(solution)/shard_map/token_features/ppermute | solution.py:54
  63.1 20.4 %collective-permute-start.12 = (bf16[8,2,56,256]{3,2,1,0:T(8,128)(2,1)S(1)}, bf16[8,2,56,256]{3,2,1,0:T(8,128)(2,1)}, u32[]{:S(2)}, u32[]{:S(2)}) collective-permute-start(bf16[8,2,56,256]{3,2,1,0:T(8,128)(2,1)S(1)} %collective-permute-done.8.refs_2_), channel_id=1, source_target_pairs={{0,1},{1,0},{2,3},{3,2},{4,5},{5,4},{6,7},{7,6},{8,9},{9,8},{10,11... | collective-permute-start | bytes 1376264 | tf_op jit(solution)/shard_map/token_features/ppermute | solution.py:54
  67.5 16.0 %collective-permute-start.13 = (bf16[8,2,56,256]{3,2,1,0:T(8,128)(2,1)S(1)}, bf16[8,2,56,256]{3,2,1,0:T(8,128)(2,1)}, u32[]{:S(2)}, u32[]{:S(2)}) collective-permute-start(bf16[8,2,56,256]{3,2,1,0:T(8,128)(2,1)S(1)} %collective-permute-done.9.refs_3_), channel_id=1, source_target_pairs={{0,1},{1,0},{2,3},{3,2},{4,5},{5,4},{6,7},{7,6},{8,9},{9,8},{10,11... | collective-permute-start | bytes 1376264 | tf_op jit(solution)/shard_map/token_features/ppermute | solution.py:54
  67.6 7.9 %collective-permute-start.20 = (bf16[448,224]{1,0:T(8,128)(2,1)S(1)}, bf16[448,224]{1,0:T(8,128)(2,1)S(1)}, u32[]{:S(2)}, u32[]{:S(2)}) collective-permute-start(bf16[448,224]{1,0:T(8,128)(2,1)S(1)} %slice.26), channel_id=1, source_target_pairs={{0,64},{64,128},{128,192},{192,0},{1,65},{65,129},{129,193},{193,1... | collective-permute-start | bytes 602120 | tf_op jit(solution)/shard_map/weight_rows/ppermute | solution.py:50
  68.4 7.9 %collective-permute-start.21 = (bf16[448,224]{1,0:T(8,128)(2,1)S(1)}, bf16[448,224]{1,0:T(8,128)(2,1)S(1)}, u32[]{:S(2)}, u32[]{:S(2)}) collective-permute-start(bf16[448,224]{1,0:T(8,128)(2,1)S(1)} %slice.27), channel_id=1, source_target_pairs={{0,192},{64,0},{128,64},{192,128},{1,193},{65,1},{129,65},{193,129... | collective-permute-start | bytes 602120 | tf_op jit(solution)/shard_map/weight_rows/ppermute | solution.py:50
  76.2 7.3 %collective-permute-start.24 = (bf16[448,224]{1,0:T(8,128)(2,1)}, bf16[448,224]{1,0:T(8,128)(2,1)}, u32[]{:S(2)}, u32[]{:S(2)}) collective-permute-start(bf16[448,224]{1,0:T(8,128)(2,1)} %slice.28), channel_id=1, source_target_pairs={{0,64},{64,128},{128,192},{192,0},{1,65},{65,129},{129,193},{193,1... | collective-permute-start | bytes 602120 | tf_op jit(solution)/shard_map/weight_rows/ppermute | solution.py:50
  76.9 6.6 %collective-permute-start.25 = (bf16[448,224]{1,0:T(8,128)(2,1)}, bf16[448,224]{1,0:T(8,128)(2,1)}, u32[]{:S(2)}, u32[]{:S(2)}) collective-permute-start(bf16[448,224]{1,0:T(8,128)(2,1)} %slice.29), channel_id=1, source_target_pairs={{0,192},{64,0},{128,64},{192,128},{1,193},{65,1},{129,65},{193,129... | collective-permute-start | bytes 602120 | tf_op jit(solution)/shard_map/weight_rows/ppermute | solution.py:50
  95.9 4.6 %collective-permute-start.26 = (bf16[4,464,256]{2,1,0:T(8,128)(2,1)}, bf16[4,464,256]{2,1,0:T(8,128)(2,1)S(1)}, u32[]{:S(2)}, u32[]{:S(2)}) collective-permute-start(bf16[4,464,256]{2,1,0:T(8,128)(2,1)} %get-tuple-element.29), channel_id=1, source_target_pairs={{0,1},{1,0},{2,3},{3,2},{4,5},{5,4},{6,7},{7,6},{8,9},{9,8},{10,11... | collective-permute-start | bytes 2850824 | tf_op jit(solution)/shard_map/hidden_sums/ppermute | solution.py:54
  102.8 8.3 %collective-permute-start.27 = (bf16[464,256]{1,0:T(8,128)(2,1)S(1)}, bf16[464,256]{1,0:T(8,128)(2,1)S(1)}, u32[]{:S(2)}, u32[]{:S(2)}) collective-permute-start(bf16[464,256]{1,0:T(8,128)(2,1)S(1)} %get-tuple-element.32), channel_id=1, source_target_pairs={{0,16},{16,32},{32,48},{48,0},{1,17},{17,33},{33,49},{49,1},{2,18}... | collective-permute-start | bytes 712712 | tf_op jit(solution)/shard_map/hidden_sums/ppermute | solution.py:50
  103.9 13.1 %collective-permute-start.28 = (bf16[464,256]{1,0:T(8,128)(2,1)S(1)}, bf16[464,256]{1,0:T(8,128)(2,1)S(1)}, u32[]{:S(2)}, u32[]{:S(2)}) collective-permute-start(bf16[464,256]{1,0:T(8,128)(2,1)S(1)} %get-tuple-element.33), channel_id=1, source_target_pairs={{0,32},{16,48},{32,0},{48,16},{1,33},{17,49},{33,1},{49,17},{2,34}... | collective-permute-start | bytes 712712 | tf_op jit(solution)/shard_map/hidden_sums/ppermute | solution.py:50
  106.3 10.6 %collective-permute-start.29 = (bf16[464,256]{1,0:T(8,128)(2,1)S(1)}, bf16[464,256]{1,0:T(8,128)(2,1)S(1)}, u32[]{:S(2)}, u32[]{:S(2)}) collective-permute-start(bf16[464,256]{1,0:T(8,128)(2,1)S(1)} %get-tuple-element.34), channel_id=1, source_target_pairs={{0,48},{16,0},{32,16},{48,32},{1,49},{17,1},{33,17},{49,33},{2,50}... | collective-permute-start | bytes 712712 | tf_op jit(solution)/shard_map/hidden_sums/ppermute | solution.py:50
  117.7 8.2 %collective-permute-start.30 = (bf16[64,256]{1,0:T(8,128)(2,1)S(1)}, bf16[64,256]{1,0:T(8,128)(2,1)S(1)}, u32[]{:S(2)}, u32[]{:S(2)}) collective-permute-start(bf16[64,256]{1,0:T(8,128)(2,1)S(1)} %get-tuple-element.37), channel_id=1, source_target_pairs={{0,2},{1,3},{2,4},{3,5},{4,6},{5,7},{6,8},{7,9},{8,10},{9,11},{10,... | collective-permute-start | bytes 98312 | tf_op jit(solution)/shard_map/hidden_sums/ppermute | solution.py:50
  118.5 9.3 %collective-permute-start.31 = (bf16[64,256]{1,0:T(8,128)(2,1)S(1)}, bf16[64,256]{1,0:T(8,128)(2,1)S(1)}, u32[]{:S(2)}, u32[]{:S(2)}) collective-permute-start(bf16[64,256]{1,0:T(8,128)(2,1)S(1)} %get-tuple-element.38), channel_id=1, source_target_pairs={{0,4},{1,5},{2,6},{3,7},{4,8},{5,9},{6,10},{7,11},{8,12},{9,13},{1... | collective-permute-start | bytes 98312 | tf_op jit(solution)/shard_map/hidden_sums/ppermute | solution.py:50
  118.5 10.8 %collective-permute-start.32 = (bf16[64,256]{1,0:T(8,128)(2,1)S(1)}, bf16[64,256]{1,0:T(8,128)(2,1)S(1)}, u32[]{:S(2)}, u32[]{:S(2)}) collective-permute-start(bf16[64,256]{1,0:T(8,128)(2,1)S(1)} %get-tuple-element.39), channel_id=1, source_target_pairs={{0,6},{1,7},{2,8},{3,9},{4,10},{5,11},{6,12},{7,13},{8,14},{9,15},... | collective-permute-start | bytes 98312 | tf_op jit(solution)/shard_map/hidden_sums/ppermute | solution.py:50
  120.5 8.9 %collective-permute-start.33 = (bf16[64,256]{1,0:T(8,128)(2,1)S(1)}, bf16[64,256]{1,0:T(8,128)(2,1)S(1)}, u32[]{:S(2)}, u32[]{:S(2)}) collective-permute-start(bf16[64,256]{1,0:T(8,128)(2,1)S(1)} %get-tuple-element.40), channel_id=1, source_target_pairs={{0,8},{1,9},{2,10},{3,11},{4,12},{5,13},{6,14},{7,15},{8,0},{9,1},... | collective-permute-start | bytes 98312 | tf_op jit(solution)/shard_map/hidden_sums/ppermute | solution.py:50
  124.0 5.3 %collective-permute-start.34 = (bf16[64,256]{1,0:T(8,128)(2,1)S(1)}, bf16[64,256]{1,0:T(8,128)(2,1)S(1)}, u32[]{:S(2)}, u32[]{:S(2)}) collective-permute-start(bf16[64,256]{1,0:T(8,128)(2,1)S(1)} %get-tuple-element.41), channel_id=1, source_target_pairs={{0,10},{1,11},{2,12},{3,13},{4,14},{5,15},{6,0},{7,1},{8,2},{9,3},... | collective-permute-start | bytes 98312 | tf_op jit(solution)/shard_map/hidden_sums/ppermute | solution.py:50
  125.9 4.8 %collective-permute-start.35 = (bf16[64,256]{1,0:T(8,128)(2,1)S(1)}, bf16[64,256]{1,0:T(8,128)(2,1)S(1)}, u32[]{:S(2)}, u32[]{:S(2)}) collective-permute-start(bf16[64,256]{1,0:T(8,128)(2,1)S(1)} %get-tuple-element.42), channel_id=1, source_target_pairs={{0,12},{1,13},{2,14},{3,15},{4,0},{5,1},{6,2},{7,3},{8,4},{9,5},{1... | collective-permute-start | bytes 98312 | tf_op jit(solution)/shard_map/hidden_sums/ppermute | solution.py:50
  127.8 3.6 %collective-permute-start.36 = (bf16[64,256]{1,0:T(8,128)(2,1)S(1)}, bf16[64,256]{1,0:T(8,128)(2,1)S(1)}, u32[]{:S(2)}, u32[]{:S(2)}) collective-permute-start(bf16[64,256]{1,0:T(8,128)(2,1)S(1)} %get-tuple-element.43), channel_id=1, source_target_pairs={{0,14},{1,15},{2,0},{3,1},{4,2},{5,3},{6,4},{7,5},{8,6},{9,7},{10,... | collective-permute-start | bytes 98312 | tf_op jit(solution)/shard_map/hidden_sums/ppermute | solution.py:50
  152.7 31.2 %copy-start.10 = (bf16[4,4096]{1,0:T(4,128)(2,1)S(1)}, bf16[4,4096]{1,0:T(4,128)(2,1)}, u32[]{:S(2)}) copy-start(bf16[4,4096]{1,0:T(4,128)(2,1)} %acts.1) | copy-start | bytes 98308
  157.1 6.7 %collective-permute-start.37 = (bf16[64,1152]{1,0:T(8,128)(2,1)S(1)}, bf16[64,1152]{1,0:T(8,128)(2,1)S(1)}, u32[]{:S(2)}, u32[]{:S(2)}) collective-permute-start(bf16[64,1152]{1,0:T(8,128)(2,1)S(1)} %get-tuple-element.49), channel_id=1, source_target_pairs={{0,16},{16,32},{32,48},{48,0},{1,17},{17,33},{33,49},{49,1},{2,18}... | collective-permute-start | bytes 442376 | tf_op jit(solution)/shard_map/decode/ppermute | solution.py:50
  158.1 9.6 %collective-permute-start.38 = (bf16[64,1152]{1,0:T(8,128)(2,1)S(1)}, bf16[64,1152]{1,0:T(8,128)(2,1)S(1)}, u32[]{:S(2)}, u32[]{:S(2)}) collective-permute-start(bf16[64,1152]{1,0:T(8,128)(2,1)S(1)} %get-tuple-element.50), channel_id=1, source_target_pairs={{0,32},{16,48},{32,0},{48,16},{1,33},{17,49},{33,1},{49,17},{2,34}... | collective-permute-start | bytes 442376 | tf_op jit(solution)/shard_map/decode/ppermute | solution.py:50
  160.6 7.1 %collective-permute-start.39 = (bf16[64,1152]{1,0:T(8,128)(2,1)S(1)}, bf16[64,1152]{1,0:T(8,128)(2,1)S(1)}, u32[]{:S(2)}, u32[]{:S(2)}) collective-permute-start(bf16[64,1152]{1,0:T(8,128)(2,1)S(1)} %get-tuple-element.51), channel_id=1, source_target_pairs={{0,48},{16,0},{32,16},{48,32},{1,49},{17,1},{33,17},{49,33},{2,50}... | collective-permute-start | bytes 442376 | tf_op jit(solution)/shard_map/decode/ppermute | solution.py:50
  168.6 15.3 %all-to-all-start = ((bf16[16,4,1152]{2,1,0:T(4,128)(2,1)}), bf16[16,4,1152]{2,1,0:T(4,128)(2,1)S(1)}, u32[]{:S(2)}, u32[]{:S(2)}) async-start(bf16[16,4,1152]{2,1,0:T(4,128)(2,1)} %reshape.38), calls=%async_computation | async-start | bytes 294912 | tf_op jit(solution)/shard_map/scores/all_to_all | solution.py:347
  (14 other events, 131.0 us)

commit v2 on v1

v2 whole, which is shorter than its diff:
```python
import functools
import math

import jax
import jax.numpy as jnp
from jax import lax
from jax.experimental import pallas as pl
from jax.experimental.pallas import tpu as pltpu
from jax.sharding import PartitionSpec as P

BLOCK = 128
N_DP, N_T, N_L, N_Z = 4, 4, 16, 8
TOK = 256
D = 3584
CHUNK = D // N_T
PIECE = CHUNK // N_L
HID = 224
HALF = CHUNK // 2
CAP = 8
SLOTS = 32
GROUP = HALF // 2
SENT = GROUP + 16
COLS = CAP * BLOCK
WIDE = COLS + BLOCK
OWN_TOK = TOK // N_T
EPS = 1e-06
F32, BF16 = jnp.float32, jnp.bfloat16

VMEM = pl.BlockSpec(memory_space=pltpu.VMEM)
SMEM = pl.BlockSpec(memory_space=pltpu.SMEM)
ANY = pl.BlockSpec(memory_space=pl.ANY)
HBM = pl.BlockSpec(memory_space=pltpu.HBM)


def shape(dims, dtype):
    return jax.ShapeDtypeStruct(dims, dtype)


def call(kernel, name, in_specs, outs, scratch=(), limit=48):
    return pl.pallas_call(
        kernel,
        name=name,
        in_specs=in_specs,
        out_specs=jax.tree.map(lambda _: VMEM, outs),
        out_shape=outs,
        scratch_shapes=list(scratch),
        compiler_params=pltpu.CompilerParams(vmem_limit_bytes=limit * 2**20),
    )


def shift(x, axis, size, by):
    return lax.ppermute(x, axis, [(i, (i + by) % size) for i in range(size)])


def swap_core(x):
    return lax.ppermute(x, "latent", [(i, i ^ 1) for i in range(N_L)])


def split(row):
    high = row.astype(BF16).astype(F32)
    return high, row - high


def rows_of(high, low, count):
    index = lax.broadcasted_iota(jnp.int32, (count, high.shape[1]), 0)
    return jnp.where(index == 0, high, jnp.where(index == 1, low, 0.0))


def mlp_kernel(idx, x0, g0, a1, a2, a3, b1, b2, b3, gain, w0, w1, w2, w3, w4, *refs):
    keep1, keep2, send1, send2, cen_out, root_out = refs[:6]
    x_scr, g_scr, grads, part, out_scr = refs[6:]
    dp, tensor, odd, core = idx[0], idx[1], lax.rem(idx[2], 2), idx[3]
    first = core == 0
    square = jnp.zeros((8, TOK), F32)
    for e, (a, b) in enumerate(((x0, g0), (a1, b1), (a2, b2), (a3, b3))):
        at = pl.ds(pl.multiple_of(lax.rem(tensor - e + N_T, N_T) * CHUNK, 16), CHUNK)
        va, vb = a[...], b[...]
        if e:
            va, vb = jnp.where(first, va, vb), jnp.where(first, vb, va)
        x_scr[at, :] = va
        g_scr[at, :] = vb
        x = va.astype(F32)
        square += jnp.sum((x * x).reshape(CHUNK // 8, 8, TOK), axis=0)
    mean = jnp.sum(square, axis=0, keepdims=True) * (1.0 / D)
    root = jnp.sqrt(mean + EPS)
    root_out[...] = root
    inv = 1.0 / root
    columns = gain[...].T
    for i in range(D // BLOCK):
        at = pl.ds(i * BLOCK, BLOCK)
        x_scr[at, :] = (x_scr[at, :].astype(F32) * inv * columns[:, i : i + 1]).astype(BF16)

    chunks = (dp, lax.rem(dp + N_DP - 1, N_DP), lax.rem(dp + 1, N_DP), lax.rem(dp + 2, N_DP))

    def forward(w, chunk):
        rows = w.shape[1]
        at = pl.ds(pl.multiple_of(chunk * CHUNK, 16), CHUNK)
        both = jnp.dot(
            w[0:2].reshape(2 * rows, CHUNK), x_scr[at, :], preferred_element_type=F32
        )
        down = jnp.dot(w[2], g_scr[at, :], preferred_element_type=F32)
        return both[:rows], both[rows:], down

    low, high = forward(w3, chunks[3]), forward(w4, chunks[3])
    sums = [jnp.concatenate(pair, axis=0) for pair in zip(low, high)]
    for w, chunk in ((w0, chunks[0]), (w1, chunks[1]), (w2, chunks[2])):
        sums = [total + v for total, v in zip(sums, forward(w, chunk))]
    gate, up, grad_a = sums
    coeff = math.sqrt(2.0 / math.pi)
    cube = 0.044715 * gate * gate
    hyper = jnp.tanh(coeff * (gate + cube * gate))
    half = 0.5 * (1.0 + hyper)
    act = gate * half
    slope = half + 0.5 * gate * (1.0 - hyper * hyper) * coeff * (1.0 + 3.0 * cube)
    grad_up = (grad_a * act).astype(BF16)
    grad_gate = (grad_a * up * slope).astype(BF16)
    center = jnp.sum(
        grad_gate.astype(F32) * gate + grad_up.astype(F32) * up, axis=0, keepdims=True
    )
    cen_out[...] = center
    high, low = split(center)
    out_scr[pl.ds(GROUP, 16), :] = rows_of(high, low, 16)
    grads[0:HID, :] = grad_gate
    grads[HID:, :] = grad_up
    near = grads[...]
    middle = HID // 2
    far_low = jnp.concatenate([grad_gate[:middle], grad_up[:middle]], axis=0)
    far_high = jnp.concatenate([grad_gate[middle:], grad_up[middle:]], axis=0)

    def backward(w, grad):
        return lax.dot_general(
            w[0:2].reshape(2 * w.shape[1], CHUNK),
            grad,
            (((0,), (0,)), ((), ())),
            preferred_element_type=F32,
        )

    for k, chunk in enumerate(chunks):
        if k < 3:
            part[...] = backward((w0, w1, w2)[k], near)
        else:
            part[...] = backward(w3, far_low) + backward(w4, far_high)
        for keep, send, parity in ((keep1, send1, 1 - odd), (keep2, send2, odd)):
            for s in range(N_Z // 2):
                base = (4 * s + 2 * parity) * PIECE
                mine = pl.multiple_of(base + core * PIECE, 8)
                theirs = pl.multiple_of(base + (1 - core) * PIECE, 8)
                keep[chunk, pl.ds(s * PIECE, PIECE), :] = part[pl.ds(mine, PIECE), :]
                out_scr[pl.ds(s * PIECE, PIECE), :] = part[pl.ds(theirs, PIECE), :]
            send[chunk] = out_scr[pl.ds(0, send.shape[1]), :].astype(BF16)


def core_sum_kernel(idx, keep1, keep2, got1, got2, cen, own1, own2, *refs):
    sends1, sends2, cen_out, scr = refs[:3], refs[3:6], refs[6], refs[7]
    tensor = idx[1]
    tail = got1[0].astype(F32)[GROUP:, :]
    center = cen[...] + tail[0:1, :] + tail[1:2, :]
    cen_out[...] = center
    high, low = split(center)
    scr[pl.ds(GROUP, 16), :] = rows_of(high, low, 16)
    own1[...] = keep1[tensor] + got1[tensor].astype(F32)[:GROUP, :]
    own2[...] = keep2[tensor] + got2[tensor].astype(F32)
    for e in (1, 2, 3):
        to = lax.rem(tensor + e, N_T)
        scr[pl.ds(0, GROUP), :] = keep1[to] + got1[to].astype(F32)[:GROUP, :]
        sends1[e - 1][...] = scr[...].astype(BF16)
        sends2[e - 1][...] = (keep2[to] + got2[to].astype(F32)).astype(BF16)


def tensor_sum_kernel(own, r1, r2, r3, cen, send, cen_out, scr):
    total = own[...]
    center = cen[...]
    for r in (r1, r2, r3):
        v = r[...].astype(F32)
        total = total + v[:GROUP, :]
        center = center + v[GROUP : GROUP + 1, :] + v[GROUP + 1 : GROUP + 2, :]
    cen_out[...] = center
    high, low = split(center)
    scr[pl.ds(0, GROUP), :] = total
    scr[pl.ds(GROUP, 16), :] = rows_of(high, low, 16)
    send[...] = scr[...].astype(BF16)


def pair_sum_kernel(own, r1, r2, r3, pair, cen, total_out, send, cen_out, scr):
    v = pair[...].astype(F32)
    total = own[...] + v[:GROUP, :]
    for r in (r1, r2, r3):
        total = total + r[...].astype(F32)
    center = cen[...] + v[GROUP : GROUP + 1, :] + v[GROUP + 1 : GROUP + 2, :]
    total_out[...] = total
    cen_out[...] = center
    high, low = split(center)
    scr[pl.ds(0, GROUP), :] = total
    scr[pl.ds(GROUP, 16), :] = rows_of(high, low, 16)
    send[...] = scr[...].astype(BF16)


def grad_kernel(idx, own, r1, r2, r3, cen, root, gain, bias, x_ref, g_ref, cast, err):
    total = own[...]
    center = cen[...]
    for r in (r1, r2, r3):
        v = r[...].astype(F32)
        total = total + v[:GROUP, :]
        center = center + v[GROUP : GROUP + 1, :] + v[GROUP + 1 : GROUP + 2, :]
    center = center * (1.0 / D)
    x = x_ref[...].astype(F32)
    inv = 1.0 / root[...]
    grad_x = g_ref[...].astype(F32) + (total * gain[...] - x * inv * center) * inv
    cast[...] = grad_x.astype(BF16)
    start = (idx[2] // 2) * PIECE
    index = lax.broadcasted_iota(jnp.int32, (GROUP, TOK), 0)
    mine = (index >= start) & (index < start + PIECE)
    terms = jnp.where(mine, grad_x * (x - bias[...]), 0.0)
    err[...] = jnp.sum(terms, axis=0, keepdims=True)


def fetch_kernel(ids, decoder, _, dec, passed, sems):
    copies = []
    for b in range(2):
        for r in range(CAP):
            rows = pl.ds(pl.multiple_of(ids[b, r] * BLOCK, BLOCK), BLOCK)
            copy = pltpu.make_async_copy(
                decoder.at[rows], dec.at[b, pl.ds(r * BLOCK, BLOCK)], sems.at[b, r]
            )
            copy.start()
            copies.append(copy)
    for copy in copies:
        copy.wait()


def stack_kernel(a, b, c, out, sems):
    copies = [pltpu.make_async_copy(w, out.at[i], sems.at[i]) for i, w in enumerate((a, b, c))]
    for copy in copies:
        copy.start()
    for copy in copies:
        copy.wait()


def decode_kernel(idx, g0, g1, g2, g3, err, dec, out, grad, scr):
    place = 2 * lax.rem(idx[2], 2) + idx[3]
    flips = (place, 2 * (1 - lax.rem(idx[2], 2)) + idx[3], 2 * lax.rem(idx[2], 2) + 1 - idx[3])
    last = 2 * (1 - lax.rem(idx[2], 2)) + 1 - idx[3]
    for g, at in zip((g0, g1, g2, g3), flips + (last,)):
        rows = g[...].astype(F32)
        for k in range(N_Z // 2):
            start = pl.multiple_of((4 * k + at) * PIECE, 8)
            scr[pl.ds(start, PIECE), :] = rows[k * PIECE : (k + 1) * PIECE, :]
    grad[...] = scr[...].astype(BF16)
    tall = jnp.broadcast_to(err[...], (BLOCK, TOK)).T
    high, low = split(tall)
    lane = lax.broadcasted_iota(jnp.int32, (TOK, BLOCK), 1)
    out[:, COLS:] = jnp.where(lane == 0, high, jnp.where(lane == 1, low, 0.0)).astype(BF16)
    for b in range(2):
        tokens = grad[:, b * BLOCK : (b + 1) * BLOCK]
        out[b * BLOCK : (b + 1) * BLOCK, :COLS] = lax.dot_general(
            tokens, dec[b], (((0,), (1,)), ((), ())), preferred_element_type=F32
        ).astype(BF16)


def score_kernel(slots, got, acts, scores, err, scr):
    for l in range(N_L):
        total = got[l].astype(F32)
        for t in range(1, N_T):
            total = total + got[t * N_L + l].astype(F32)
        scr[l] = total
    total = jnp.zeros((4, BLOCK), F32)
    for k in range(SLOTS):
        at = pl.ds(pl.multiple_of(slots[1, k] * BLOCK, BLOCK), BLOCK)
        live = slots[2, k].astype(F32)
        value = scr[slots[0, k], :, at] * (acts[:, k * BLOCK : (k + 1) * BLOCK].astype(F32) * live)
        total += value
        scores[:, k * BLOCK : (k + 1) * BLOCK] = value.astype(BF16)
    extra = jnp.sum(scr[:, :, COLS:], axis=0)
    rest = jnp.concatenate([extra - total, jnp.zeros((4, BLOCK), F32)], axis=0).T
    err[...] = jnp.sum(rest, axis=0, keepdims=True)[:, :4] * (1.0 / math.sqrt(D))


def on_device(
    resid,
    out_grad,
    norm_gain,
    w_gate,
    w_up,
    w_down_t,
    decoder,
    dec_bias,
    block_ids,
    counts,
    latent_acts,
):
    dp, tensor, latent = (lax.axis_index(a) for a in ("dp", "tensor", "latent"))
    idx = jnp.stack([dp, tensor, latent // 2, latent % 2]).astype(jnp.int32)

    with jax.named_scope("slots"):
        owner = block_ids // SLOTS
        same = owner[:, :, None] == owner[:, None, :]
        before = jnp.tril(jnp.ones((SLOTS, SLOTS), bool), -1)
        rank = jnp.sum(same & before, axis=2, dtype=jnp.int32)
        takes = (owner == latent)[:, :, None] & (rank[:, :, None] == jnp.arange(CAP))
        local = jnp.sum(jnp.where(takes, (block_ids % SLOTS)[:, :, None], 0), axis=1)
        token_block = tensor // 2
        live = jnp.arange(SLOTS, dtype=jnp.int32) < counts[token_block]
        slots = jnp.stack([owner[token_block], rank[token_block], live.astype(jnp.int32)])
    with jax.named_scope("weight_rows"):
        rows = call(
            stack_kernel,
            "stack",
            [HBM] * 3,
            shape((3, HID, CHUNK), BF16),
            [pltpu.SemaphoreType.DMA((3,))],
            limit=60,
        )(w_gate.T, w_up.T, w_down_t.T)
        below = shift(rows, "dp", N_DP, 1)
        above = shift(rows, "dp", N_DP, -1)
        middle = HID // 2
        far_low = shift(below[:, :middle], "dp", N_DP, 1)
        far_high = shift(above[:, middle:], "dp", N_DP, -1)

    with jax.named_scope("token_features"):
        x_own, g_own = resid.T, out_grad.T
        column = lax.all_gather(jnp.concatenate([x_own, g_own]), "latent", axis=0)
        x_all = column[:, :PIECE].reshape(CHUNK, TOK)
        g_all = column[:, PIECE:].reshape(CHUNK, TOK)
        fetch = jnp.where(latent % 2 == 0, x_all, g_all)
        own = [shift(fetch, "tensor", N_T, e) for e in range(1, N_T)]
        dec, own[0] = pl.pallas_call(
            fetch_kernel,
            name="fetch",
            in_specs=[SMEM, HBM, ANY],
            out_specs=(VMEM, ANY),
            out_shape=(shape((2, COLS, CHUNK), BF16), shape((CHUNK, TOK), BF16)),
            input_output_aliases={2: 1},
            scratch_shapes=[pltpu.SemaphoreType.DMA((2, CAP))],
            compiler_params=pltpu.CompilerParams(vmem_limit_bytes=8 * 2**20),
        )(local.astype(jnp.int32), decoder, own[0])
        other = [swap_core(a) for a in own]

    with jax.named_scope("mlp"):
        row = shape((1, TOK), F32)
        keep1, keep2, send1, send2, cen, root = call(
            mlp_kernel,
            "mlp",
            [SMEM] + [VMEM] * 14,
            (
                shape((N_T, GROUP, TOK), F32),
                shape((N_T, GROUP, TOK), F32),
                shape((N_T, SENT, TOK), BF16),
                shape((N_T, GROUP, TOK), BF16),
                row,
                row,
            ),
            [
                pltpu.VMEM((D, TOK), BF16),
                pltpu.VMEM((D, TOK), BF16),
                pltpu.VMEM((2 * HID, TOK), BF16),
                pltpu.VMEM((CHUNK, TOK), F32),
                pltpu.VMEM((SENT, TOK), F32),
            ],
            limit=26,
        )(
            idx, x_all, g_all, *own, *other, norm_gain.reshape(D // BLOCK, BLOCK),
            rows, below, above, far_low, far_high,
        )

    with jax.named_scope("hidden_sums"):
        tensor_shifts = (1, 2, 3)
        got1, got2 = swap_core(send1), swap_core(send2)
        group = shape((GROUP, TOK), F32)
        own1, own2, *sends, cen = call(
            core_sum_kernel,
            "core_sum",
            [SMEM] + [VMEM] * 5,
            (group, group)
            + (shape((SENT, TOK), BF16),) * 3
            + (shape((GROUP, TOK), BF16),) * 3
            + (row,),
            [pltpu.VMEM((SENT, TOK), F32)],
            limit=12,
        )(idx, keep1, keep2, got1, got2, cen)
        parts1 = [shift(s, "tensor", N_T, e) for e, s in zip(tensor_shifts, sends[:3])]
        parts2 = [shift(s, "tensor", N_T, e) for e, s in zip(tensor_shifts, sends[3:])]
        send, cen = call(
            tensor_sum_kernel,
            "tensor_sum",
            [VMEM] * 5,
            (shape((SENT, TOK), BF16), row),
            [pltpu.VMEM((SENT, TOK), F32)],
            limit=8,
        )(own1, *parts1, cen)
        pair = lax.ppermute(send, "latent", [(i, i ^ 2) for i in range(N_L)])
        total, send, cen = call(
            pair_sum_kernel,
            "pair_sum",
            [VMEM] * 6,
            (group, shape((SENT, TOK), BF16), row),
            [pltpu.VMEM((SENT, TOK), F32)],
            limit=8,
        )(own2, *parts2, pair, cen)
        got = [shift(send, "latent", N_L, 4 * d) for d in (1, 2, 3)]

        def group_rows(array):
            pieces = array.reshape(N_Z // 2, 4, PIECE, -1)
            return lax.dynamic_index_in_dim(pieces, latent % 4, 1, False).reshape(GROUP, -1)

        gain_own, bias_own = (
            group_rows(lax.dynamic_slice_in_dim(v, tensor * CHUNK, CHUNK, 0))
            for v in (norm_gain, dec_bias)
        )
        cast, err = call(
            grad_kernel,
            "grad",
            [SMEM] + [VMEM] * 10,
            (shape((GROUP, TOK), BF16), row),
            limit=8,
        )(idx, total, *got, cen, root, gain_own, bias_own, group_rows(x_all), group_rows(g_all))

    with jax.named_scope("decode"):
        across = lax.ppermute(cast, "latent", [(i, i ^ 2) for i in range(N_L)])
        products = call(
            decode_kernel,
            "decode",
            [SMEM] + [VMEM] * 6,
            shape((TOK, WIDE), BF16),
            [pltpu.VMEM((CHUNK, TOK), BF16), pltpu.VMEM((CHUNK, TOK), F32)],
            limit=14,
        )(idx, cast, across, swap_core(cast), swap_core(across), err, dec)

    with jax.named_scope("scores"):
        got = lax.all_to_all(
            products.reshape(N_T * N_L, 4, WIDE), ("tensor", "latent"), 0, 0, tiled=True
        )
        scores, err = call(
            score_kernel,
            "score",
            [SMEM, VMEM, VMEM],
            (shape((4, SLOTS * BLOCK), BF16), shape((1, 4), F32)),
            [pltpu.VMEM((N_L, 4, WIDE), F32)],
            limit=8,
        )(slots, got, latent_acts)
    return scores, err.reshape(4)


def solution(mesh):
    return jax.shard_map(
        on_device,
        mesh=mesh,
        in_specs=(
            P("dp", ("tensor", "latent")),
            P("dp", ("tensor", "latent")),
            P(),
            P("dp", ("tensor", "latent")),
            P("dp", ("tensor", "latent")),
            P("dp", ("tensor", "latent")),
            P("latent", "tensor"),
            P(),
            P("dp", None),
            P("dp"),
            P(("dp", "tensor", "latent"), None),
        ),
        out_specs=(P(("dp", "tensor", "latent"), None), P(("dp", "tensor", "latent"))),
        check_vma=False,
    )
```

time: 186 us -> 144 us (0.77)
  starting transfers between devices: 73.9 us -> 38 us
  waiting for transfers between devices: 55.2 us -> 47.9 us
  Pallas kernels: 17 us -> 19.4 us
  blocking collectives: 21.2 us -> 23.4 us
    ppermute x35 -> x16, starting transfers between devices: 56.7 us -> 26 us  [shift(): return lax.ppermute(x, axis, [(i, (i + by) % size) for i in range(size)])]
    ppermute x35 -> x16, waiting for transfers between devices: 44.3 us -> 22.4 us  [shift(): return lax.ppermute(x, axis, [(i, (i + by) % size) for i in range(size)])]
    all_to_all x1, waiting for transfers between devices: 8.63 us -> 17.4 us  [on_device(): lax.all_to_all(products.reshape(N_T * N_L, 4, WIDE), ('tensor', 'latent')...]
    ppermute x5 -> x7, starting transfers between devices: 11.3 us -> 5.38 us  [swap_core(): return lax.ppermute(x, 'latent', [(i, i ^ 1) for i in range(N_L)])]
    ppermute x5 -> x7, waiting for transfers between devices: 2.27 us -> 5.48 us  [swap_core(): return lax.ppermute(x, 'latent', [(i, i ^ 1) for i in range(N_L)])]
    ppermute x0 -> x2, waiting for transfers between devices: none -> 2.6 us  [the longest x1 2.59 us: on_device(): across = lax.ppermute(cast, 'latent', [(i, i ^ 2) for i in range(N_L)])]
    pallas_call x6 -> x8, Pallas kernels: 15.8 us -> 18.1 us  [the longest x1 6.73 us: on_device(): call(mlp_kernel, 'mlp', [SMEM] + [VMEM] * 14, (shape((N_T, GROUP, TOK), F...]
    all_gather x1, blocking collectives: 21.2 us -> 23.4 us  [on_device(): column = lax.all_gather(jnp.concatenate([x_own, g_own]), 'latent', axis=0)]
  transfers between devices with their start and end apart: 41 -> 26, of which waited for: 14 -> 16; matrix products, arithmetic and copies ran while one was open for 5% -> 4% of each run, Pallas kernels for 0% -> 4%
where the time goes in v2:
time: 144 us
  waiting for transfers between devices  47.9 us (33%)
  starting transfers between devices  38 us (26%)
  blocking collectives  23.4 us (16%)
  Pallas kernels  19.4 us (13%)
  local copies, waits for them, and re-layouts  13 us (9%)
    ppermute x16, starting transfers between devices, shift(): return lax.ppermute(x, axis, [(i, (i + by) % size) for i in range(size)])  26 us
    all_gather x1, blocking collectives, on_device(): column = lax.all_gather(jnp.concatenate([x_own, g_own]), 'latent', axis=0)  23.4 us
    ppermute x16, waiting for transfers between devices, shift(): return lax.ppermute(x, axis, [(i, (i + by) % size) for i in range(size)])  22.4 us
    all_to_all x1, waiting for transfers between devices, on_device(): lax.all_to_all(products.reshape(N_T * N_L, 4, WIDE), ('tensor', 'latent')...  17.4 us
    unnamed x24, local copies, waits for them, and re-layouts  8.21 us
    pallas_call x1, Pallas kernels, on_device(): call(mlp_kernel, 'mlp', [SMEM] + [VMEM] * 14, (shape((N_T, GROUP, TOK), F...  6.73 us
    all_to_all x1, starting transfers between devices, on_device(): lax.all_to_all(products.reshape(N_T * N_L, 4, WIDE), ('tensor', 'latent')...  6.39 us
    pallas_call x1, Pallas kernels, on_device(): pl.pallas_call(fetch_kernel, name='fetch', in_specs=[SMEM, HBM, ANY], out...  5.52 us
  transfers between devices with their start and end apart: 26, of which 16 were waited for; matrix products, arithmetic and copies ran while one was open for 4% of the time, Pallas kernels for 4%

profile of v2, /device:TPU:1, one launch (start us, length us, event | category | flops | bytes accessed | tf_op | source)
XLA Modules:
  0.0 143.9 jit_solution(1675084295190943760)
XLA Ops:
  0.7 2.3 %stack.26.w0 = bf16[3,224,896]{2,1,0:T(8,128)(2,1)} custom-call(bf16[224,896]{1,0:T(8,128)(2,1)} %bitcast.29, bf16[224,896]{1,0:T(8,128)(2,1)} %bitcast.30, bf16[224,896]{1,0:T(8,128)(2,1)} %bitcast.31), custom_call_target="tpu_custom_call" | custom-call | tf_op jit(solution)/shard_map/weight_rows/stack/pallas_call | solution.py:305
  3.0 2.2 %collective-permute-start.6 = (bf16[3,224,896]{2,1,0:T(8,128)(2,1)}, bf16[3,224,896]{2,1,0:T(8,128)(2,1)S(1)}, u32[]{:S(2)}, u32[]{:S(2)}) collective-permute-start(bf16[3,224,896]{2,1,0:T(8,128)(2,1)} %stack.26.w0), channel_id=1, source_target_pairs={{0,64},{64,128},{128,192},{192,0},{1,65},{65,129},{129,193},{193,1... | collective-permute-start | bytes 3612680 | tf_op jit(solution)/shard_map/weight_rows/ppermute | solution.py:52
  5.2 1.5 %collective-permute-start.7 = (bf16[3,224,896]{2,1,0:T(8,128)(2,1)}, bf16[3,224,896]{2,1,0:T(8,128)(2,1)S(1)}, u32[]{:S(2)}, u32[]{:S(2)}) collective-permute-start(bf16[3,224,896]{2,1,0:T(8,128)(2,1)} %stack.26.w0), channel_id=1, source_target_pairs={{0,192},{64,0},{128,64},{192,128},{1,193},{65,1},{129,65},{193,129... | collective-permute-start | bytes 3612680 | tf_op jit(solution)/shard_map/weight_rows/ppermute | solution.py:52
  6.7 23.4 %all-gather = bf16[1792,256]{1,0:T(8,128)(2,1)S(1)} all-gather(bf16[112,256]{1,0:T(8,128)(2,1)S(1)} %pad_maximum_fusion), channel_id=2, replica_groups=mesh['dp'=4,'tensor'=4,'latent'=16] {'latent'}, dimensions={0}, use_global_device_ids=true | all-gather | bytes 974848 | tf_op jit(solution)/shard_map/token_features/all_gather | solution.py:321
  30.3 1.3 collective-permute-start
  31.6 2.5 %collective-permute-start.1 = (bf16[896,256]{1,0:T(8,128)(2,1)S(1)}, bf16[896,256]{1,0:T(8,128)(2,1)}, u32[]{:S(2)}, u32[]{:S(2)}) collective-permute-start(bf16[896,256]{1,0:T(8,128)(2,1)S(1)} %broadcast_select_fusion), channel_id=1, source_target_pairs={{0,32},{16,48},{32,0},{48,16},{1,33},{17,49},{33,1},{49,17},{2,34}... | collective-permute-start | bytes 1376264 | tf_op jit(solution)/shard_map/token_features/ppermute | solution.py:52
  34.1 1.2 collective-permute-start.2
  35.3 0.9 slice.18
  36.3 1.0 slice.19
  37.3 2.6 %collective-permute-start.9 = (bf16[3,112,896]{2,1,0:T(8,128)(2,1)}, bf16[3,112,896]{2,1,0:T(8,128)(2,1)}, u32[]{:S(2)}, u32[]{:S(2)}) collective-permute-start(bf16[3,112,896]{2,1,0:T(8,128)(2,1)} %slice.19), channel_id=1, source_target_pairs={{0,192},{64,0},{128,64},{192,128},{1,193},{65,1},{129,65},{193,129... | collective-permute-start | bytes 1806344 | tf_op jit(solution)/shard_map/weight_rows/ppermute | solution.py:52
  40.2 3.4 %collective-permute-done._ = bf16[896,256]{1,0:T(8,128)(2,1)} collective-permute-done((bf16[896,256]{1,0:T(8,128)(2,1)S(1)}, bf16[896,256]{1,0:T(8,128)(2,1)}, u32[]{:S(2)}, u32[]{:S(2)}) %collective-permute-start) | collective-permute-done | bytes 458784 | tf_op jit(solution)/shard_map/token_features/ppermute | solution.py:52
  43.7 3.1 %copy-done = bf16[4096,896]{1,0:T(8,128)(2,1)S(1)} copy-done((bf16[4096,896]{1,0:T(8,128)(2,1)S(1)}, bf16[4096,896]{1,0:T(8,128)(2,1)}, u32[]{:S(2)}) %copy-start) | copy-done | bytes 7340056
  46.8 5.5 %fetch.1 = (bf16[2,1024,896]{2,1,0:T(8,128)(2,1)S(1)}, bf16[896,256]{1,0:T(8,128)(2,1)}) custom-call(s32[2,8]{1,0:T(2,128)S(1)} %select_reduce_fusion.ids, bf16[4096,896]{1,0:T(8,128)(2,1)S(1)} %copy-done, bf16[896,256]{1,0:T(8,128)(2,1)} %collective-permute-done._), custom_call_target="tpu_custom_call", output_to_operand_aliasing={{1}: (2, {})} | custom-call | tf_op jit(solution)/shard_map/token_features/fetch/pallas_call | solution.py:326
  52.3 1.8 %copy-done.2 = bf16[2,1024,896]{2,1,0:T(8,128)(2,1)} copy-done((bf16[2,1024,896]{2,1,0:T(8,128)(2,1)}, bf16[2,1024,896]{2,1,0:T(8,128)(2,1)S(1)}, u32[]{:S(2)}) %copy-start.2) | copy-done | bytes 3670040
  54.1 1.0 collective-permute-start.3
  55.6 1.2 collective-permute-done.3.b1
  56.8 0.7 collective-permute-done.4.b2
  57.5 0.7 collective-permute-done.5.b3
  58.2 1.3 copy-done.5
  59.4 6.7 %mlp.1 = (f32[4,224,256]{2,1,0:T(8,128)S(1)}, f32[4,224,256]{2,1,0:T(8,128)S(1)}, bf16[4,240,256]{2,1,0:T(8,128)(2,1)S(1)}, bf16[4,224,256]{2,1,0:T(8,128)(2,1)S...) custom-call(s32[4]{0:T(128)S(1)} %pad_add_fusion.1.idx, bf16[896,256]{1,0:T(8,128)(2,1)S(1)} %bitcast.23, ...), custom_call_target="tpu_custom_call" | custom-call | tf_op jit(solution)/shard_map/mlp/mlp/pallas_call | solution.py:340
  67.0 2.0 %collective-permute-done.11.got2 = bf16[4,224,256]{2,1,0:T(8,128)(2,1)S(1)} collective-permute-done((bf16[4,224,256]{2,1,0:T(8,128)(2,1)S(1)}, bf16[4,224,256]{2,1,0:T(8,128)(2,1)S(1)}, u32[]{:S(2)}, u32[]{:S(2)}) %collective-permute-start.11) | collective-permute-done | bytes 458784 | tf_op jit(solution)/shard_map/hidden_sums/ppermute | solution.py:56
  69.0 0.7 core_sum.1
  70.4 2.4 %collective-permute-start.16 = (bf16[240,256]{1,0:T(8,128)(2,1)S(1)}, bf16[240,256]{1,0:T(8,128)(2,1)S(1)}, u32[]{:S(2)}, u32[]{:S(2)}) collective-permute-start(bf16[240,256]{1,0:T(8,128)(2,1)S(1)} %get-tuple-element.40), channel_id=1, source_target_pairs={{0,32},{16,48},{32,0},{48,16},{1,33},{17,49},{33,1},{49,17},{2,34}... | collective-permute-start | bytes 368648 | tf_op jit(solution)/shard_map/hidden_sums/ppermute | solution.py:52
  72.8 1.2 collective-permute-start.17
  74.0 1.6 %collective-permute-done.15.r1 = bf16[240,256]{1,0:T(8,128)(2,1)S(1)} collective-permute-done((bf16[240,256]{1,0:T(8,128)(2,1)S(1)}, bf16[240,256]{1,0:T(8,128)(2,1)S(1)}, u32[]{:S(2)}, u32[]{:S(2)}) %collective-permute-start.15) | collective-permute-done | bytes 122912 | tf_op jit(solution)/shard_map/hidden_sums/ppermute | solution.py:52
  75.5 3.0 %collective-permute-done.16.r2 = bf16[240,256]{1,0:T(8,128)(2,1)S(1)} collective-permute-done((bf16[240,256]{1,0:T(8,128)(2,1)S(1)}, bf16[240,256]{1,0:T(8,128)(2,1)S(1)}, u32[]{:S(2)}, u32[]{:S(2)}) %collective-permute-start.16) | collective-permute-done | bytes 122912 | tf_op jit(solution)/shard_map/hidden_sums/ppermute | solution.py:52
  78.7 2.5 %collective-permute-start.12 = (bf16[224,256]{1,0:T(8,128)(2,1)S(1)}, bf16[224,256]{1,0:T(8,128)(2,1)S(1)}, u32[]{:S(2)}, u32[]{:S(2)}) collective-permute-start(bf16[224,256]{1,0:T(8,128)(2,1)S(1)} %get-tuple-element.35), channel_id=1, source_target_pairs={{0,16},{16,32},{32,48},{48,0},{1,17},{17,33},{33,49},{49,1},{2,18}... | collective-permute-start | bytes 344072 | tf_op jit(solution)/shard_map/hidden_sums/ppermute | solution.py:52
  81.1 1.6 %collective-permute-start.13 = (bf16[224,256]{1,0:T(8,128)(2,1)S(1)}, bf16[224,256]{1,0:T(8,128)(2,1)S(1)}, u32[]{:S(2)}, u32[]{:S(2)}) collective-permute-start(bf16[224,256]{1,0:T(8,128)(2,1)S(1)} %get-tuple-element.36), channel_id=1, source_target_pairs={{0,32},{16,48},{32,0},{48,16},{1,33},{17,49},{33,1},{49,17},{2,34}... | collective-permute-start | bytes 344072 | tf_op jit(solution)/shard_map/hidden_sums/ppermute | solution.py:52
  82.8 0.8 collective-permute-start.14
  83.8 3.6 %collective-permute-done.13.r2 = bf16[224,256]{1,0:T(8,128)(2,1)S(1)} collective-permute-done((bf16[224,256]{1,0:T(8,128)(2,1)S(1)}, bf16[224,256]{1,0:T(8,128)(2,1)S(1)}, u32[]{:S(2)}, u32[]{:S(2)}) %collective-permute-start.13) | collective-permute-done | bytes 114720 | tf_op jit(solution)/shard_map/hidden_sums/ppermute | solution.py:52
  88.2 2.9 %collective-permute-start.20 = (bf16[240,256]{1,0:T(8,128)(2,1)S(1)}, bf16[240,256]{1,0:T(8,128)(2,1)S(1)}, u32[]{:S(2)}, u32[]{:S(2)}) collective-permute-start(bf16[240,256]{1,0:T(8,128)(2,1)S(1)} %get-tuple-element.46), channel_id=1, source_target_pairs={{0,8},{1,9},{2,10},{3,11},{4,12},{5,13},{6,14},{7,15},{8,0},{9,1},... | collective-permute-start | bytes 368648 | tf_op jit(solution)/shard_map/hidden_sums/ppermute | solution.py:52
  91.0 2.5 %collective-permute-start.21 = (bf16[240,256]{1,0:T(8,128)(2,1)S(1)}, bf16[240,256]{1,0:T(8,128)(2,1)S(1)}, u32[]{:S(2)}, u32[]{:S(2)}) collective-permute-start(bf16[240,256]{1,0:T(8,128)(2,1)S(1)} %get-tuple-element.46), channel_id=1, source_target_pairs={{0,12},{1,13},{2,14},{3,15},{4,0},{5,1},{6,2},{7,3},{8,4},{9,5},{1... | collective-permute-start | bytes 368648 | tf_op jit(solution)/shard_map/hidden_sums/ppermute | solution.py:52
  93.7 0.8 dynamic_slice.34
  94.9 2.4 %collective-permute-done.19.r1 = bf16[240,256]{1,0:T(8,128)(2,1)S(1)} collective-permute-done((bf16[240,256]{1,0:T(8,128)(2,1)S(1)}, bf16[240,256]{1,0:T(8,128)(2,1)S(1)}, u32[]{:S(2)}, u32[]{:S(2)}) %collective-permute-start.19) | collective-permute-done | bytes 122912 | tf_op jit(solution)/shard_map/hidden_sums/ppermute | solution.py:52
  97.4 1.8 %collective-permute-done.20.r2 = bf16[240,256]{1,0:T(8,128)(2,1)S(1)} collective-permute-done((bf16[240,256]{1,0:T(8,128)(2,1)S(1)}, bf16[240,256]{1,0:T(8,128)(2,1)S(1)}, u32[]{:S(2)}, u32[]{:S(2)}) %collective-permute-start.20) | collective-permute-done | bytes 122912 | tf_op jit(solution)/shard_map/hidden_sums/ppermute | solution.py:52
  99.2 5.8 %collective-permute-done.21.r3 = bf16[240,256]{1,0:T(8,128)(2,1)S(1)} collective-permute-done((bf16[240,256]{1,0:T(8,128)(2,1)S(1)}, bf16[240,256]{1,0:T(8,128)(2,1)S(1)}, u32[]{:S(2)}, u32[]{:S(2)}) %collective-permute-start.21) | collective-permute-done | bytes 122912 | tf_op jit(solution)/shard_map/hidden_sums/ppermute | solution.py:52
  105.0 0.7 grad.1
  105.8 1.0 collective-permute-start.23
  106.9 2.6 %collective-permute-done.22.g1 = bf16[224,256]{1,0:T(8,128)(2,1)S(1)} collective-permute-done((bf16[224,256]{1,0:T(8,128)(2,1)S(1)}, bf16[224,256]{1,0:T(8,128)(2,1)S(1)}, u32[]{:S(2)}, u32[]{:S(2)}) %collective-permute-start.22) | collective-permute-done | bytes 114720 | tf_op jit(solution)/shard_map/decode/ppermute | solution.py:418
  109.5 2.1 %collective-permute-start.24 = (bf16[224,256]{1,0:T(8,128)(2,1)S(1)}, bf16[224,256]{1,0:T(8,128)(2,1)S(1)}, u32[]{:S(2)}, u32[]{:S(2)}) collective-permute-start(bf16[224,256]{1,0:T(8,128)(2,1)S(1)} %collective-permute-done.22.g1), channel_id=1, source_target_pairs={{0,1},{1,0},{2,3},{3,2},{4,5},{5,4},{6,7},{7,6},{8,9},{9,8},{10,11... | collective-permute-start | bytes 344072 | tf_op jit(solution)/shard_map/decode/ppermute | solution.py:56
  111.6 1.0 collective-permute-done.24.g3
  112.5 2.0 %copy-done.3 = bf16[2,1024,896]{2,1,0:T(8,128)(2,1)S(1)} copy-done((bf16[2,1024,896]{2,1,0:T(8,128)(2,1)S(1)}, bf16[2,1024,896]{2,1,0:T(8,128)(2,1)}, u32[]{:S(2)}) %copy-start.3) | copy-done | bytes 3670040
  114.6 1.9 %decode.1 = bf16[256,1152]{1,0:T(8,128)(2,1)S(1)} custom-call(s32[4]{0:T(128)S(1)} %pad_add_fusion.1.idx, bf16[224,256]{1,0:T(8,128)(2,1)S(1)} %get-tuple-element.49.g0, bf16[224,256]{1,0:T(8,128)(2,1)S(1)} %collective-permute-done.22.g1, bf16[224,256]{1,0:T(8,128)(2,1)S(1)} %collective-permute-done.23.g2, bf16[224,256]{1,0:T(8,128)(2,1)S(1)} %collective-permute-done.24.g3, ...), custom_call_target="tpu_custom_call" | custom-call | tf_op jit(solution)/shard_map/decode/decode/pallas_call | solution.py:419
  116.5 1.0 reshape.86
  117.5 6.4 %all-to-all-start = ((bf16[64,4,1152]{2,1,0:T(4,128)(2,1)}), bf16[64,4,1152]{2,1,0:T(4,128)(2,1)S(1)}, u32[]{:S(2)}, u32[]{:S(2)}) async-start(bf16[64,4,1152]{2,1,0:T(4,128)(2,1)} %reshape.86), calls=%async_computation | async-start | bytes 1179648 | tf_op jit(solution)/shard_map/scores/all_to_all | solution.py:429
  124.5 0.6 compare_convert_fusion
  125.2 17.4 %all-to-all-done.got = bf16[64,4,1152]{2,1,0:T(4,128)(2,1)S(1)} async-done(((bf16[64,4,1152]{2,1,0:T(4,128)(2,1)}), bf16[64,4,1152]{2,1,0:T(4,128)(2,1)S(1)}, u32[]{:S(2)}, u32[]{:S(2)}) %all-to-all-start) | async-done | bytes 589856 | tf_op jit(solution)/shard_map/scores/all_to_all | solution.py:429
  142.6 1.3 score.1
  (63 shorter events, 5.1 us)
Async XLA Ops:
  0.6 6.1 %copy-start.8 = (bf16[256,56]{0,1:T(8,128)(2,1)S(1)}, bf16[256,56]{0,1:T(8,128)(2,1)}, u32[]{:S(2)}) copy-start(bf16[256,56]{0,1:T(8,128)(2,1)} %param.12) | copy-start | bytes 86020
  0.6 6.1 %copy-start.9 = (bf16[256,56]{0,1:T(8,128)(2,1)S(1)}, bf16[256,56]{0,1:T(8,128)(2,1)}, u32[]{:S(2)}) copy-start(bf16[256,56]{0,1:T(8,128)(2,1)} %param.11) | copy-start | bytes 86020
  3.0 32.4 %collective-permute-start.6 = (bf16[3,224,896]{2,1,0:T(8,128)(2,1)}, bf16[3,224,896]{2,1,0:T(8,128)(2,1)S(1)}, u32[]{:S(2)}, u32[]{:S(2)}) collective-permute-start(bf16[3,224,896]{2,1,0:T(8,128)(2,1)} %stack.26.w0), channel_id=1, source_target_pairs={{0,64},{64,128},{128,192},{192,0},{1,65},{65,129},{129,193},{193,1... | collective-permute-start | bytes 3612680 | tf_op jit(solution)/shard_map/weight_rows/ppermute | solution.py:52
  5.2 31.2 %collective-permute-start.7 = (bf16[3,224,896]{2,1,0:T(8,128)(2,1)}, bf16[3,224,896]{2,1,0:T(8,128)(2,1)S(1)}, u32[]{:S(2)}, u32[]{:S(2)}) collective-permute-start(bf16[3,224,896]{2,1,0:T(8,128)(2,1)} %stack.26.w0), channel_id=1, source_target_pairs={{0,192},{64,0},{128,64},{192,128},{1,193},{65,1},{129,65},{193,129... | collective-permute-start | bytes 3612680 | tf_op jit(solution)/shard_map/weight_rows/ppermute | solution.py:52
  30.1 5.1 %copy-start.10 = (s32[2,32]{1,0:T(2,128)S(1)}, s32[2,32]{1,0:T(2,128)}, u32[]{:S(2)}) copy-start(s32[2,32]{1,0:T(2,128)} %param.19) | copy-start | bytes 772
  30.3 13.4 %collective-permute-start = (bf16[896,256]{1,0:T(8,128)(2,1)S(1)}, bf16[896,256]{1,0:T(8,128)(2,1)}, u32[]{:S(2)}, u32[]{:S(2)}) collective-permute-start(bf16[896,256]{1,0:T(8,128)(2,1)S(1)} %broadcast_select_fusion), channel_id=1, source_target_pairs={{0,16},{16,32},{32,48},{48,0},{1,17},{17,33},{33,49},{49,1},{2,18}... | collective-permute-start | bytes 1376264 | tf_op jit(solution)/shard_map/token_features/ppermute | solution.py:52
  31.6 23.4 %collective-permute-start.1 = (bf16[896,256]{1,0:T(8,128)(2,1)S(1)}, bf16[896,256]{1,0:T(8,128)(2,1)}, u32[]{:S(2)}, u32[]{:S(2)}) collective-permute-start(bf16[896,256]{1,0:T(8,128)(2,1)S(1)} %broadcast_select_fusion), channel_id=1, source_target_pairs={{0,32},{16,48},{32,0},{48,16},{1,33},{17,49},{33,1},{49,17},{2,34}... | collective-permute-start | bytes 1376264 | tf_op jit(solution)/shard_map/token_features/ppermute | solution.py:52
  34.1 21.4 %collective-permute-start.2 = (bf16[896,256]{1,0:T(8,128)(2,1)S(1)}, bf16[896,256]{1,0:T(8,128)(2,1)}, u32[]{:S(2)}, u32[]{:S(2)}) collective-permute-start(bf16[896,256]{1,0:T(8,128)(2,1)S(1)} %broadcast_select_fusion), channel_id=1, source_target_pairs={{0,48},{16,0},{32,16},{48,32},{1,49},{17,1},{33,17},{49,33},{2,50}... | collective-permute-start | bytes 1376264 | tf_op jit(solution)/shard_map/token_features/ppermute | solution.py:52
  36.3 21.9 %collective-permute-start.8 = (bf16[3,112,896]{2,1,0:T(8,128)(2,1)}, bf16[3,112,896]{2,1,0:T(8,128)(2,1)}, u32[]{:S(2)}, u32[]{:S(2)}) collective-permute-start(bf16[3,112,896]{2,1,0:T(8,128)(2,1)} %slice.18), channel_id=1, source_target_pairs={{0,64},{64,128},{128,192},{192,0},{1,65},{65,129},{129,193},{193,1... | collective-permute-start | bytes 1806344 | tf_op jit(solution)/shard_map/weight_rows/ppermute | solution.py:52
  36.3 3.9 %copy-start.4 = (bf16[3,224,896]{2,1,0:T(8,128)(2,1)}, bf16[3,224,896]{2,1,0:T(8,128)(2,1)S(1)}, u32[]{:S(2)}) copy-start(bf16[3,224,896]{2,1,0:T(8,128)(2,1)S(1)} %collective-permute-done.7.w2) | copy-start | bytes 3612676
  37.3 20.8 %collective-permute-start.9 = (bf16[3,112,896]{2,1,0:T(8,128)(2,1)}, bf16[3,112,896]{2,1,0:T(8,128)(2,1)}, u32[]{:S(2)}, u32[]{:S(2)}) collective-permute-start(bf16[3,112,896]{2,1,0:T(8,128)(2,1)} %slice.19), channel_id=1, source_target_pairs={{0,192},{64,0},{128,64},{192,128},{1,193},{65,1},{129,65},{193,129... | collective-permute-start | bytes 1806344 | tf_op jit(solution)/shard_map/weight_rows/ppermute | solution.py:52
  43.7 3.1 %copy-start = (bf16[4096,896]{1,0:T(8,128)(2,1)S(1)}, bf16[4096,896]{1,0:T(8,128)(2,1)}, u32[]{:S(2)}) copy-start(bf16[4096,896]{1,0:T(8,128)(2,1)} %decoder.1) | copy-start | bytes 22020100
  46.8 11.4 %copy-start.1 = (bf16[3,224,896]{2,1,0:T(8,128)(2,1)S(1)}, bf16[3,224,896]{2,1,0:T(8,128)(2,1)}, u32[]{:S(2)}) copy-start(bf16[3,224,896]{2,1,0:T(8,128)(2,1)} %stack.26.w0) | copy-start | bytes 3612676
  46.8 11.4 %copy-start.7 = (f32[3584]{0:T(1024)S(1)}, f32[3584]{0:T(1024)}, u32[]{:S(2)}) copy-start(f32[3584]{0:T(1024)} %param.13) | copy-start | bytes 43012
  52.3 1.8 %copy-start.2 = (bf16[2,1024,896]{2,1,0:T(8,128)(2,1)}, bf16[2,1024,896]{2,1,0:T(8,128)(2,1)S(1)}, u32[]{:S(2)}) copy-start(bf16[2,1024,896]{2,1,0:T(8,128)(2,1)S(1)} %get-tuple-element.51.dec) | copy-start | bytes 11010052
  54.1 2.7 %collective-permute-start.3 = (bf16[896,256]{1,0:T(8,128)(2,1)}, bf16[896,256]{1,0:T(8,128)(2,1)}, u32[]{:S(2)}, u32[]{:S(2)}) collective-permute-start(bf16[896,256]{1,0:T(8,128)(2,1)} %get-tuple-element.28.a1), channel_id=1, source_target_pairs={{0,1},{1,0},{2,3},{3,2},{4,5},{5,4},{6,7},{7,6},{8,9},{9,8},{10,11... | collective-permute-start | bytes 1376264 | tf_op jit(solution)/shard_map/token_features/ppermute | solution.py:56
  55.0 2.4 %collective-permute-start.4 = (bf16[896,256]{1,0:T(8,128)(2,1)}, bf16[896,256]{1,0:T(8,128)(2,1)}, u32[]{:S(2)}, u32[]{:S(2)}) collective-permute-start(bf16[896,256]{1,0:T(8,128)(2,1)} %collective-permute-done.1.a2), channel_id=1, source_target_pairs={{0,1},{1,0},{2,3},{3,2},{4,5},{5,4},{6,7},{7,6},{8,9},{9,8},{10,11... | collective-permute-start | bytes 1376264 | tf_op jit(solution)/shard_map/token_features/ppermute | solution.py:56
  55.5 2.7 %collective-permute-start.5 = (bf16[896,256]{1,0:T(8,128)(2,1)}, bf16[896,256]{1,0:T(8,128)(2,1)}, u32[]{:S(2)}, u32[]{:S(2)}) collective-permute-start(bf16[896,256]{1,0:T(8,128)(2,1)} %collective-permute-done.2.a3), channel_id=1, source_target_pairs={{0,1},{1,0},{2,3},{3,2},{4,5},{5,4},{6,7},{7,6},{8,9},{9,8},{10,11... | collective-permute-start | bytes 1376264 | tf_op jit(solution)/shard_map/token_features/ppermute | solution.py:56
  58.2 1.3 copy-start.5
  66.2 2.8 %collective-permute-start.10 = (bf16[4,240,256]{2,1,0:T(8,128)(2,1)S(1)}, bf16[4,240,256]{2,1,0:T(8,128)(2,1)S(1)}, u32[]{:S(2)}, u32[]{:S(2)}) collective-permute-start(bf16[4,240,256]{2,1,0:T(8,128)(2,1)S(1)} %get-tuple-element.31), channel_id=1, source_target_pairs={{0,1},{1,0},{2,3},{3,2},{4,5},{5,4},{6,7},{7,6},{8,9},{9,8},{10,11... | collective-permute-start | bytes 1474568 | tf_op jit(solution)/shard_map/hidden_sums/ppermute | solution.py:56
  66.8 2.2 %collective-permute-start.11 = (bf16[4,224,256]{2,1,0:T(8,128)(2,1)S(1)}, bf16[4,224,256]{2,1,0:T(8,128)(2,1)S(1)}, u32[]{:S(2)}, u32[]{:S(2)}) collective-permute-start(bf16[4,224,256]{2,1,0:T(8,128)(2,1)S(1)} %get-tuple-element.32), channel_id=1, source_target_pairs={{0,1},{1,0},{2,3},{3,2},{4,5},{5,4},{6,7},{7,6},{8,9},{9,8},{10,11... | collective-permute-start | bytes 1376264 | tf_op jit(solution)/shard_map/hidden_sums/ppermute | solution.py:56
  69.7 5.8 %collective-permute-start.15 = (bf16[240,256]{1,0:T(8,128)(2,1)S(1)}, bf16[240,256]{1,0:T(8,128)(2,1)S(1)}, u32[]{:S(2)}, u32[]{:S(2)}) collective-permute-start(bf16[240,256]{1,0:T(8,128)(2,1)S(1)} %get-tuple-element.39), channel_id=1, source_target_pairs={{0,16},{16,32},{32,48},{48,0},{1,17},{17,33},{33,49},{49,1},{2,18}... | collective-permute-start | bytes 368648 | tf_op jit(solution)/shard_map/hidden_sums/ppermute | solution.py:52
  70.4 8.2 %collective-permute-start.16 = (bf16[240,256]{1,0:T(8,128)(2,1)S(1)}, bf16[240,256]{1,0:T(8,128)(2,1)S(1)}, u32[]{:S(2)}, u32[]{:S(2)}) collective-permute-start(bf16[240,256]{1,0:T(8,128)(2,1)S(1)} %get-tuple-element.40), channel_id=1, source_target_pairs={{0,32},{16,48},{32,0},{48,16},{1,33},{17,49},{33,1},{49,17},{2,34}... | collective-permute-start | bytes 368648 | tf_op jit(solution)/shard_map/hidden_sums/ppermute | solution.py:52
  72.8 5.7 %collective-permute-start.17 = (bf16[240,256]{1,0:T(8,128)(2,1)S(1)}, bf16[240,256]{1,0:T(8,128)(2,1)S(1)}, u32[]{:S(2)}, u32[]{:S(2)}) collective-permute-start(bf16[240,256]{1,0:T(8,128)(2,1)S(1)} %get-tuple-element.41), channel_id=1, source_target_pairs={{0,48},{16,0},{32,16},{48,32},{1,49},{17,1},{33,17},{49,33},{2,50}... | collective-permute-start | bytes 368648 | tf_op jit(solution)/shard_map/hidden_sums/ppermute | solution.py:52
  78.6 9.4 %collective-permute-start.18 = (bf16[240,256]{1,0:T(8,128)(2,1)S(1)}, bf16[240,256]{1,0:T(8,128)(2,1)S(1)}, u32[]{:S(2)}, u32[]{:S(2)}) collective-permute-start(bf16[240,256]{1,0:T(8,128)(2,1)S(1)} %get-tuple-element.43), channel_id=1, source_target_pairs={{0,2},{1,3},{2,0},{3,1},{4,6},{5,7},{6,4},{7,5},{8,10},{9,11},{10,... | collective-permute-start | bytes 368648 | tf_op jit(solution)/shard_map/hidden_sums/ppermute | solution.py:390
  78.7 5.1 %collective-permute-start.12 = (bf16[224,256]{1,0:T(8,128)(2,1)S(1)}, bf16[224,256]{1,0:T(8,128)(2,1)S(1)}, u32[]{:S(2)}, u32[]{:S(2)}) collective-permute-start(bf16[224,256]{1,0:T(8,128)(2,1)S(1)} %get-tuple-element.35), channel_id=1, source_target_pairs={{0,16},{16,32},{32,48},{48,0},{1,17},{17,33},{33,49},{49,1},{2,18}... | collective-permute-start | bytes 344072 | tf_op jit(solution)/shard_map/hidden_sums/ppermute | solution.py:52
  81.1 6.2 %collective-permute-start.13 = (bf16[224,256]{1,0:T(8,128)(2,1)S(1)}, bf16[224,256]{1,0:T(8,128)(2,1)S(1)}, u32[]{:S(2)}, u32[]{:S(2)}) collective-permute-start(bf16[224,256]{1,0:T(8,128)(2,1)S(1)} %get-tuple-element.36), channel_id=1, source_target_pairs={{0,32},{16,48},{32,0},{48,16},{1,33},{17,49},{33,1},{49,17},{2,34}... | collective-permute-start | bytes 344072 | tf_op jit(solution)/shard_map/hidden_sums/ppermute | solution.py:52
  82.8 5.2 %collective-permute-start.14 = (bf16[224,256]{1,0:T(8,128)(2,1)S(1)}, bf16[224,256]{1,0:T(8,128)(2,1)S(1)}, u32[]{:S(2)}, u32[]{:S(2)}) collective-permute-start(bf16[224,256]{1,0:T(8,128)(2,1)S(1)} %get-tuple-element.37), channel_id=1, source_target_pairs={{0,48},{16,0},{32,16},{48,32},{1,49},{17,1},{33,17},{49,33},{2,50}... | collective-permute-start | bytes 344072 | tf_op jit(solution)/shard_map/hidden_sums/ppermute | solution.py:52
  88.0 9.3 %collective-permute-start.19 = (bf16[240,256]{1,0:T(8,128)(2,1)S(1)}, bf16[240,256]{1,0:T(8,128)(2,1)S(1)}, u32[]{:S(2)}, u32[]{:S(2)}) collective-permute-start(bf16[240,256]{1,0:T(8,128)(2,1)S(1)} %get-tuple-element.46), channel_id=1, source_target_pairs={{0,4},{1,5},{2,6},{3,7},{4,8},{5,9},{6,10},{7,11},{8,12},{9,13},{1... | collective-permute-start | bytes 368648 | tf_op jit(solution)/shard_map/hidden_sums/ppermute | solution.py:52
  88.2 11.0 %collective-permute-start.20 = (bf16[240,256]{1,0:T(8,128)(2,1)S(1)}, bf16[240,256]{1,0:T(8,128)(2,1)S(1)}, u32[]{:S(2)}, u32[]{:S(2)}) collective-permute-start(bf16[240,256]{1,0:T(8,128)(2,1)S(1)} %get-tuple-element.46), channel_id=1, source_target_pairs={{0,8},{1,9},{2,10},{3,11},{4,12},{5,13},{6,14},{7,15},{8,0},{9,1},... | collective-permute-start | bytes 368648 | tf_op jit(solution)/shard_map/hidden_sums/ppermute | solution.py:52
  91.0 13.9 %collective-permute-start.21 = (bf16[240,256]{1,0:T(8,128)(2,1)S(1)}, bf16[240,256]{1,0:T(8,128)(2,1)S(1)}, u32[]{:S(2)}, u32[]{:S(2)}) collective-permute-start(bf16[240,256]{1,0:T(8,128)(2,1)S(1)} %get-tuple-element.46), channel_id=1, source_target_pairs={{0,12},{1,13},{2,14},{3,15},{4,0},{5,1},{6,2},{7,3},{8,4},{9,5},{1... | collective-permute-start | bytes 368648 | tf_op jit(solution)/shard_map/hidden_sums/ppermute | solution.py:52
  105.7 3.7 %collective-permute-start.22 = (bf16[224,256]{1,0:T(8,128)(2,1)S(1)}, bf16[224,256]{1,0:T(8,128)(2,1)S(1)}, u32[]{:S(2)}, u32[]{:S(2)}) collective-permute-start(bf16[224,256]{1,0:T(8,128)(2,1)S(1)} %get-tuple-element.49.g0), channel_id=1, source_target_pairs={{0,2},{1,3},{2,0},{3,1},{4,6},{5,7},{6,4},{7,5},{8,10},{9,11},{10,... | collective-permute-start | bytes 344072 | tf_op jit(solution)/shard_map/decode/ppermute | solution.py:418
  105.8 5.7 %collective-permute-start.23 = (bf16[224,256]{1,0:T(8,128)(2,1)S(1)}, bf16[224,256]{1,0:T(8,128)(2,1)S(1)}, u32[]{:S(2)}, u32[]{:S(2)}) collective-permute-start(bf16[224,256]{1,0:T(8,128)(2,1)S(1)} %get-tuple-element.49.g0), channel_id=1, source_target_pairs={{0,1},{1,0},{2,3},{3,2},{4,5},{5,4},{6,7},{7,6},{8,9},{9,8},{10,11... | collective-permute-start | bytes 344072 | tf_op jit(solution)/shard_map/decode/ppermute | solution.py:56
  109.5 3.1 %collective-permute-start.24 = (bf16[224,256]{1,0:T(8,128)(2,1)S(1)}, bf16[224,256]{1,0:T(8,128)(2,1)S(1)}, u32[]{:S(2)}, u32[]{:S(2)}) collective-permute-start(bf16[224,256]{1,0:T(8,128)(2,1)S(1)} %collective-permute-done.22.g1), channel_id=1, source_target_pairs={{0,1},{1,0},{2,3},{3,2},{4,5},{5,4},{6,7},{7,6},{8,9},{9,8},{10,11... | collective-permute-start | bytes 344072 | tf_op jit(solution)/shard_map/decode/ppermute | solution.py:56
  112.5 2.0 %copy-start.3 = (bf16[2,1024,896]{2,1,0:T(8,128)(2,1)S(1)}, bf16[2,1024,896]{2,1,0:T(8,128)(2,1)}, u32[]{:S(2)}) copy-start(bf16[2,1024,896]{2,1,0:T(8,128)(2,1)} %copy-done.2) | copy-start | bytes 11010052
  116.5 7.4 %copy-start.11 = (s32[2]{0:T(128)S(1)}, s32[2]{0:T(128)}, u32[]{:S(2)}) copy-start(s32[2]{0:T(128)} %param.20) | copy-start | bytes 28
  116.5 26.1 %copy-start.6 = (bf16[4,4096]{1,0:T(4,128)(2,1)S(1)}, bf16[4,4096]{1,0:T(4,128)(2,1)}, u32[]{:S(2)}) copy-start(bf16[4,4096]{1,0:T(4,128)(2,1)} %acts.1) | copy-start | bytes 98308
  117.5 25.1 %all-to-all-start = ((bf16[64,4,1152]{2,1,0:T(4,128)(2,1)}), bf16[64,4,1152]{2,1,0:T(4,128)(2,1)S(1)}, u32[]{:S(2)}, u32[]{:S(2)}) async-start(bf16[64,4,1152]{2,1,0:T(4,128)(2,1)} %reshape.86), calls=%async_computation | async-start | bytes 1179648 | tf_op jit(solution)/shard_map/scores/all_to_all | solution.py:429

commit v3 on v2

--- a/solution.py
+++ b/solution.py
@@ -72,7 +72,7 @@
     dp, tensor, odd, core = idx[0], idx[1], lax.rem(idx[2], 2), idx[3]
     first = core == 0
     square = jnp.zeros((8, TOK), F32)
-    for e, (a, b) in enumerate(((x0, g0), (a1, b1), (a2, b2), (a3, b3))):
+    for e, a, b in ((0, x0, g0), (1, a1, b1), (3, a2, b2), (2, a3, b3)):
         at = pl.ds(pl.multiple_of(lax.rem(tensor - e + N_T, N_T) * CHUNK, 16), CHUNK)
         va, vb = a[...], b[...]
         if e:
@@ -215,17 +215,19 @@
 
 
 def fetch_kernel(ids, decoder, _, dec, passed, sems):
-    copies = []
-    for b in range(2):
-        for r in range(CAP):
-            rows = pl.ds(pl.multiple_of(ids[b, r] * BLOCK, BLOCK), BLOCK)
-            copy = pltpu.make_async_copy(
-                decoder.at[rows], dec.at[b, pl.ds(r * BLOCK, BLOCK)], sems.at[b, r]
-            )
-            copy.start()
-            copies.append(copy)
-    for copy in copies:
-        copy.wait()
+    def each(act):
+        for b in range(2):
+            for r in range(CAP):
+                index = ids[b, r]
+
+                @pl.when(index >= 0)
+                def _():
+                    rows = pl.ds(pl.multiple_of(jnp.maximum(index, 0) * BLOCK, BLOCK), BLOCK)
+                    into = dec.at[b, pl.ds(r * BLOCK, BLOCK)]
+                    act(pltpu.make_async_copy(decoder.at[rows], into, sems.at[b, r]))
+
+    each(lambda copy: copy.start())
+    each(lambda copy: copy.wait())
 
 
 def stack_kernel(a, b, c, out, sems):
@@ -266,8 +268,8 @@
     total = jnp.zeros((4, BLOCK), F32)
     for k in range(SLOTS):
         at = pl.ds(pl.multiple_of(slots[1, k] * BLOCK, BLOCK), BLOCK)
-        live = slots[2, k].astype(F32)
-        value = scr[slots[0, k], :, at] * (acts[:, k * BLOCK : (k + 1) * BLOCK].astype(F32) * live)
+        value = scr[slots[0, k], :, at] * acts[:, k * BLOCK : (k + 1) * BLOCK].astype(F32)
+        value = jnp.where(slots[2, k] > 0, value, 0.0)
         total += value
         scores[:, k * BLOCK : (k + 1) * BLOCK] = value.astype(BF16)
     extra = jnp.sum(scr[:, :, COLS:], axis=0)
@@ -296,11 +298,11 @@
         same = owner[:, :, None] == owner[:, None, :]
         before = jnp.tril(jnp.ones((SLOTS, SLOTS), bool), -1)
         rank = jnp.sum(same & before, axis=2, dtype=jnp.int32)
-        takes = (owner == latent)[:, :, None] & (rank[:, :, None] == jnp.arange(CAP))
-        local = jnp.sum(jnp.where(takes, (block_ids % SLOTS)[:, :, None], 0), axis=1)
-        token_block = tensor // 2
-        live = jnp.arange(SLOTS, dtype=jnp.int32) < counts[token_block]
-        slots = jnp.stack([owner[token_block], rank[token_block], live.astype(jnp.int32)])
+        live = jnp.arange(SLOTS, dtype=jnp.int32) < counts[:, None]
+        mine = live & (owner == latent)
+        takes = mine[:, :, None] & (rank[:, :, None] == jnp.arange(CAP))
+        local = jnp.sum(jnp.where(takes, (block_ids % SLOTS)[:, :, None] + 1, 0), axis=1) - 1
+        slots = jnp.stack([owner, rank, live.astype(jnp.int32)])[:, tensor // 2]
     with jax.named_scope("weight_rows"):
         rows = call(
             stack_kernel,
@@ -322,17 +324,7 @@
         x_all = column[:, :PIECE].reshape(CHUNK, TOK)
         g_all = column[:, PIECE:].reshape(CHUNK, TOK)
         fetch = jnp.where(latent % 2 == 0, x_all, g_all)
-        own = [shift(fetch, "tensor", N_T, e) for e in range(1, N_T)]
-        dec, own[0] = pl.pallas_call(
-            fetch_kernel,
-            name="fetch",
-            in_specs=[SMEM, HBM, ANY],
-            out_specs=(VMEM, ANY),
-            out_shape=(shape((2, COLS, CHUNK), BF16), shape((CHUNK, TOK), BF16)),
-            input_output_aliases={2: 1},
-            scratch_shapes=[pltpu.SemaphoreType.DMA((2, CAP))],
-            compiler_params=pltpu.CompilerParams(vmem_limit_bytes=8 * 2**20),
-        )(local.astype(jnp.int32), decoder, own[0])
+        own = [shift(fetch, "tensor", N_T, e) for e in (1, 3, 2)]
         other = [swap_core(a) for a in own]
 
     with jax.named_scope("mlp"):
@@ -356,7 +348,7 @@
                 pltpu.VMEM((CHUNK, TOK), F32),
                 pltpu.VMEM((SENT, TOK), F32),
             ],
-            limit=26,
+            limit=20,
         )(
             idx, x_all, g_all, *own, *other, norm_gain.reshape(D // BLOCK, BLOCK),
             rows, below, above, far_low, far_high,
@@ -398,6 +390,17 @@
         )(own2, *parts2, pair, cen)
         got = [shift(send, "latent", N_L, 4 * d) for d in (1, 2, 3)]
 
+        dec, total = pl.pallas_call(
+            fetch_kernel,
+            name="fetch",
+            in_specs=[SMEM, HBM, ANY],
+            out_specs=(VMEM, ANY),
+            out_shape=(shape((2, COLS, CHUNK), BF16), group),
+            input_output_aliases={2: 1},
+            scratch_shapes=[pltpu.SemaphoreType.DMA((2, CAP))],
+            compiler_params=pltpu.CompilerParams(vmem_limit_bytes=8 * 2**20),
+        )(local.astype(jnp.int32), decoder, total)
+
         def group_rows(array):
             pieces = array.reshape(N_Z // 2, 4, PIECE, -1)
             return lax.dynamic_index_in_dim(pieces, latent % 4, 1, False).reshape(GROUP, -1)

time: 144 us -> 137 us (0.951)
  starting transfers between devices: 38 us -> 44.9 us
  waiting for transfers between devices: 47.9 us -> 42.1 us
  local copies, waits for them, and re-layouts: 13 us -> 8.3 us
  Pallas kernels: 19.4 us -> 16.3 us
    ppermute x7, starting transfers between devices: 5.38 us -> 13.6 us  [swap_core(): return lax.ppermute(x, 'latent', [(i, i ^ 1) for i in range(N_L)])]
    ppermute x16, waiting for transfers between devices: 22.4 us -> 15.5 us  [shift(): return lax.ppermute(x, axis, [(i, (i + by) % size) for i in range(size)])]
    unnamed x24 -> x17, local copies, waits for them, and re-layouts: 8.21 us -> 3.12 us
    pallas_call x1, Pallas kernels: 5.52 us -> 2.08 us  [on_device(): pl.pallas_call(fetch_kernel, name='fetch', in_specs=[SMEM, HBM, ANY], out...]
    ppermute x16, starting transfers between devices: 26 us -> 23.5 us  [shift(): return lax.ppermute(x, axis, [(i, (i + by) % size) for i in range(size)])]
  transfers between devices with their start and end apart: 26 -> 26, of which waited for: 16 -> 12; matrix products, arithmetic and copies ran while one was open for 4% -> 4% of each run, Pallas kernels for 4% -> 2%
where the time goes in v3:
time: 137 us
  starting transfers between devices  44.9 us (33%)
  waiting for transfers between devices  42.1 us (31%)
  blocking collectives  23.4 us (17%)
  Pallas kernels  16.3 us (12%)
  local copies, waits for them, and re-layouts  8.3 us (6%)
    ppermute x16, starting transfers between devices, shift(): return lax.ppermute(x, axis, [(i, (i + by) % size) for i in range(size)])  23.5 us
    all_gather x1, blocking collectives, on_device(): column = lax.all_gather(jnp.concatenate([x_own, g_own]), 'latent', axis=0)  23.4 us
    all_to_all x1, waiting for transfers between devices, on_device(): lax.all_to_all(products.reshape(N_T * N_L, 4, WIDE), ('tensor', 'latent')...  18.6 us
    ppermute x16, waiting for transfers between devices, shift(): return lax.ppermute(x, axis, [(i, (i + by) % size) for i in range(size)])  15.5 us
    ppermute x7, starting transfers between devices, swap_core(): return lax.ppermute(x, 'latent', [(i, i ^ 1) for i in range(N_L)])  13.6 us
    all_to_all x1, starting transfers between devices, on_device(): lax.all_to_all(products.reshape(N_T * N_L, 4, WIDE), ('tensor', 'latent')...  7.64 us
    pallas_call x1, Pallas kernels, on_device(): call(mlp_kernel, 'mlp', [SMEM] + [VMEM] * 14, (shape((N_T, GROUP, TOK), F...  7.1 us
    ppermute x7, waiting for transfers between devices, swap_core(): return lax.ppermute(x, 'latent', [(i, i ^ 1) for i in range(N_L)])  4.38 us
  transfers between devices with their start and end apart: 26, of which 12 were waited for; matrix products, arithmetic and copies ran while one was open for 4% of the time, Pallas kernels for 2%

profile of v3, /device:TPU:1, one launch (start us, length us, event | category | flops | bytes accessed | tf_op | source)
XLA Modules:
  0.0 136.7 jit_solution(15619121014235142110)
XLA Ops:
  0.7 2.3 %stack.34.w0 = bf16[3,224,896]{2,1,0:T(8,128)(2,1)} custom-call(bf16[224,896]{1,0:T(8,128)(2,1)} %bitcast.34, bf16[224,896]{1,0:T(8,128)(2,1)} %bitcast.35, bf16[224,896]{1,0:T(8,128)(2,1)} %bitcast.36), custom_call_target="tpu_custom_call" | custom-call | tf_op jit(solution)/shard_map/weight_rows/stack/pallas_call | solution.py:307
  3.0 2.2 %collective-permute-start.6 = (bf16[3,224,896]{2,1,0:T(8,128)(2,1)}, bf16[3,224,896]{2,1,0:T(8,128)(2,1)S(1)}, u32[]{:S(2)}, u32[]{:S(2)}) collective-permute-start(bf16[3,224,896]{2,1,0:T(8,128)(2,1)} %stack.34.w0), channel_id=1, source_target_pairs={{0,64},{64,128},{128,192},{192,0},{1,65},{65,129},{129,193},{193,1... | collective-permute-start | bytes 3612680 | tf_op jit(solution)/shard_map/weight_rows/ppermute | solution.py:52
  5.2 1.5 %collective-permute-start.7 = (bf16[3,224,896]{2,1,0:T(8,128)(2,1)}, bf16[3,224,896]{2,1,0:T(8,128)(2,1)}, u32[]{:S(2)}, u32[]{:S(2)}) collective-permute-start(bf16[3,224,896]{2,1,0:T(8,128)(2,1)} %stack.34.w0), channel_id=1, source_target_pairs={{0,192},{64,0},{128,64},{192,128},{1,193},{65,1},{129,65},{193,129... | collective-permute-start | bytes 3612680 | tf_op jit(solution)/shard_map/weight_rows/ppermute | solution.py:52
  6.7 23.4 %all-gather = bf16[1792,256]{1,0:T(8,128)(2,1)S(1)} all-gather(bf16[112,256]{1,0:T(8,128)(2,1)S(1)} %pad_maximum_fusion), channel_id=2, replica_groups=mesh['dp'=4,'tensor'=4,'latent'=16] {'latent'}, dimensions={0}, use_global_device_ids=true | all-gather | bytes 974848 | tf_op jit(solution)/shard_map/token_features/all_gather | solution.py:323
  30.3 1.3 collective-permute-start
  31.6 1.5 %collective-permute-start.1 = (bf16[896,256]{1,0:T(8,128)(2,1)S(1)}, bf16[896,256]{1,0:T(8,128)(2,1)}, u32[]{:S(2)}, u32[]{:S(2)}) collective-permute-start(bf16[896,256]{1,0:T(8,128)(2,1)S(1)} %broadcast_select_fusion), channel_id=1, source_target_pairs={{0,48},{16,0},{32,16},{48,32},{1,49},{17,1},{33,17},{49,33},{2,50}... | collective-permute-start | bytes 1376264 | tf_op jit(solution)/shard_map/token_features/ppermute | solution.py:52
  33.1 1.5 %collective-permute-start.2 = (bf16[896,256]{1,0:T(8,128)(2,1)S(1)}, bf16[896,256]{1,0:T(8,128)(2,1)}, u32[]{:S(2)}, u32[]{:S(2)}) collective-permute-start(bf16[896,256]{1,0:T(8,128)(2,1)S(1)} %broadcast_select_fusion), channel_id=1, source_target_pairs={{0,32},{16,48},{32,0},{48,16},{1,33},{17,49},{33,1},{49,17},{2,34}... | collective-permute-start | bytes 1376264 | tf_op jit(solution)/shard_map/token_features/ppermute | solution.py:52
  34.6 0.9 slice.18
  35.6 1.9 %slice.19 = bf16[3,112,896]{2,1,0:T(8,128)(2,1)} slice(bf16[3,224,896]{2,1,0:T(8,128)(2,1)} %collective-permute-done.7.w2), slice={[0:3], [112:224], [0:896]} | slice | bytes 1204224 | tf_op jit(solution)/shard_map/weight_rows/slice | solution.py:319
  37.5 2.6 %collective-permute-start.9 = (bf16[3,112,896]{2,1,0:T(8,128)(2,1)}, bf16[3,112,896]{2,1,0:T(8,128)(2,1)}, u32[]{:S(2)}, u32[]{:S(2)}) collective-permute-start(bf16[3,112,896]{2,1,0:T(8,128)(2,1)} %slice.19), channel_id=1, source_target_pairs={{0,192},{64,0},{128,64},{192,128},{1,193},{65,1},{129,65},{193,129... | collective-permute-start | bytes 1806344 | tf_op jit(solution)/shard_map/weight_rows/ppermute | solution.py:52
  40.1 3.6 %collective-permute-done.a1 = bf16[896,256]{1,0:T(8,128)(2,1)} collective-permute-done((bf16[896,256]{1,0:T(8,128)(2,1)S(1)}, bf16[896,256]{1,0:T(8,128)(2,1)}, u32[]{:S(2)}, u32[]{:S(2)}) %collective-permute-start) | collective-permute-done | bytes 458784 | tf_op jit(solution)/shard_map/token_features/ppermute | solution.py:52
  43.7 1.0 collective-permute-start.3
  44.7 9.0 %collective-permute-start.4 = (bf16[896,256]{1,0:T(8,128)(2,1)}, bf16[896,256]{1,0:T(8,128)(2,1)}, u32[]{:S(2)}, u32[]{:S(2)}) collective-permute-start(bf16[896,256]{1,0:T(8,128)(2,1)} %collective-permute-done.1.a2), channel_id=1, source_target_pairs={{0,1},{1,0},{2,3},{3,2},{4,5},{5,4},{6,7},{7,6},{8,9},{9,8},{10,11... | collective-permute-start | bytes 1376264 | tf_op jit(solution)/shard_map/token_features/ppermute | solution.py:56
  53.7 0.8 collective-permute-done.2.a3
  54.5 1.0 collective-permute-start.5
  55.6 1.7 %collective-permute-done.5.b3 = bf16[896,256]{1,0:T(8,128)(2,1)} collective-permute-done((bf16[896,256]{1,0:T(8,128)(2,1)}, bf16[896,256]{1,0:T(8,128)(2,1)}, u32[]{:S(2)}, u32[]{:S(2)}) %collective-permute-start.5) | collective-permute-done | bytes 458784 | tf_op jit(solution)/shard_map/token_features/ppermute | solution.py:56
  57.3 7.1 %mlp.1 = (f32[4,224,256]{2,1,0:T(8,128)S(1)}, f32[4,224,256]{2,1,0:T(8,128)S(1)}, bf16[4,240,256]{2,1,0:T(8,128)(2,1)S(1)}, bf16[4,224,256]{2,1,0:T(8,128)(2,1)S...) custom-call(s32[4]{0:T(128)S(1)} %pad_add_fusion.idx, bf16[896,256]{1,0:T(8,128)(2,1)S(1)} %bitcast.27, ...), custom_call_target="tpu_custom_call" | custom-call | tf_op jit(solution)/shard_map/mlp/mlp/pallas_call | solution.py:332
  64.4 0.5 collective-permute-start.10
  64.9 0.3 collective-permute-start.11
  65.3 1.7 %collective-permute-done.11.got2 = bf16[4,224,256]{2,1,0:T(8,128)(2,1)S(1)} collective-permute-done((bf16[4,224,256]{2,1,0:T(8,128)(2,1)S(1)}, bf16[4,224,256]{2,1,0:T(8,128)(2,1)S(1)}, u32[]{:S(2)}, u32[]{:S(2)}) %collective-permute-start.11) | collective-permute-done | bytes 458784 | tf_op jit(solution)/shard_map/hidden_sums/ppermute | solution.py:56
  67.0 0.7 core_sum.1
  67.8 0.9 collective-permute-start.15
  68.7 2.7 %collective-permute-start.16 = (bf16[240,256]{1,0:T(8,128)(2,1)S(1)}, bf16[240,256]{1,0:T(8,128)(2,1)S(1)}, u32[]{:S(2)}, u32[]{:S(2)}) collective-permute-start(bf16[240,256]{1,0:T(8,128)(2,1)S(1)} %get-tuple-element.39), channel_id=1, source_target_pairs={{0,32},{16,48},{32,0},{48,16},{1,33},{17,49},{33,1},{49,17},{2,34}... | collective-permute-start | bytes 368648 | tf_op jit(solution)/shard_map/hidden_sums/ppermute | solution.py:52
  71.4 1.5 %collective-permute-start.12 = (bf16[224,256]{1,0:T(8,128)(2,1)S(1)}, bf16[224,256]{1,0:T(8,128)(2,1)S(1)}, u32[]{:S(2)}, u32[]{:S(2)}) collective-permute-start(bf16[224,256]{1,0:T(8,128)(2,1)S(1)} %get-tuple-element.34), channel_id=1, source_target_pairs={{0,16},{16,32},{32,48},{48,0},{1,17},{17,33},{33,49},{49,1},{2,18}... | collective-permute-start | bytes 344072 | tf_op jit(solution)/shard_map/hidden_sums/ppermute | solution.py:52
  72.8 0.3 collective-permute-start.13
  73.1 0.4 collective-permute-done.15.r1
  73.6 1.7 %collective-permute-start.14 = (bf16[224,256]{1,0:T(8,128)(2,1)S(1)}, bf16[224,256]{1,0:T(8,128)(2,1)S(1)}, u32[]{:S(2)}, u32[]{:S(2)}) collective-permute-start(bf16[224,256]{1,0:T(8,128)(2,1)S(1)} %get-tuple-element.36), channel_id=1, source_target_pairs={{0,48},{16,0},{32,16},{48,32},{1,49},{17,1},{33,17},{49,33},{2,50}... | collective-permute-start | bytes 344072 | tf_op jit(solution)/shard_map/hidden_sums/ppermute | solution.py:52
  75.3 1.8 %collective-permute-done.16.r2 = bf16[240,256]{1,0:T(8,128)(2,1)S(1)} collective-permute-done((bf16[240,256]{1,0:T(8,128)(2,1)S(1)}, bf16[240,256]{1,0:T(8,128)(2,1)S(1)}, u32[]{:S(2)}, u32[]{:S(2)}) %collective-permute-start.16) | collective-permute-done | bytes 122912 | tf_op jit(solution)/shard_map/hidden_sums/ppermute | solution.py:52
  77.3 0.2 convert_reduce_fusion
  77.5 0.2 select_reduce_fusion
  77.6 1.9 %collective-permute-done.12.r1 = bf16[224,256]{1,0:T(8,128)(2,1)S(1)} collective-permute-done((bf16[224,256]{1,0:T(8,128)(2,1)S(1)}, bf16[224,256]{1,0:T(8,128)(2,1)S(1)}, u32[]{:S(2)}, u32[]{:S(2)}) %collective-permute-start.12) | collective-permute-done | bytes 114720 | tf_op jit(solution)/shard_map/hidden_sums/ppermute | solution.py:52
  79.5 2.5 %collective-permute-done.13.r2 = bf16[224,256]{1,0:T(8,128)(2,1)S(1)} collective-permute-done((bf16[224,256]{1,0:T(8,128)(2,1)S(1)}, bf16[224,256]{1,0:T(8,128)(2,1)S(1)}, u32[]{:S(2)}, u32[]{:S(2)}) %collective-permute-start.13) | collective-permute-done | bytes 114720 | tf_op jit(solution)/shard_map/hidden_sums/ppermute | solution.py:52
  82.2 3.0 %collective-permute-start.20 = (bf16[240,256]{1,0:T(8,128)(2,1)S(1)}, bf16[240,256]{1,0:T(8,128)(2,1)S(1)}, u32[]{:S(2)}, u32[]{:S(2)}) collective-permute-start(bf16[240,256]{1,0:T(8,128)(2,1)S(1)} %get-tuple-element.46), channel_id=1, source_target_pairs={{0,8},{1,9},{2,10},{3,11},{4,12},{5,13},{6,14},{7,15},{8,0},{9,1},... | collective-permute-start | bytes 368648 | tf_op jit(solution)/shard_map/hidden_sums/ppermute | solution.py:52
  85.2 2.6 %collective-permute-start.21 = (bf16[240,256]{1,0:T(8,128)(2,1)S(1)}, bf16[240,256]{1,0:T(8,128)(2,1)S(1)}, u32[]{:S(2)}, u32[]{:S(2)}) collective-permute-start(bf16[240,256]{1,0:T(8,128)(2,1)S(1)} %get-tuple-element.46), channel_id=1, source_target_pairs={{0,12},{1,13},{2,14},{3,15},{4,0},{5,1},{6,2},{7,3},{8,4},{9,5},{1... | collective-permute-start | bytes 368648 | tf_op jit(solution)/shard_map/hidden_sums/ppermute | solution.py:52
  88.0 0.8 dynamic_slice.26
  89.2 3.1 %copy-done = bf16[4096,896]{1,0:T(8,128)(2,1)S(1)} copy-done((bf16[4096,896]{1,0:T(8,128)(2,1)S(1)}, bf16[4096,896]{1,0:T(8,128)(2,1)}, u32[]{:S(2)}) %copy-start) | copy-done | bytes 7340056
  92.3 2.1 %fetch.1 = (bf16[2,1024,896]{2,1,0:T(8,128)(2,1)S(1)}, f32[224,256]{1,0:T(8,128)S(1)}) custom-call(s32[2,8]{1,0:T(2,128)S(1)} %broadcast_add_fusion.ids, bf16[4096,896]{1,0:T(8,128)(2,1)S(1)} %copy-done, f32[224,256]{1,0:T(8,128)S(1)} %get-tuple-element.44._), custom_call_target="tpu_custom_call", output_to_operand_aliasing={{1}: (2, {})} | custom-call | tf_op jit(solution)/shard_map/hidden_sums/fetch/pallas_call | solution.py:393
  94.4 4.4 %collective-permute-done.21.r3 = bf16[240,256]{1,0:T(8,128)(2,1)S(1)} collective-permute-done((bf16[240,256]{1,0:T(8,128)(2,1)S(1)}, bf16[240,256]{1,0:T(8,128)(2,1)S(1)}, u32[]{:S(2)}, u32[]{:S(2)}) %collective-permute-start.21) | collective-permute-done | bytes 122912 | tf_op jit(solution)/shard_map/hidden_sums/ppermute | solution.py:52
  98.8 0.7 grad.1
  99.6 0.6 collective-permute-start.23
  100.2 3.6 %collective-permute-done.22.g1 = bf16[224,256]{1,0:T(8,128)(2,1)S(1)} collective-permute-done((bf16[224,256]{1,0:T(8,128)(2,1)S(1)}, bf16[224,256]{1,0:T(8,128)(2,1)S(1)}, u32[]{:S(2)}, u32[]{:S(2)}) %collective-permute-start.22) | collective-permute-done | bytes 114720 | tf_op jit(solution)/shard_map/decode/ppermute | solution.py:421
  103.8 1.3 collective-permute-start.24
  105.2 1.0 collective-permute-done.24.g3
  106.1 1.9 %decode.1 = bf16[256,1152]{1,0:T(8,128)(2,1)S(1)} custom-call(s32[4]{0:T(128)S(1)} %pad_add_fusion.idx, bf16[224,256]{1,0:T(8,128)(2,1)S(1)} %get-tuple-element.49.g0, bf16[224,256]{1,0:T(8,128)(2,1)S(1)} %collective-permute-done.22.g1, bf16[224,256]{1,0:T(8,128)(2,1)S(1)} %collective-permute-done.23.g2, bf16[224,256]{1,0:T(8,128)(2,1)S(1)} %collective-permute-done.24.g3, ...), custom_call_target="tpu_custom_call" | custom-call | tf_op jit(solution)/shard_map/decode/decode/pallas_call | solution.py:422
  108.1 1.0 reshape.108
  109.0 7.6 %all-to-all-start = ((bf16[64,4,1152]{2,1,0:T(4,128)(2,1)}), bf16[64,4,1152]{2,1,0:T(4,128)(2,1)S(1)}, u32[]{:S(2)}, u32[]{:S(2)}) async-start(bf16[64,4,1152]{2,1,0:T(4,128)(2,1)} %reshape.108), calls=%async_computation | async-start | bytes 1179648 | tf_op jit(solution)/shard_map/scores/all_to_all | solution.py:432
  116.8 18.6 %all-to-all-done.got = bf16[64,4,1152]{2,1,0:T(4,128)(2,1)S(1)} async-done(((bf16[64,4,1152]{2,1,0:T(4,128)(2,1)}), bf16[64,4,1152]{2,1,0:T(4,128)(2,1)S(1)}, u32[]{:S(2)}, u32[]{:S(2)}) %all-to-all-start) | async-done | bytes 589856 | tf_op jit(solution)/shard_map/scores/all_to_all | solution.py:432
  135.4 1.3 score.1
  (55 shorter events, 1.6 us)
Async XLA Ops:
  0.6 6.1 %copy-start.4 = (bf16[256,56]{0,1:T(8,128)(2,1)S(1)}, bf16[256,56]{0,1:T(8,128)(2,1)}, u32[]{:S(2)}) copy-start(bf16[256,56]{0,1:T(8,128)(2,1)} %param.12) | copy-start | bytes 86020
  0.6 6.1 %copy-start.5 = (bf16[256,56]{0,1:T(8,128)(2,1)S(1)}, bf16[256,56]{0,1:T(8,128)(2,1)}, u32[]{:S(2)}) copy-start(bf16[256,56]{0,1:T(8,128)(2,1)} %param.11) | copy-start | bytes 86020
  3.0 31.7 %collective-permute-start.6 = (bf16[3,224,896]{2,1,0:T(8,128)(2,1)}, bf16[3,224,896]{2,1,0:T(8,128)(2,1)S(1)}, u32[]{:S(2)}, u32[]{:S(2)}) collective-permute-start(bf16[3,224,896]{2,1,0:T(8,128)(2,1)} %stack.34.w0), channel_id=1, source_target_pairs={{0,64},{64,128},{128,192},{192,0},{1,65},{65,129},{129,193},{193,1... | collective-permute-start | bytes 3612680 | tf_op jit(solution)/shard_map/weight_rows/ppermute | solution.py:52
  5.2 30.4 %collective-permute-start.7 = (bf16[3,224,896]{2,1,0:T(8,128)(2,1)}, bf16[3,224,896]{2,1,0:T(8,128)(2,1)}, u32[]{:S(2)}, u32[]{:S(2)}) collective-permute-start(bf16[3,224,896]{2,1,0:T(8,128)(2,1)} %stack.34.w0), channel_id=1, source_target_pairs={{0,192},{64,0},{128,64},{192,128},{1,193},{65,1},{129,65},{193,129... | collective-permute-start | bytes 3612680 | tf_op jit(solution)/shard_map/weight_rows/ppermute | solution.py:52
  30.3 27.0 %copy-start.1 = (bf16[3,224,896]{2,1,0:T(8,128)(2,1)S(1)}, bf16[3,224,896]{2,1,0:T(8,128)(2,1)}, u32[]{:S(2)}) copy-start(bf16[3,224,896]{2,1,0:T(8,128)(2,1)} %stack.34.w0) | copy-start | bytes 3612676
  30.3 27.0 %copy-start.3 = (f32[3584]{0:T(1024)S(1)}, f32[3584]{0:T(1024)}, u32[]{:S(2)}) copy-start(f32[3584]{0:T(1024)} %param.13) | copy-start | bytes 43012
  30.3 13.4 %collective-permute-start = (bf16[896,256]{1,0:T(8,128)(2,1)S(1)}, bf16[896,256]{1,0:T(8,128)(2,1)}, u32[]{:S(2)}, u32[]{:S(2)}) collective-permute-start(bf16[896,256]{1,0:T(8,128)(2,1)S(1)} %broadcast_select_fusion), channel_id=1, source_target_pairs={{0,16},{16,32},{32,48},{48,0},{1,17},{17,33},{33,49},{49,1},{2,18}... | collective-permute-start | bytes 1376264 | tf_op jit(solution)/shard_map/token_features/ppermute | solution.py:52
  31.6 13.0 %collective-permute-start.1 = (bf16[896,256]{1,0:T(8,128)(2,1)S(1)}, bf16[896,256]{1,0:T(8,128)(2,1)}, u32[]{:S(2)}, u32[]{:S(2)}) collective-permute-start(bf16[896,256]{1,0:T(8,128)(2,1)S(1)} %broadcast_select_fusion), channel_id=1, source_target_pairs={{0,48},{16,0},{32,16},{48,32},{1,49},{17,1},{33,17},{49,33},{2,50}... | collective-permute-start | bytes 1376264 | tf_op jit(solution)/shard_map/token_features/ppermute | solution.py:52
  33.1 21.4 %collective-permute-start.2 = (bf16[896,256]{1,0:T(8,128)(2,1)S(1)}, bf16[896,256]{1,0:T(8,128)(2,1)}, u32[]{:S(2)}, u32[]{:S(2)}) collective-permute-start(bf16[896,256]{1,0:T(8,128)(2,1)S(1)} %broadcast_select_fusion), channel_id=1, source_target_pairs={{0,32},{16,48},{32,0},{48,16},{1,33},{17,49},{33,1},{49,17},{2,34}... | collective-permute-start | bytes 1376264 | tf_op jit(solution)/shard_map/token_features/ppermute | solution.py:52
  35.5 21.8 %collective-permute-start.8 = (bf16[3,112,896]{2,1,0:T(8,128)(2,1)}, bf16[3,112,896]{2,1,0:T(8,128)(2,1)}, u32[]{:S(2)}, u32[]{:S(2)}) collective-permute-start(bf16[3,112,896]{2,1,0:T(8,128)(2,1)} %slice.18), channel_id=1, source_target_pairs={{0,64},{64,128},{128,192},{192,0},{1,65},{65,129},{129,193},{193,1... | collective-permute-start | bytes 1806344 | tf_op jit(solution)/shard_map/weight_rows/ppermute | solution.py:52
  37.5 19.7 %collective-permute-start.9 = (bf16[3,112,896]{2,1,0:T(8,128)(2,1)}, bf16[3,112,896]{2,1,0:T(8,128)(2,1)}, u32[]{:S(2)}, u32[]{:S(2)}) collective-permute-start(bf16[3,112,896]{2,1,0:T(8,128)(2,1)} %slice.19), channel_id=1, source_target_pairs={{0,192},{64,0},{128,64},{192,128},{1,193},{65,1},{129,65},{193,129... | collective-permute-start | bytes 1806344 | tf_op jit(solution)/shard_map/weight_rows/ppermute | solution.py:52
  43.7 11.9 %collective-permute-start.3 = (bf16[896,256]{1,0:T(8,128)(2,1)}, bf16[896,256]{1,0:T(8,128)(2,1)}, u32[]{:S(2)}, u32[]{:S(2)}) collective-permute-start(bf16[896,256]{1,0:T(8,128)(2,1)} %collective-permute-done.a1), channel_id=1, source_target_pairs={{0,1},{1,0},{2,3},{3,2},{4,5},{5,4},{6,7},{7,6},{8,9},{9,8},{10,11... | collective-permute-start | bytes 1376264 | tf_op jit(solution)/shard_map/token_features/ppermute | solution.py:56
  44.7 10.9 %collective-permute-start.4 = (bf16[896,256]{1,0:T(8,128)(2,1)}, bf16[896,256]{1,0:T(8,128)(2,1)}, u32[]{:S(2)}, u32[]{:S(2)}) collective-permute-start(bf16[896,256]{1,0:T(8,128)(2,1)} %collective-permute-done.1.a2), channel_id=1, source_target_pairs={{0,1},{1,0},{2,3},{3,2},{4,5},{5,4},{6,7},{7,6},{8,9},{9,8},{10,11... | collective-permute-start | bytes 1376264 | tf_op jit(solution)/shard_map/token_features/ppermute | solution.py:56
  54.5 2.7 %collective-permute-start.5 = (bf16[896,256]{1,0:T(8,128)(2,1)}, bf16[896,256]{1,0:T(8,128)(2,1)}, u32[]{:S(2)}, u32[]{:S(2)}) collective-permute-start(bf16[896,256]{1,0:T(8,128)(2,1)} %collective-permute-done.2.a3), channel_id=1, source_target_pairs={{0,1},{1,0},{2,3},{3,2},{4,5},{5,4},{6,7},{7,6},{8,9},{9,8},{10,11... | collective-permute-start | bytes 1376264 | tf_op jit(solution)/shard_map/token_features/ppermute | solution.py:56
  57.3 7.9 %copy-start.6 = (s32[2,32]{1,0:T(2,128)S(1)}, s32[2,32]{1,0:T(2,128)}, u32[]{:S(2)}) copy-start(s32[2,32]{1,0:T(2,128)} %param.19) | copy-start | bytes 772
  57.3 7.9 %copy-start.7 = (s32[2]{0:T(128)S(1)}, s32[2]{0:T(128)}, u32[]{:S(2)}) copy-start(s32[2]{0:T(128)} %param.20) | copy-start | bytes 28
  64.4 2.6 %collective-permute-start.10 = (bf16[4,240,256]{2,1,0:T(8,128)(2,1)S(1)}, bf16[4,240,256]{2,1,0:T(8,128)(2,1)S(1)}, u32[]{:S(2)}, u32[]{:S(2)}) collective-permute-start(bf16[4,240,256]{2,1,0:T(8,128)(2,1)S(1)} %get-tuple-element.30), channel_id=1, source_target_pairs={{0,1},{1,0},{2,3},{3,2},{4,5},{5,4},{6,7},{7,6},{8,9},{9,8},{10,11... | collective-permute-start | bytes 1474568 | tf_op jit(solution)/shard_map/hidden_sums/ppermute | solution.py:56
  64.9 2.1 %collective-permute-start.11 = (bf16[4,224,256]{2,1,0:T(8,128)(2,1)S(1)}, bf16[4,224,256]{2,1,0:T(8,128)(2,1)S(1)}, u32[]{:S(2)}, u32[]{:S(2)}) collective-permute-start(bf16[4,224,256]{2,1,0:T(8,128)(2,1)S(1)} %get-tuple-element.31), channel_id=1, source_target_pairs={{0,1},{1,0},{2,3},{3,2},{4,5},{5,4},{6,7},{7,6},{8,9},{9,8},{10,11... | collective-permute-start | bytes 1376264 | tf_op jit(solution)/shard_map/hidden_sums/ppermute | solution.py:56
  67.8 5.8 %collective-permute-start.15 = (bf16[240,256]{1,0:T(8,128)(2,1)S(1)}, bf16[240,256]{1,0:T(8,128)(2,1)S(1)}, u32[]{:S(2)}, u32[]{:S(2)}) collective-permute-start(bf16[240,256]{1,0:T(8,128)(2,1)S(1)} %get-tuple-element.38), channel_id=1, source_target_pairs={{0,16},{16,32},{32,48},{48,0},{1,17},{17,33},{33,49},{49,1},{2,18}... | collective-permute-start | bytes 368648 | tf_op jit(solution)/shard_map/hidden_sums/ppermute | solution.py:52
  68.7 8.4 %collective-permute-start.16 = (bf16[240,256]{1,0:T(8,128)(2,1)S(1)}, bf16[240,256]{1,0:T(8,128)(2,1)S(1)}, u32[]{:S(2)}, u32[]{:S(2)}) collective-permute-start(bf16[240,256]{1,0:T(8,128)(2,1)S(1)} %get-tuple-element.39), channel_id=1, source_target_pairs={{0,32},{16,48},{32,0},{48,16},{1,33},{17,49},{33,1},{49,17},{2,34}... | collective-permute-start | bytes 368648 | tf_op jit(solution)/shard_map/hidden_sums/ppermute | solution.py:52
  71.4 5.7 %collective-permute-start.17 = (bf16[240,256]{1,0:T(8,128)(2,1)S(1)}, bf16[240,256]{1,0:T(8,128)(2,1)S(1)}, u32[]{:S(2)}, u32[]{:S(2)}) collective-permute-start(bf16[240,256]{1,0:T(8,128)(2,1)S(1)} %get-tuple-element.40), channel_id=1, source_target_pairs={{0,48},{16,0},{32,16},{48,32},{1,49},{17,1},{33,17},{49,33},{2,50}... | collective-permute-start | bytes 368648 | tf_op jit(solution)/shard_map/hidden_sums/ppermute | solution.py:52
  71.4 8.1 %collective-permute-start.12 = (bf16[224,256]{1,0:T(8,128)(2,1)S(1)}, bf16[224,256]{1,0:T(8,128)(2,1)S(1)}, u32[]{:S(2)}, u32[]{:S(2)}) collective-permute-start(bf16[224,256]{1,0:T(8,128)(2,1)S(1)} %get-tuple-element.34), channel_id=1, source_target_pairs={{0,16},{16,32},{32,48},{48,0},{1,17},{17,33},{33,49},{49,1},{2,18}... | collective-permute-start | bytes 344072 | tf_op jit(solution)/shard_map/hidden_sums/ppermute | solution.py:52
  72.8 9.2 %collective-permute-start.13 = (bf16[224,256]{1,0:T(8,128)(2,1)S(1)}, bf16[224,256]{1,0:T(8,128)(2,1)S(1)}, u32[]{:S(2)}, u32[]{:S(2)}) collective-permute-start(bf16[224,256]{1,0:T(8,128)(2,1)S(1)} %get-tuple-element.35), channel_id=1, source_target_pairs={{0,32},{16,48},{32,0},{48,16},{1,33},{17,49},{33,1},{49,17},{2,34}... | collective-permute-start | bytes 344072 | tf_op jit(solution)/shard_map/hidden_sums/ppermute | solution.py:52
  73.6 8.4 %collective-permute-start.14 = (bf16[224,256]{1,0:T(8,128)(2,1)S(1)}, bf16[224,256]{1,0:T(8,128)(2,1)S(1)}, u32[]{:S(2)}, u32[]{:S(2)}) collective-permute-start(bf16[224,256]{1,0:T(8,128)(2,1)S(1)} %get-tuple-element.36), channel_id=1, source_target_pairs={{0,48},{16,0},{32,16},{48,32},{1,49},{17,1},{33,17},{49,33},{2,50}... | collective-permute-start | bytes 344072 | tf_op jit(solution)/shard_map/hidden_sums/ppermute | solution.py:52
  77.2 4.8 %collective-permute-start.18 = (bf16[240,256]{1,0:T(8,128)(2,1)S(1)}, bf16[240,256]{1,0:T(8,128)(2,1)S(1)}, u32[]{:S(2)}, u32[]{:S(2)}) collective-permute-start(bf16[240,256]{1,0:T(8,128)(2,1)S(1)} %get-tuple-element.42), channel_id=1, source_target_pairs={{0,2},{1,3},{2,0},{3,1},{4,6},{5,7},{6,4},{7,5},{8,10},{9,11},{10,... | collective-permute-start | bytes 368648 | tf_op jit(solution)/shard_map/hidden_sums/ppermute | solution.py:382
  82.1 12.2 %collective-permute-start.19 = (bf16[240,256]{1,0:T(8,128)(2,1)S(1)}, bf16[240,256]{1,0:T(8,128)(2,1)S(1)}, u32[]{:S(2)}, u32[]{:S(2)}) collective-permute-start(bf16[240,256]{1,0:T(8,128)(2,1)S(1)} %get-tuple-element.46), channel_id=1, source_target_pairs={{0,4},{1,5},{2,6},{3,7},{4,8},{5,9},{6,10},{7,11},{8,12},{9,13},{1... | collective-permute-start | bytes 368648 | tf_op jit(solution)/shard_map/hidden_sums/ppermute | solution.py:52
  82.2 12.2 %collective-permute-start.20 = (bf16[240,256]{1,0:T(8,128)(2,1)S(1)}, bf16[240,256]{1,0:T(8,128)(2,1)S(1)}, u32[]{:S(2)}, u32[]{:S(2)}) collective-permute-start(bf16[240,256]{1,0:T(8,128)(2,1)S(1)} %get-tuple-element.46), channel_id=1, source_target_pairs={{0,8},{1,9},{2,10},{3,11},{4,12},{5,13},{6,14},{7,15},{8,0},{9,1},... | collective-permute-start | bytes 368648 | tf_op jit(solution)/shard_map/hidden_sums/ppermute | solution.py:52
  85.2 13.6 %collective-permute-start.21 = (bf16[240,256]{1,0:T(8,128)(2,1)S(1)}, bf16[240,256]{1,0:T(8,128)(2,1)S(1)}, u32[]{:S(2)}, u32[]{:S(2)}) collective-permute-start(bf16[240,256]{1,0:T(8,128)(2,1)S(1)} %get-tuple-element.46), channel_id=1, source_target_pairs={{0,12},{1,13},{2,14},{3,15},{4,0},{5,1},{6,2},{7,3},{8,4},{9,5},{1... | collective-permute-start | bytes 368648 | tf_op jit(solution)/shard_map/hidden_sums/ppermute | solution.py:52
  89.2 3.1 %copy-start = (bf16[4096,896]{1,0:T(8,128)(2,1)S(1)}, bf16[4096,896]{1,0:T(8,128)(2,1)}, u32[]{:S(2)}) copy-start(bf16[4096,896]{1,0:T(8,128)(2,1)} %decoder.1) | copy-start | bytes 22020100
  99.5 4.3 %collective-permute-start.22 = (bf16[224,256]{1,0:T(8,128)(2,1)S(1)}, bf16[224,256]{1,0:T(8,128)(2,1)S(1)}, u32[]{:S(2)}, u32[]{:S(2)}) collective-permute-start(bf16[224,256]{1,0:T(8,128)(2,1)S(1)} %get-tuple-element.49.g0), channel_id=1, source_target_pairs={{0,2},{1,3},{2,0},{3,1},{4,6},{5,7},{6,4},{7,5},{8,10},{9,11},{10,... | collective-permute-start | bytes 344072 | tf_op jit(solution)/shard_map/decode/ppermute | solution.py:421
  99.6 5.6 %collective-permute-start.23 = (bf16[224,256]{1,0:T(8,128)(2,1)S(1)}, bf16[224,256]{1,0:T(8,128)(2,1)S(1)}, u32[]{:S(2)}, u32[]{:S(2)}) collective-permute-start(bf16[224,256]{1,0:T(8,128)(2,1)S(1)} %get-tuple-element.49.g0), channel_id=1, source_target_pairs={{0,1},{1,0},{2,3},{3,2},{4,5},{5,4},{6,7},{7,6},{8,9},{9,8},{10,11... | collective-permute-start | bytes 344072 | tf_op jit(solution)/shard_map/decode/ppermute | solution.py:56
  103.8 2.3 %collective-permute-start.24 = (bf16[224,256]{1,0:T(8,128)(2,1)S(1)}, bf16[224,256]{1,0:T(8,128)(2,1)S(1)}, u32[]{:S(2)}, u32[]{:S(2)}) collective-permute-start(bf16[224,256]{1,0:T(8,128)(2,1)S(1)} %collective-permute-done.22.g1), channel_id=1, source_target_pairs={{0,1},{1,0},{2,3},{3,2},{4,5},{5,4},{6,7},{7,6},{8,9},{9,8},{10,11... | collective-permute-start | bytes 344072 | tf_op jit(solution)/shard_map/decode/ppermute | solution.py:56
  108.1 27.3 %copy-start.2 = (bf16[4,4096]{1,0:T(4,128)(2,1)S(1)}, bf16[4,4096]{1,0:T(4,128)(2,1)}, u32[]{:S(2)}) copy-start(bf16[4,4096]{1,0:T(4,128)(2,1)} %acts.1) | copy-start | bytes 98308
  109.0 26.4 %all-to-all-start = ((bf16[64,4,1152]{2,1,0:T(4,128)(2,1)}), bf16[64,4,1152]{2,1,0:T(4,128)(2,1)S(1)}, u32[]{:S(2)}, u32[]{:S(2)}) async-start(bf16[64,4,1152]{2,1,0:T(4,128)(2,1)} %reshape.108), calls=%async_computation | async-start | bytes 1179648 | tf_op jit(solution)/shard_map/scores/all_to_all | solution.py:432

commit v4 on v3

--- a/solution.py
+++ b/solution.py
@@ -238,7 +238,7 @@
         copy.wait()
 
 
-def decode_kernel(idx, g0, g1, g2, g3, err, dec, out, grad, scr):
+def decode_kernel(idx, g0, g1, g2, g3, err, dec, own, s1, s2, s3, grad, scr, wide):
     place = 2 * lax.rem(idx[2], 2) + idx[3]
     flips = (place, 2 * (1 - lax.rem(idx[2], 2)) + idx[3], 2 * lax.rem(idx[2], 2) + 1 - idx[3])
     last = 2 * (1 - lax.rem(idx[2], 2)) + 1 - idx[3]
@@ -251,20 +251,32 @@
     tall = jnp.broadcast_to(err[...], (BLOCK, TOK)).T
     high, low = split(tall)
     lane = lax.broadcasted_iota(jnp.int32, (TOK, BLOCK), 1)
-    out[:, COLS:] = jnp.where(lane == 0, high, jnp.where(lane == 1, low, 0.0)).astype(BF16)
+    wide[:, COLS:] = jnp.where(lane == 0, high, jnp.where(lane == 1, low, 0.0))
     for b in range(2):
         tokens = grad[:, b * BLOCK : (b + 1) * BLOCK]
-        out[b * BLOCK : (b + 1) * BLOCK, :COLS] = lax.dot_general(
+        wide[b * BLOCK : (b + 1) * BLOCK, :COLS] = lax.dot_general(
             tokens, dec[b], (((0,), (1,)), ((), ())), preferred_element_type=F32
-        ).astype(BF16)
+        )
+    tensor = idx[1]
+    own[...] = wide[pl.ds(pl.multiple_of(tensor * OWN_TOK, OWN_TOK), OWN_TOK), :]
+    for e, out in ((1, s1), (2, s2), (3, s3)):
+        to = lax.rem(tensor + e, N_T)
+        rows = pl.ds(pl.multiple_of(to * OWN_TOK, OWN_TOK), OWN_TOK)
+        out[...] = wide[rows, :].astype(BF16)
+
+
+def product_sum_kernel(own, r1, r2, r3, out):
+    total = own[...]
+    for r in (r1, r2, r3):
+        total = total + r[...].astype(F32)
+    out[:, :COLS] = total[:, :COLS].astype(BF16)
+    high, low = split(total[:, COLS : COLS + 1] + total[:, COLS + 1 : COLS + 2])
+    lane = lax.broadcasted_iota(jnp.int32, (OWN_TOK, BLOCK), 1)
+    out[:, COLS:] = jnp.where(lane == 0, high, jnp.where(lane == 1, low, 0.0)).astype(BF16)
 
 
 def score_kernel(slots, got, acts, scores, err, scr):
-    for l in range(N_L):
-        total = got[l].astype(F32)
-        for t in range(1, N_T):
-            total = total + got[t * N_L + l].astype(F32)
-        scr[l] = total
+    scr[...] = got[...].astype(F32)
     total = jnp.zeros((4, BLOCK), F32)
     for k in range(SLOTS):
         at = pl.ds(pl.multiple_of(slots[1, k] * BLOCK, BLOCK), BLOCK)
@@ -419,19 +431,26 @@
 
     with jax.named_scope("decode"):
         across = lax.ppermute(cast, "latent", [(i, i ^ 2) for i in range(N_L)])
-        products = call(
+        kept, *sends = call(
             decode_kernel,
             "decode",
             [SMEM] + [VMEM] * 6,
-            shape((TOK, WIDE), BF16),
-            [pltpu.VMEM((CHUNK, TOK), BF16), pltpu.VMEM((CHUNK, TOK), F32)],
+            (shape((OWN_TOK, WIDE), F32),) + (shape((OWN_TOK, WIDE), BF16),) * 3,
+            [
+                pltpu.VMEM((CHUNK, TOK), BF16),
+                pltpu.VMEM((CHUNK, TOK), F32),
+                pltpu.VMEM((TOK, WIDE), F32),
+            ],
             limit=14,
         )(idx, cast, across, swap_core(cast), swap_core(across), err, dec)
 
+        moved = [shift(s, "tensor", N_T, e) for e, s in zip(tensor_shifts, sends)]
+        products = call(
+            product_sum_kernel, "product_sum", [VMEM] * 4, shape((OWN_TOK, WIDE), BF16), limit=8
+        )(kept, *moved)
+
     with jax.named_scope("scores"):
-        got = lax.all_to_all(
-            products.reshape(N_T * N_L, 4, WIDE), ("tensor", "latent"), 0, 0, tiled=True
-        )
+        got = lax.all_to_all(products.reshape(N_L, 4, WIDE), "latent", 0, 0, tiled=True)
         scores, err = call(
             score_kernel,
             "score",

time: 137 us -> 136 us (level)
  waiting for transfers between devices: 42.1 us -> 39.8 us
  starting transfers between devices: 44.9 us -> 46.7 us
    all_to_all x1, waiting for transfers between devices: 18.6 us -> 9.23 us  [on_device(): lax.all_to_all(products.reshape(N_L, 4, WIDE), 'latent', 0, 0, tiled=True)]
    ppermute x16 -> x19, waiting for transfers between devices: 15.5 us -> 22.5 us  [shift(): return lax.ppermute(x, axis, [(i, (i + by) % size) for i in range(size)])]
    ppermute x16 -> x19, starting transfers between devices: 23.5 us -> 27.8 us  [shift(): return lax.ppermute(x, axis, [(i, (i + by) % size) for i in range(size)])]
    all_to_all x1, starting transfers between devices: 7.64 us -> 5.15 us  [on_device(): lax.all_to_all(products.reshape(N_L, 4, WIDE), 'latent', 0, 0, tiled=True)]
  transfers between devices with their start and end apart: 26 -> 29, of which waited for: 12 -> 14; matrix products, arithmetic and copies ran while one was open for 4% -> 4% of each run, Pallas kernels for 2% -> 1%
where the time goes in v4:
time: 136 us
  starting transfers between devices  46.7 us (34%)
  waiting for transfers between devices  39.8 us (29%)
  blocking collectives  23.4 us (17%)
  Pallas kernels  16.4 us (12%)
  local copies, waits for them, and re-layouts  8.03 us (6%)
    ppermute x19, starting transfers between devices, shift(): return lax.ppermute(x, axis, [(i, (i + by) % size) for i in range(size)])  27.8 us
    all_gather x1, blocking collectives, on_device(): column = lax.all_gather(jnp.concatenate([x_own, g_own]), 'latent', axis=0)  23.4 us
    ppermute x19, waiting for transfers between devices, shift(): return lax.ppermute(x, axis, [(i, (i + by) % size) for i in range(size)])  22.5 us
    ppermute x7, starting transfers between devices, swap_core(): return lax.ppermute(x, 'latent', [(i, i ^ 1) for i in range(N_L)])  13.6 us
    all_to_all x1, waiting for transfers between devices, on_device(): lax.all_to_all(products.reshape(N_L, 4, WIDE), 'latent', 0, 0, tiled=True)  9.23 us
    pallas_call x1, Pallas kernels, on_device(): call(mlp_kernel, 'mlp', [SMEM] + [VMEM] * 14, (shape((N_T, GROUP, TOK), F...  7.1 us
    all_to_all x1, starting transfers between devices, on_device(): lax.all_to_all(products.reshape(N_L, 4, WIDE), 'latent', 0, 0, tiled=True)  5.15 us
    ppermute x7, waiting for transfers between devices, swap_core(): return lax.ppermute(x, 'latent', [(i, i ^ 1) for i in range(N_L)])  4.38 us
  transfers between devices with their start and end apart: 29, of which 14 were waited for; matrix products, arithmetic and copies ran while one was open for 4% of the time, Pallas kernels for 1%

profile of v4, /device:TPU:1, one launch (start us, length us, event | category | flops | bytes accessed | tf_op | source)
XLA Modules:
  0.0 136.0 jit_solution(261321823297478777)
XLA Ops:
  0.7 2.3 %stack.34.w0 = bf16[3,224,896]{2,1,0:T(8,128)(2,1)} custom-call(bf16[224,896]{1,0:T(8,128)(2,1)} %bitcast.34, bf16[224,896]{1,0:T(8,128)(2,1)} %bitcast.35, bf16[224,896]{1,0:T(8,128)(2,1)} %bitcast.36), custom_call_target="tpu_custom_call" | custom-call | tf_op jit(solution)/shard_map/weight_rows/stack/pallas_call | solution.py:319
  3.0 2.2 %collective-permute-start.6 = (bf16[3,224,896]{2,1,0:T(8,128)(2,1)}, bf16[3,224,896]{2,1,0:T(8,128)(2,1)S(1)}, u32[]{:S(2)}, u32[]{:S(2)}) collective-permute-start(bf16[3,224,896]{2,1,0:T(8,128)(2,1)} %stack.34.w0), channel_id=1, source_target_pairs={{0,64},{64,128},{128,192},{192,0},{1,65},{65,129},{129,193},{193,1... | collective-permute-start | bytes 3612680 | tf_op jit(solution)/shard_map/weight_rows/ppermute | solution.py:52
  5.2 1.5 %collective-permute-start.7 = (bf16[3,224,896]{2,1,0:T(8,128)(2,1)}, bf16[3,224,896]{2,1,0:T(8,128)(2,1)}, u32[]{:S(2)}, u32[]{:S(2)}) collective-permute-start(bf16[3,224,896]{2,1,0:T(8,128)(2,1)} %stack.34.w0), channel_id=1, source_target_pairs={{0,192},{64,0},{128,64},{192,128},{1,193},{65,1},{129,65},{193,129... | collective-permute-start | bytes 3612680 | tf_op jit(solution)/shard_map/weight_rows/ppermute | solution.py:52
  6.7 23.4 %all-gather = bf16[1792,256]{1,0:T(8,128)(2,1)S(1)} all-gather(bf16[112,256]{1,0:T(8,128)(2,1)S(1)} %pad_maximum_fusion), channel_id=2, replica_groups=mesh['dp'=4,'tensor'=4,'latent'=16] {'latent'}, dimensions={0}, use_global_device_ids=true | all-gather | bytes 974848 | tf_op jit(solution)/shard_map/token_features/all_gather | solution.py:335
  30.4 1.3 collective-permute-start
  31.6 1.5 %collective-permute-start.1 = (bf16[896,256]{1,0:T(8,128)(2,1)S(1)}, bf16[896,256]{1,0:T(8,128)(2,1)}, u32[]{:S(2)}, u32[]{:S(2)}) collective-permute-start(bf16[896,256]{1,0:T(8,128)(2,1)S(1)} %broadcast_select_fusion), channel_id=1, source_target_pairs={{0,48},{16,0},{32,16},{48,32},{1,49},{17,1},{33,17},{49,33},{2,50}... | collective-permute-start | bytes 1376264 | tf_op jit(solution)/shard_map/token_features/ppermute | solution.py:52
  33.1 1.5 %collective-permute-start.2 = (bf16[896,256]{1,0:T(8,128)(2,1)S(1)}, bf16[896,256]{1,0:T(8,128)(2,1)}, u32[]{:S(2)}, u32[]{:S(2)}) collective-permute-start(bf16[896,256]{1,0:T(8,128)(2,1)S(1)} %broadcast_select_fusion), channel_id=1, source_target_pairs={{0,32},{16,48},{32,0},{48,16},{1,33},{17,49},{33,1},{49,17},{2,34}... | collective-permute-start | bytes 1376264 | tf_op jit(solution)/shard_map/token_features/ppermute | solution.py:52
  34.6 0.9 slice.18
  35.6 2.0 %slice.19 = bf16[3,112,896]{2,1,0:T(8,128)(2,1)} slice(bf16[3,224,896]{2,1,0:T(8,128)(2,1)} %collective-permute-done.7.w2), slice={[0:3], [112:224], [0:896]} | slice | bytes 1204224 | tf_op jit(solution)/shard_map/weight_rows/slice | solution.py:331
  37.6 2.6 %collective-permute-start.9 = (bf16[3,112,896]{2,1,0:T(8,128)(2,1)}, bf16[3,112,896]{2,1,0:T(8,128)(2,1)}, u32[]{:S(2)}, u32[]{:S(2)}) collective-permute-start(bf16[3,112,896]{2,1,0:T(8,128)(2,1)} %slice.19), channel_id=1, source_target_pairs={{0,192},{64,0},{128,64},{192,128},{1,193},{65,1},{129,65},{193,129... | collective-permute-start | bytes 1806344 | tf_op jit(solution)/shard_map/weight_rows/ppermute | solution.py:52
  40.2 3.6 %collective-permute-done.a1 = bf16[896,256]{1,0:T(8,128)(2,1)} collective-permute-done((bf16[896,256]{1,0:T(8,128)(2,1)S(1)}, bf16[896,256]{1,0:T(8,128)(2,1)}, u32[]{:S(2)}, u32[]{:S(2)}) %collective-permute-start) | collective-permute-done | bytes 458784 | tf_op jit(solution)/shard_map/token_features/ppermute | solution.py:52
  43.7 1.0 collective-permute-start.3
  44.7 9.0 %collective-permute-start.4 = (bf16[896,256]{1,0:T(8,128)(2,1)}, bf16[896,256]{1,0:T(8,128)(2,1)}, u32[]{:S(2)}, u32[]{:S(2)}) collective-permute-start(bf16[896,256]{1,0:T(8,128)(2,1)} %collective-permute-done.1.a2), channel_id=1, source_target_pairs={{0,1},{1,0},{2,3},{3,2},{4,5},{5,4},{6,7},{7,6},{8,9},{9,8},{10,11... | collective-permute-start | bytes 1376264 | tf_op jit(solution)/shard_map/token_features/ppermute | solution.py:56
  53.7 0.8 collective-permute-done.2.a3
  54.5 1.0 collective-permute-start.5
  55.6 1.7 %collective-permute-done.5.b3 = bf16[896,256]{1,0:T(8,128)(2,1)} collective-permute-done((bf16[896,256]{1,0:T(8,128)(2,1)}, bf16[896,256]{1,0:T(8,128)(2,1)}, u32[]{:S(2)}, u32[]{:S(2)}) %collective-permute-start.5) | collective-permute-done | bytes 458784 | tf_op jit(solution)/shard_map/token_features/ppermute | solution.py:56
  57.3 7.1 %mlp.1 = (f32[4,224,256]{2,1,0:T(8,128)S(1)}, f32[4,224,256]{2,1,0:T(8,128)S(1)}, bf16[4,240,256]{2,1,0:T(8,128)(2,1)S(1)}, bf16[4,224,256]{2,1,0:T(8,128)(2,1)S...) custom-call(s32[4]{0:T(128)S(1)} %pad_add_fusion.idx, bf16[896,256]{1,0:T(8,128)(2,1)S(1)} %bitcast.27, ...), custom_call_target="tpu_custom_call" | custom-call | tf_op jit(solution)/shard_map/mlp/mlp/pallas_call | solution.py:344
  64.4 0.5 collective-permute-start.10
  65.3 1.7 %collective-permute-done.11.got2 = bf16[4,224,256]{2,1,0:T(8,128)(2,1)S(1)} collective-permute-done((bf16[4,224,256]{2,1,0:T(8,128)(2,1)S(1)}, bf16[4,224,256]{2,1,0:T(8,128)(2,1)S(1)}, u32[]{:S(2)}, u32[]{:S(2)}) %collective-permute-start.11) | collective-permute-done | bytes 458784 | tf_op jit(solution)/shard_map/hidden_sums/ppermute | solution.py:56
  67.0 0.7 core_sum.1
  67.8 0.9 collective-permute-start.15
  68.7 2.7 %collective-permute-start.16 = (bf16[240,256]{1,0:T(8,128)(2,1)S(1)}, bf16[240,256]{1,0:T(8,128)(2,1)S(1)}, u32[]{:S(2)}, u32[]{:S(2)}) collective-permute-start(bf16[240,256]{1,0:T(8,128)(2,1)S(1)} %get-tuple-element.43), channel_id=1, source_target_pairs={{0,32},{16,48},{32,0},{48,16},{1,33},{17,49},{33,1},{49,17},{2,34}... | collective-permute-start | bytes 368648 | tf_op jit(solution)/shard_map/hidden_sums/ppermute | solution.py:52
  71.4 1.5 %collective-permute-start.12 = (bf16[224,256]{1,0:T(8,128)(2,1)S(1)}, bf16[224,256]{1,0:T(8,128)(2,1)S(1)}, u32[]{:S(2)}, u32[]{:S(2)}) collective-permute-start(bf16[224,256]{1,0:T(8,128)(2,1)S(1)} %get-tuple-element.38), channel_id=1, source_target_pairs={{0,16},{16,32},{32,48},{48,0},{1,17},{17,33},{33,49},{49,1},{2,18}... | collective-permute-start | bytes 344072 | tf_op jit(solution)/shard_map/hidden_sums/ppermute | solution.py:52
  73.1 0.4 collective-permute-done.15.r1
  73.6 1.7 %collective-permute-start.14 = (bf16[224,256]{1,0:T(8,128)(2,1)S(1)}, bf16[224,256]{1,0:T(8,128)(2,1)S(1)}, u32[]{:S(2)}, u32[]{:S(2)}) collective-permute-start(bf16[224,256]{1,0:T(8,128)(2,1)S(1)} %get-tuple-element.40), channel_id=1, source_target_pairs={{0,48},{16,0},{32,16},{48,32},{1,49},{17,1},{33,17},{49,33},{2,50}... | collective-permute-start | bytes 344072 | tf_op jit(solution)/shard_map/hidden_sums/ppermute | solution.py:52
  75.3 1.8 %collective-permute-done.16.r2 = bf16[240,256]{1,0:T(8,128)(2,1)S(1)} collective-permute-done((bf16[240,256]{1,0:T(8,128)(2,1)S(1)}, bf16[240,256]{1,0:T(8,128)(2,1)S(1)}, u32[]{:S(2)}, u32[]{:S(2)}) %collective-permute-start.16) | collective-permute-done | bytes 122912 | tf_op jit(solution)/shard_map/hidden_sums/ppermute | solution.py:52
  77.6 1.9 %collective-permute-done.12.r1 = bf16[224,256]{1,0:T(8,128)(2,1)S(1)} collective-permute-done((bf16[224,256]{1,0:T(8,128)(2,1)S(1)}, bf16[224,256]{1,0:T(8,128)(2,1)S(1)}, u32[]{:S(2)}, u32[]{:S(2)}) %collective-permute-start.12) | collective-permute-done | bytes 114720 | tf_op jit(solution)/shard_map/hidden_sums/ppermute | solution.py:52
  79.5 2.5 %collective-permute-done.13.r2 = bf16[224,256]{1,0:T(8,128)(2,1)S(1)} collective-permute-done((bf16[224,256]{1,0:T(8,128)(2,1)S(1)}, bf16[224,256]{1,0:T(8,128)(2,1)S(1)}, u32[]{:S(2)}, u32[]{:S(2)}) %collective-permute-start.13) | collective-permute-done | bytes 114720 | tf_op jit(solution)/shard_map/hidden_sums/ppermute | solution.py:52
  82.2 3.0 %collective-permute-start.20 = (bf16[240,256]{1,0:T(8,128)(2,1)S(1)}, bf16[240,256]{1,0:T(8,128)(2,1)S(1)}, u32[]{:S(2)}, u32[]{:S(2)}) collective-permute-start(bf16[240,256]{1,0:T(8,128)(2,1)S(1)} %get-tuple-element.50), channel_id=1, source_target_pairs={{0,8},{1,9},{2,10},{3,11},{4,12},{5,13},{6,14},{7,15},{8,0},{9,1},... | collective-permute-start | bytes 368648 | tf_op jit(solution)/shard_map/hidden_sums/ppermute | solution.py:52
  85.3 2.6 %collective-permute-start.21 = (bf16[240,256]{1,0:T(8,128)(2,1)S(1)}, bf16[240,256]{1,0:T(8,128)(2,1)S(1)}, u32[]{:S(2)}, u32[]{:S(2)}) collective-permute-start(bf16[240,256]{1,0:T(8,128)(2,1)S(1)} %get-tuple-element.50), channel_id=1, source_target_pairs={{0,12},{1,13},{2,14},{3,15},{4,0},{5,1},{6,2},{7,3},{8,4},{9,5},{1... | collective-permute-start | bytes 368648 | tf_op jit(solution)/shard_map/hidden_sums/ppermute | solution.py:52
  88.0 0.8 dynamic_slice.26
  89.2 3.1 %copy-done = bf16[4096,896]{1,0:T(8,128)(2,1)S(1)} copy-done((bf16[4096,896]{1,0:T(8,128)(2,1)S(1)}, bf16[4096,896]{1,0:T(8,128)(2,1)}, u32[]{:S(2)}) %copy-start) | copy-done | bytes 7340056
  92.3 1.8 %fetch.1 = (bf16[2,1024,896]{2,1,0:T(8,128)(2,1)S(1)}, f32[224,256]{1,0:T(8,128)S(1)}) custom-call(s32[2,8]{1,0:T(2,128)S(1)} %broadcast_add_fusion.ids, bf16[4096,896]{1,0:T(8,128)(2,1)S(1)} %copy-done, f32[224,256]{1,0:T(8,128)S(1)} %get-tuple-element.48._), custom_call_target="tpu_custom_call", output_to_operand_aliasing={{1}: (2, {})} | custom-call | tf_op jit(solution)/shard_map/hidden_sums/fetch/pallas_call | solution.py:405
  94.1 4.7 %collective-permute-done.21.r3 = bf16[240,256]{1,0:T(8,128)(2,1)S(1)} collective-permute-done((bf16[240,256]{1,0:T(8,128)(2,1)S(1)}, bf16[240,256]{1,0:T(8,128)(2,1)S(1)}, u32[]{:S(2)}, u32[]{:S(2)}) %collective-permute-start.21) | collective-permute-done | bytes 122912 | tf_op jit(solution)/shard_map/hidden_sums/ppermute | solution.py:52
  98.8 0.7 grad.1
  99.6 0.6 collective-permute-start.23
  100.2 3.6 %collective-permute-done.22.g1 = bf16[224,256]{1,0:T(8,128)(2,1)S(1)} collective-permute-done((bf16[224,256]{1,0:T(8,128)(2,1)S(1)}, bf16[224,256]{1,0:T(8,128)(2,1)S(1)}, u32[]{:S(2)}, u32[]{:S(2)}) %collective-permute-start.22) | collective-permute-done | bytes 114720 | tf_op jit(solution)/shard_map/decode/ppermute | solution.py:433
  103.8 1.3 collective-permute-start.24
  105.2 1.0 collective-permute-done.24.g3
  106.1 2.0 %decode.1 = (f32[64,1152]{1,0:T(8,128)S(1)}, bf16[64,1152]{1,0:T(8,128)(2,1)S(1)}, bf16[64,1152]{1,0:T(8,128)(2,1)S(1)}, bf16[64,1152]{1,0:T(8,128)(2,1)S(1)}) custom-call(s32[4]{0:T(128)S(1)} %pad_add_fusion.idx, bf16[224,256]{1,0:T(8,128)(2,1)S(1)} %get-tuple-element.53.g0, bf16[224,256]{1,0:T(8,128)(2,1)S(1)} %collective-permute-done.22.g1, ...), custom_call_target="tpu_custom_call" | custom-call | tf_op jit(solution)/shard_map/decode/decode/pallas_call | solution.py:434
  108.2 1.2 collective-permute-start.25
  109.4 3.1 %collective-permute-start.26 = (bf16[64,1152]{1,0:T(8,128)(2,1)S(1)}, bf16[64,1152]{1,0:T(8,128)(2,1)S(1)}, u32[]{:S(2)}, u32[]{:S(2)}) collective-permute-start(bf16[64,1152]{1,0:T(8,128)(2,1)S(1)} %get-tuple-element.58), channel_id=1, source_target_pairs={{0,32},{16,48},{32,0},{48,16},{1,33},{17,49},{33,1},{49,17},{2,34}... | collective-permute-start | bytes 442376 | tf_op jit(solution)/shard_map/decode/ppermute | solution.py:52
  112.5 2.7 %collective-permute-done.25.r1 = bf16[64,1152]{1,0:T(8,128)(2,1)S(1)} collective-permute-done((bf16[64,1152]{1,0:T(8,128)(2,1)S(1)}, bf16[64,1152]{1,0:T(8,128)(2,1)S(1)}, u32[]{:S(2)}, u32[]{:S(2)}) %collective-permute-start.25) | collective-permute-done | bytes 147488 | tf_op jit(solution)/shard_map/decode/ppermute | solution.py:52
  115.3 4.0 %collective-permute-done.26.r2 = bf16[64,1152]{1,0:T(8,128)(2,1)S(1)} collective-permute-done((bf16[64,1152]{1,0:T(8,128)(2,1)S(1)}, bf16[64,1152]{1,0:T(8,128)(2,1)S(1)}, u32[]{:S(2)}, u32[]{:S(2)}) %collective-permute-start.26) | collective-permute-done | bytes 147488 | tf_op jit(solution)/shard_map/decode/ppermute | solution.py:52
  119.5 0.7 reshape.108
  120.2 5.2 %all-to-all-start = ((bf16[16,4,1152]{2,1,0:T(4,128)(2,1)}), bf16[16,4,1152]{2,1,0:T(4,128)(2,1)S(1)}, u32[]{:S(2)}, u32[]{:S(2)}) async-start(bf16[16,4,1152]{2,1,0:T(4,128)(2,1)} %reshape.108), calls=%async_computation | async-start | bytes 294912 | tf_op jit(solution)/shard_map/scores/all_to_all | solution.py:453
  125.5 9.2 %all-to-all-done.got = bf16[16,4,1152]{2,1,0:T(4,128)(2,1)S(1)} async-done(((bf16[16,4,1152]{2,1,0:T(4,128)(2,1)}), bf16[16,4,1152]{2,1,0:T(4,128)(2,1)S(1)}, u32[]{:S(2)}, u32[]{:S(2)}) %all-to-all-start) | async-done | bytes 147488 | tf_op jit(solution)/shard_map/scores/all_to_all | solution.py:453
  134.7 1.3 score.1
  (62 shorter events, 2.8 us)
Async XLA Ops:
  0.6 6.1 %copy-start.4 = (bf16[256,56]{0,1:T(8,128)(2,1)S(1)}, bf16[256,56]{0,1:T(8,128)(2,1)}, u32[]{:S(2)}) copy-start(bf16[256,56]{0,1:T(8,128)(2,1)} %param.12) | copy-start | bytes 86020
  0.6 6.1 %copy-start.5 = (bf16[256,56]{0,1:T(8,128)(2,1)S(1)}, bf16[256,56]{0,1:T(8,128)(2,1)}, u32[]{:S(2)}) copy-start(bf16[256,56]{0,1:T(8,128)(2,1)} %param.11) | copy-start | bytes 86020
  3.0 31.7 %collective-permute-start.6 = (bf16[3,224,896]{2,1,0:T(8,128)(2,1)}, bf16[3,224,896]{2,1,0:T(8,128)(2,1)S(1)}, u32[]{:S(2)}, u32[]{:S(2)}) collective-permute-start(bf16[3,224,896]{2,1,0:T(8,128)(2,1)} %stack.34.w0), channel_id=1, source_target_pairs={{0,64},{64,128},{128,192},{192,0},{1,65},{65,129},{129,193},{193,1... | collective-permute-start | bytes 3612680 | tf_op jit(solution)/shard_map/weight_rows/ppermute | solution.py:52
  5.2 30.4 %collective-permute-start.7 = (bf16[3,224,896]{2,1,0:T(8,128)(2,1)}, bf16[3,224,896]{2,1,0:T(8,128)(2,1)}, u32[]{:S(2)}, u32[]{:S(2)}) collective-permute-start(bf16[3,224,896]{2,1,0:T(8,128)(2,1)} %stack.34.w0), channel_id=1, source_target_pairs={{0,192},{64,0},{128,64},{192,128},{1,193},{65,1},{129,65},{193,129... | collective-permute-start | bytes 3612680 | tf_op jit(solution)/shard_map/weight_rows/ppermute | solution.py:52
  30.3 27.0 %copy-start.1 = (bf16[3,224,896]{2,1,0:T(8,128)(2,1)S(1)}, bf16[3,224,896]{2,1,0:T(8,128)(2,1)}, u32[]{:S(2)}) copy-start(bf16[3,224,896]{2,1,0:T(8,128)(2,1)} %stack.34.w0) | copy-start | bytes 3612676
  30.3 27.0 %copy-start.3 = (f32[3584]{0:T(1024)S(1)}, f32[3584]{0:T(1024)}, u32[]{:S(2)}) copy-start(f32[3584]{0:T(1024)} %param.13) | copy-start | bytes 43012
  30.4 13.4 %collective-permute-start = (bf16[896,256]{1,0:T(8,128)(2,1)S(1)}, bf16[896,256]{1,0:T(8,128)(2,1)}, u32[]{:S(2)}, u32[]{:S(2)}) collective-permute-start(bf16[896,256]{1,0:T(8,128)(2,1)S(1)} %broadcast_select_fusion), channel_id=1, source_target_pairs={{0,16},{16,32},{32,48},{48,0},{1,17},{17,33},{33,49},{49,1},{2,18}... | collective-permute-start | bytes 1376264 | tf_op jit(solution)/shard_map/token_features/ppermute | solution.py:52
  31.6 13.0 %collective-permute-start.1 = (bf16[896,256]{1,0:T(8,128)(2,1)S(1)}, bf16[896,256]{1,0:T(8,128)(2,1)}, u32[]{:S(2)}, u32[]{:S(2)}) collective-permute-start(bf16[896,256]{1,0:T(8,128)(2,1)S(1)} %broadcast_select_fusion), channel_id=1, source_target_pairs={{0,48},{16,0},{32,16},{48,32},{1,49},{17,1},{33,17},{49,33},{2,50}... | collective-permute-start | bytes 1376264 | tf_op jit(solution)/shard_map/token_features/ppermute | solution.py:52
  33.1 21.4 %collective-permute-start.2 = (bf16[896,256]{1,0:T(8,128)(2,1)S(1)}, bf16[896,256]{1,0:T(8,128)(2,1)}, u32[]{:S(2)}, u32[]{:S(2)}) collective-permute-start(bf16[896,256]{1,0:T(8,128)(2,1)S(1)} %broadcast_select_fusion), channel_id=1, source_target_pairs={{0,32},{16,48},{32,0},{48,16},{1,33},{17,49},{33,1},{49,17},{2,34}... | collective-permute-start | bytes 1376264 | tf_op jit(solution)/shard_map/token_features/ppermute | solution.py:52
  35.5 21.8 %collective-permute-start.8 = (bf16[3,112,896]{2,1,0:T(8,128)(2,1)}, bf16[3,112,896]{2,1,0:T(8,128)(2,1)}, u32[]{:S(2)}, u32[]{:S(2)}) collective-permute-start(bf16[3,112,896]{2,1,0:T(8,128)(2,1)} %slice.18), channel_id=1, source_target_pairs={{0,64},{64,128},{128,192},{192,0},{1,65},{65,129},{129,193},{193,1... | collective-permute-start | bytes 1806344 | tf_op jit(solution)/shard_map/weight_rows/ppermute | solution.py:52
  37.6 19.7 %collective-permute-start.9 = (bf16[3,112,896]{2,1,0:T(8,128)(2,1)}, bf16[3,112,896]{2,1,0:T(8,128)(2,1)}, u32[]{:S(2)}, u32[]{:S(2)}) collective-permute-start(bf16[3,112,896]{2,1,0:T(8,128)(2,1)} %slice.19), channel_id=1, source_target_pairs={{0,192},{64,0},{128,64},{192,128},{1,193},{65,1},{129,65},{193,129... | collective-permute-start | bytes 1806344 | tf_op jit(solution)/shard_map/weight_rows/ppermute | solution.py:52
  43.7 11.9 %collective-permute-start.3 = (bf16[896,256]{1,0:T(8,128)(2,1)}, bf16[896,256]{1,0:T(8,128)(2,1)}, u32[]{:S(2)}, u32[]{:S(2)}) collective-permute-start(bf16[896,256]{1,0:T(8,128)(2,1)} %collective-permute-done.a1), channel_id=1, source_target_pairs={{0,1},{1,0},{2,3},{3,2},{4,5},{5,4},{6,7},{7,6},{8,9},{9,8},{10,11... | collective-permute-start | bytes 1376264 | tf_op jit(solution)/shard_map/token_features/ppermute | solution.py:56
  44.7 10.9 %collective-permute-start.4 = (bf16[896,256]{1,0:T(8,128)(2,1)}, bf16[896,256]{1,0:T(8,128)(2,1)}, u32[]{:S(2)}, u32[]{:S(2)}) collective-permute-start(bf16[896,256]{1,0:T(8,128)(2,1)} %collective-permute-done.1.a2), channel_id=1, source_target_pairs={{0,1},{1,0},{2,3},{3,2},{4,5},{5,4},{6,7},{7,6},{8,9},{9,8},{10,11... | collective-permute-start | bytes 1376264 | tf_op jit(solution)/shard_map/token_features/ppermute | solution.py:56
  54.5 2.7 %collective-permute-start.5 = (bf16[896,256]{1,0:T(8,128)(2,1)}, bf16[896,256]{1,0:T(8,128)(2,1)}, u32[]{:S(2)}, u32[]{:S(2)}) collective-permute-start(bf16[896,256]{1,0:T(8,128)(2,1)} %collective-permute-done.2.a3), channel_id=1, source_target_pairs={{0,1},{1,0},{2,3},{3,2},{4,5},{5,4},{6,7},{7,6},{8,9},{9,8},{10,11... | collective-permute-start | bytes 1376264 | tf_op jit(solution)/shard_map/token_features/ppermute | solution.py:56
  57.3 7.9 %copy-start.6 = (s32[2,32]{1,0:T(2,128)S(1)}, s32[2,32]{1,0:T(2,128)}, u32[]{:S(2)}) copy-start(s32[2,32]{1,0:T(2,128)} %param.19) | copy-start | bytes 772
  57.3 7.9 %copy-start.7 = (s32[2]{0:T(128)S(1)}, s32[2]{0:T(128)}, u32[]{:S(2)}) copy-start(s32[2]{0:T(128)} %param.20) | copy-start | bytes 28
  64.4 2.6 %collective-permute-start.10 = (bf16[4,240,256]{2,1,0:T(8,128)(2,1)S(1)}, bf16[4,240,256]{2,1,0:T(8,128)(2,1)S(1)}, u32[]{:S(2)}, u32[]{:S(2)}) collective-permute-start(bf16[4,240,256]{2,1,0:T(8,128)(2,1)S(1)} %get-tuple-element.34), channel_id=1, source_target_pairs={{0,1},{1,0},{2,3},{3,2},{4,5},{5,4},{6,7},{7,6},{8,9},{9,8},{10,11... | collective-permute-start | bytes 1474568 | tf_op jit(solution)/shard_map/hidden_sums/ppermute | solution.py:56
  64.9 2.1 %collective-permute-start.11 = (bf16[4,224,256]{2,1,0:T(8,128)(2,1)S(1)}, bf16[4,224,256]{2,1,0:T(8,128)(2,1)S(1)}, u32[]{:S(2)}, u32[]{:S(2)}) collective-permute-start(bf16[4,224,256]{2,1,0:T(8,128)(2,1)S(1)} %get-tuple-element.35), channel_id=1, source_target_pairs={{0,1},{1,0},{2,3},{3,2},{4,5},{5,4},{6,7},{7,6},{8,9},{9,8},{10,11... | collective-permute-start | bytes 1376264 | tf_op jit(solution)/shard_map/hidden_sums/ppermute | solution.py:56
  67.8 5.8 %collective-permute-start.15 = (bf16[240,256]{1,0:T(8,128)(2,1)S(1)}, bf16[240,256]{1,0:T(8,128)(2,1)S(1)}, u32[]{:S(2)}, u32[]{:S(2)}) collective-permute-start(bf16[240,256]{1,0:T(8,128)(2,1)S(1)} %get-tuple-element.42), channel_id=1, source_target_pairs={{0,16},{16,32},{32,48},{48,0},{1,17},{17,33},{33,49},{49,1},{2,18}... | collective-permute-start | bytes 368648 | tf_op jit(solution)/shard_map/hidden_sums/ppermute | solution.py:52
  68.7 8.4 %collective-permute-start.16 = (bf16[240,256]{1,0:T(8,128)(2,1)S(1)}, bf16[240,256]{1,0:T(8,128)(2,1)S(1)}, u32[]{:S(2)}, u32[]{:S(2)}) collective-permute-start(bf16[240,256]{1,0:T(8,128)(2,1)S(1)} %get-tuple-element.43), channel_id=1, source_target_pairs={{0,32},{16,48},{32,0},{48,16},{1,33},{17,49},{33,1},{49,17},{2,34}... | collective-permute-start | bytes 368648 | tf_op jit(solution)/shard_map/hidden_sums/ppermute | solution.py:52
  71.4 5.7 %collective-permute-start.17 = (bf16[240,256]{1,0:T(8,128)(2,1)S(1)}, bf16[240,256]{1,0:T(8,128)(2,1)S(1)}, u32[]{:S(2)}, u32[]{:S(2)}) collective-permute-start(bf16[240,256]{1,0:T(8,128)(2,1)S(1)} %get-tuple-element.44), channel_id=1, source_target_pairs={{0,48},{16,0},{32,16},{48,32},{1,49},{17,1},{33,17},{49,33},{2,50}... | collective-permute-start | bytes 368648 | tf_op jit(solution)/shard_map/hidden_sums/ppermute | solution.py:52
  71.4 8.1 %collective-permute-start.12 = (bf16[224,256]{1,0:T(8,128)(2,1)S(1)}, bf16[224,256]{1,0:T(8,128)(2,1)S(1)}, u32[]{:S(2)}, u32[]{:S(2)}) collective-permute-start(bf16[224,256]{1,0:T(8,128)(2,1)S(1)} %get-tuple-element.38), channel_id=1, source_target_pairs={{0,16},{16,32},{32,48},{48,0},{1,17},{17,33},{33,49},{49,1},{2,18}... | collective-permute-start | bytes 344072 | tf_op jit(solution)/shard_map/hidden_sums/ppermute | solution.py:52
  72.8 9.2 %collective-permute-start.13 = (bf16[224,256]{1,0:T(8,128)(2,1)S(1)}, bf16[224,256]{1,0:T(8,128)(2,1)S(1)}, u32[]{:S(2)}, u32[]{:S(2)}) collective-permute-start(bf16[224,256]{1,0:T(8,128)(2,1)S(1)} %get-tuple-element.39), channel_id=1, source_target_pairs={{0,32},{16,48},{32,0},{48,16},{1,33},{17,49},{33,1},{49,17},{2,34}... | collective-permute-start | bytes 344072 | tf_op jit(solution)/shard_map/hidden_sums/ppermute | solution.py:52
  73.6 8.4 %collective-permute-start.14 = (bf16[224,256]{1,0:T(8,128)(2,1)S(1)}, bf16[224,256]{1,0:T(8,128)(2,1)S(1)}, u32[]{:S(2)}, u32[]{:S(2)}) collective-permute-start(bf16[224,256]{1,0:T(8,128)(2,1)S(1)} %get-tuple-element.40), channel_id=1, source_target_pairs={{0,48},{16,0},{32,16},{48,32},{1,49},{17,1},{33,17},{49,33},{2,50}... | collective-permute-start | bytes 344072 | tf_op jit(solution)/shard_map/hidden_sums/ppermute | solution.py:52
  77.2 4.8 %collective-permute-start.18 = (bf16[240,256]{1,0:T(8,128)(2,1)S(1)}, bf16[240,256]{1,0:T(8,128)(2,1)S(1)}, u32[]{:S(2)}, u32[]{:S(2)}) collective-permute-start(bf16[240,256]{1,0:T(8,128)(2,1)S(1)} %get-tuple-element.46), channel_id=1, source_target_pairs={{0,2},{1,3},{2,0},{3,1},{4,6},{5,7},{6,4},{7,5},{8,10},{9,11},{10,... | collective-permute-start | bytes 368648 | tf_op jit(solution)/shard_map/hidden_sums/ppermute | solution.py:394
  82.1 11.9 %collective-permute-start.19 = (bf16[240,256]{1,0:T(8,128)(2,1)S(1)}, bf16[240,256]{1,0:T(8,128)(2,1)S(1)}, u32[]{:S(2)}, u32[]{:S(2)}) collective-permute-start(bf16[240,256]{1,0:T(8,128)(2,1)S(1)} %get-tuple-element.50), channel_id=1, source_target_pairs={{0,4},{1,5},{2,6},{3,7},{4,8},{5,9},{6,10},{7,11},{8,12},{9,13},{1... | collective-permute-start | bytes 368648 | tf_op jit(solution)/shard_map/hidden_sums/ppermute | solution.py:52
  82.2 11.9 %collective-permute-start.20 = (bf16[240,256]{1,0:T(8,128)(2,1)S(1)}, bf16[240,256]{1,0:T(8,128)(2,1)S(1)}, u32[]{:S(2)}, u32[]{:S(2)}) collective-permute-start(bf16[240,256]{1,0:T(8,128)(2,1)S(1)} %get-tuple-element.50), channel_id=1, source_target_pairs={{0,8},{1,9},{2,10},{3,11},{4,12},{5,13},{6,14},{7,15},{8,0},{9,1},... | collective-permute-start | bytes 368648 | tf_op jit(solution)/shard_map/hidden_sums/ppermute | solution.py:52
  85.3 13.5 %collective-permute-start.21 = (bf16[240,256]{1,0:T(8,128)(2,1)S(1)}, bf16[240,256]{1,0:T(8,128)(2,1)S(1)}, u32[]{:S(2)}, u32[]{:S(2)}) collective-permute-start(bf16[240,256]{1,0:T(8,128)(2,1)S(1)} %get-tuple-element.50), channel_id=1, source_target_pairs={{0,12},{1,13},{2,14},{3,15},{4,0},{5,1},{6,2},{7,3},{8,4},{9,5},{1... | collective-permute-start | bytes 368648 | tf_op jit(solution)/shard_map/hidden_sums/ppermute | solution.py:52
  89.2 3.1 %copy-start = (bf16[4096,896]{1,0:T(8,128)(2,1)S(1)}, bf16[4096,896]{1,0:T(8,128)(2,1)}, u32[]{:S(2)}) copy-start(bf16[4096,896]{1,0:T(8,128)(2,1)} %decoder.1) | copy-start | bytes 22020100
  99.5 4.3 %collective-permute-start.22 = (bf16[224,256]{1,0:T(8,128)(2,1)S(1)}, bf16[224,256]{1,0:T(8,128)(2,1)S(1)}, u32[]{:S(2)}, u32[]{:S(2)}) collective-permute-start(bf16[224,256]{1,0:T(8,128)(2,1)S(1)} %get-tuple-element.53.g0), channel_id=1, source_target_pairs={{0,2},{1,3},{2,0},{3,1},{4,6},{5,7},{6,4},{7,5},{8,10},{9,11},{10,... | collective-permute-start | bytes 344072 | tf_op jit(solution)/shard_map/decode/ppermute | solution.py:433
  99.6 5.6 %collective-permute-start.23 = (bf16[224,256]{1,0:T(8,128)(2,1)S(1)}, bf16[224,256]{1,0:T(8,128)(2,1)S(1)}, u32[]{:S(2)}, u32[]{:S(2)}) collective-permute-start(bf16[224,256]{1,0:T(8,128)(2,1)S(1)} %get-tuple-element.53.g0), channel_id=1, source_target_pairs={{0,1},{1,0},{2,3},{3,2},{4,5},{5,4},{6,7},{7,6},{8,9},{9,8},{10,11... | collective-permute-start | bytes 344072 | tf_op jit(solution)/shard_map/decode/ppermute | solution.py:56
  103.8 2.3 %collective-permute-start.24 = (bf16[224,256]{1,0:T(8,128)(2,1)S(1)}, bf16[224,256]{1,0:T(8,128)(2,1)S(1)}, u32[]{:S(2)}, u32[]{:S(2)}) collective-permute-start(bf16[224,256]{1,0:T(8,128)(2,1)S(1)} %collective-permute-done.22.g1), channel_id=1, source_target_pairs={{0,1},{1,0},{2,3},{3,2},{4,5},{5,4},{6,7},{7,6},{8,9},{9,8},{10,11... | collective-permute-start | bytes 344072 | tf_op jit(solution)/shard_map/decode/ppermute | solution.py:56
  108.2 26.5 %copy-start.2 = (bf16[4,4096]{1,0:T(4,128)(2,1)S(1)}, bf16[4,4096]{1,0:T(4,128)(2,1)}, u32[]{:S(2)}) copy-start(bf16[4,4096]{1,0:T(4,128)(2,1)} %acts.1) | copy-start | bytes 98308
  108.2 7.1 %collective-permute-start.25 = (bf16[64,1152]{1,0:T(8,128)(2,1)S(1)}, bf16[64,1152]{1,0:T(8,128)(2,1)S(1)}, u32[]{:S(2)}, u32[]{:S(2)}) collective-permute-start(bf16[64,1152]{1,0:T(8,128)(2,1)S(1)} %get-tuple-element.57), channel_id=1, source_target_pairs={{0,16},{16,32},{32,48},{48,0},{1,17},{17,33},{33,49},{49,1},{2,18}... | collective-permute-start | bytes 442376 | tf_op jit(solution)/shard_map/decode/ppermute | solution.py:52
  109.4 9.8 %collective-permute-start.26 = (bf16[64,1152]{1,0:T(8,128)(2,1)S(1)}, bf16[64,1152]{1,0:T(8,128)(2,1)S(1)}, u32[]{:S(2)}, u32[]{:S(2)}) collective-permute-start(bf16[64,1152]{1,0:T(8,128)(2,1)S(1)} %get-tuple-element.58), channel_id=1, source_target_pairs={{0,32},{16,48},{32,0},{48,16},{1,33},{17,49},{33,1},{49,17},{2,34}... | collective-permute-start | bytes 442376 | tf_op jit(solution)/shard_map/decode/ppermute | solution.py:52
  112.5 6.8 %collective-permute-start.27 = (bf16[64,1152]{1,0:T(8,128)(2,1)S(1)}, bf16[64,1152]{1,0:T(8,128)(2,1)S(1)}, u32[]{:S(2)}, u32[]{:S(2)}) collective-permute-start(bf16[64,1152]{1,0:T(8,128)(2,1)S(1)} %get-tuple-element.59), channel_id=1, source_target_pairs={{0,48},{16,0},{32,16},{48,32},{1,49},{17,1},{33,17},{49,33},{2,50}... | collective-permute-start | bytes 442376 | tf_op jit(solution)/shard_map/decode/ppermute | solution.py:52
  120.2 14.5 %all-to-all-start = ((bf16[16,4,1152]{2,1,0:T(4,128)(2,1)}), bf16[16,4,1152]{2,1,0:T(4,128)(2,1)S(1)}, u32[]{:S(2)}, u32[]{:S(2)}) async-start(bf16[16,4,1152]{2,1,0:T(4,128)(2,1)} %reshape.108), calls=%async_computation | async-start | bytes 294912 | tf_op jit(solution)/shard_map/scores/all_to_all | solution.py:453

commit v5 on v4

--- a/solution.py
+++ b/solution.py
@@ -66,21 +66,36 @@
     return jnp.where(index == 0, high, jnp.where(index == 1, low, 0.0))
 
 
-def mlp_kernel(idx, x0, g0, a1, a2, a3, b1, b2, b3, gain, w0, w1, w2, w3, w4, *refs):
+def early_kernel(idx, x0, g0, a1, a2, b1, b2, x_out, g_out, square_out):
+    tensor, core = idx[1], idx[3]
+    first = core == 0
+    square = jnp.zeros((8, TOK), F32)
+    for e, a, b in ((0, x0, g0), (1, a1, b1), (3, a2, b2)):
+        at = pl.ds(pl.multiple_of(lax.rem(tensor - e + N_T, N_T) * CHUNK, 16), CHUNK)
+        va, vb = a[...], b[...]
+        if e:
+            va, vb = jnp.where(first, va, vb), jnp.where(first, vb, va)
+        x_out[at, :] = va
+        g_out[at, :] = vb
+        x = va.astype(F32)
+        square += jnp.sum((x * x).reshape(CHUNK // 8, 8, TOK), axis=0)
+    square_out[...] = square
+
+
+def mlp_kernel(idx, x_in, g_in, square_in, a3, b3, gain, w0, w1, w2, w3, w4, *refs):
     keep1, keep2, send1, send2, cen_out, root_out = refs[:6]
     x_scr, g_scr, grads, part, out_scr = refs[6:]
     dp, tensor, odd, core = idx[0], idx[1], lax.rem(idx[2], 2), idx[3]
     first = core == 0
-    square = jnp.zeros((8, TOK), F32)
-    for e, a, b in ((0, x0, g0), (1, a1, b1), (3, a2, b2), (2, a3, b3)):
-        at = pl.ds(pl.multiple_of(lax.rem(tensor - e + N_T, N_T) * CHUNK, 16), CHUNK)
-        va, vb = a[...], b[...]
-        if e:
-            va, vb = jnp.where(first, va, vb), jnp.where(first, vb, va)
-        x_scr[at, :] = va
-        g_scr[at, :] = vb
-        x = va.astype(F32)
-        square += jnp.sum((x * x).reshape(CHUNK // 8, 8, TOK), axis=0)
+    x_scr[...] = x_in[...]
+    g_scr[...] = g_in[...]
+    at = pl.ds(pl.multiple_of(lax.rem(tensor + 2, N_T) * CHUNK, 16), CHUNK)
+    va, vb = a3[...], b3[...]
+    va, vb = jnp.where(first, va, vb), jnp.where(first, vb, va)
+    x_scr[at, :] = va
+    g_scr[at, :] = vb
+    x = va.astype(F32)
+    square = square_in[...] + jnp.sum((x * x).reshape(CHUNK // 8, 8, TOK), axis=0)
     mean = jnp.sum(square, axis=0, keepdims=True) * (1.0 / D)
     root = jnp.sqrt(mean + EPS)
     root_out[...] = root
@@ -341,10 +356,17 @@
 
     with jax.named_scope("mlp"):
         row = shape((1, TOK), F32)
+        early = call(
+            early_kernel,
+            "early",
+            [SMEM] + [VMEM] * 6,
+            (shape((D, TOK), BF16), shape((D, TOK), BF16), shape((8, TOK), F32)),
+            limit=14,
+        )(idx, x_all, g_all, own[0], own[1], other[0], other[1])
         keep1, keep2, send1, send2, cen, root = call(
             mlp_kernel,
             "mlp",
-            [SMEM] + [VMEM] * 14,
+            [SMEM] + [VMEM] * 11,
             (
                 shape((N_T, GROUP, TOK), F32),
                 shape((N_T, GROUP, TOK), F32),
@@ -362,7 +384,7 @@
             ],
             limit=20,
         )(
-            idx, x_all, g_all, *own, *other, norm_gain.reshape(D // BLOCK, BLOCK),
+            idx, *early, own[2], other[2], norm_gain.reshape(D // BLOCK, BLOCK),
             rows, below, above, far_low, far_high,
         )
 

time: 136 us -> 138 us (1.015)
  Pallas kernels: 16.4 us -> 19 us
    ppermute x7, starting transfers between devices: 13.6 us -> 8.26 us  [swap_core(): return lax.ppermute(x, 'latent', [(i, i ^ 1) for i in range(N_L)])]
    ppermute x1, starting transfers between devices: 0.09 us -> 5 us  [on_device(): across = lax.ppermute(cast, 'latent', [(i, i ^ 2) for i in range(N_L)])]
    ppermute x19, waiting for transfers between devices: 22.5 us -> 25.2 us  [shift(): return lax.ppermute(x, axis, [(i, (i + by) % size) for i in range(size)])]
    ppermute x1, waiting for transfers between devices: 3.63 us -> 1.2 us  [on_device(): across = lax.ppermute(cast, 'latent', [(i, i ^ 2) for i in range(N_L)])]
    pallas_call x1, Pallas kernels: 1.78 us -> 3.26 us  [on_device(): pl.pallas_call(fetch_kernel, name='fetch', in_specs=[SMEM, HBM, ANY], out...]
    pallas_call x1 -> x2, Pallas kernels: 7.1 us -> 8.17 us  [the longest x1 6.55 us: on_device(): call(mlp_kernel, 'mlp', [SMEM] + [VMEM] * 11, (shape((N_T, GROUP, TOK), F...]
  transfers between devices with their start and end apart: 29 -> 29, of which waited for: 14 -> 14; matrix products, arithmetic and copies ran while one was open for 4% -> 4% of each run, Pallas kernels for 1% -> 4%
where the time goes in v5:
time: 138 us
  starting transfers between devices  46.1 us (33%)
  waiting for transfers between devices  40 us (29%)
  blocking collectives  23.3 us (17%)
  Pallas kernels  19 us (14%)
  local copies, waits for them, and re-layouts  8.02 us (6%)
    ppermute x19, starting transfers between devices, shift(): return lax.ppermute(x, axis, [(i, (i + by) % size) for i in range(size)])  26.9 us
    ppermute x19, waiting for transfers between devices, shift(): return lax.ppermute(x, axis, [(i, (i + by) % size) for i in range(size)])  25.2 us
    all_gather x1, blocking collectives, on_device(): column = lax.all_gather(jnp.concatenate([x_own, g_own]), 'latent', axis=0)  23.3 us
    all_to_all x1, waiting for transfers between devices, on_device(): lax.all_to_all(products.reshape(N_L, 4, WIDE), 'latent', 0, 0, tiled=True)  9.23 us
    ppermute x7, starting transfers between devices, swap_core(): return lax.ppermute(x, 'latent', [(i, i ^ 1) for i in range(N_L)])  8.26 us
    pallas_call x1, Pallas kernels, on_device(): call(mlp_kernel, 'mlp', [SMEM] + [VMEM] * 11, (shape((N_T, GROUP, TOK), F...  6.55 us
    all_to_all x1, starting transfers between devices, on_device(): lax.all_to_all(products.reshape(N_L, 4, WIDE), 'latent', 0, 0, tiled=True)  5.86 us
    ppermute x1, starting transfers between devices, on_device(): across = lax.ppermute(cast, 'latent', [(i, i ^ 2) for i in range(N_L)])  5 us
  transfers between devices with their start and end apart: 29, of which 14 were waited for; matrix products, arithmetic and copies ran while one was open for 4% of the time, Pallas kernels for 4%

profile of v5, /device:TPU:1, one launch (start us, length us, event | category | flops | bytes accessed | tf_op | source)
XLA Modules:
  0.0 138.0 jit_solution(11366815634397409666)
XLA Ops:
  0.7 2.3 %stack.34.w0 = bf16[3,224,896]{2,1,0:T(8,128)(2,1)} custom-call(bf16[224,896]{1,0:T(8,128)(2,1)} %bitcast.34, bf16[224,896]{1,0:T(8,128)(2,1)} %bitcast.35, bf16[224,896]{1,0:T(8,128)(2,1)} %bitcast.36), custom_call_target="tpu_custom_call" | custom-call | tf_op jit(solution)/shard_map/weight_rows/stack/pallas_call | solution.py:334
  3.0 3.6 %collective-permute-start.7 = (bf16[3,224,896]{2,1,0:T(8,128)(2,1)}, bf16[3,224,896]{2,1,0:T(8,128)(2,1)S(1)}, u32[]{:S(2)}, u32[]{:S(2)}) collective-permute-start(bf16[3,224,896]{2,1,0:T(8,128)(2,1)} %stack.34.w0), channel_id=1, source_target_pairs={{0,192},{64,0},{128,64},{192,128},{1,193},{65,1},{129,65},{193,129... | collective-permute-start | bytes 3612680 | tf_op jit(solution)/shard_map/weight_rows/ppermute | solution.py:52
  6.6 23.3 %all-gather = bf16[1792,256]{1,0:T(8,128)(2,1)S(1)} all-gather(bf16[112,256]{1,0:T(8,128)(2,1)S(1)} %pad_maximum_fusion), channel_id=2, replica_groups=mesh['dp'=4,'tensor'=4,'latent'=16] {'latent'}, dimensions={0}, use_global_device_ids=true | all-gather | bytes 974848 | tf_op jit(solution)/shard_map/token_features/all_gather | solution.py:350
  30.1 2.6 %collective-permute-start.1 = (bf16[896,256]{1,0:T(8,128)(2,1)S(1)}, bf16[896,256]{1,0:T(8,128)(2,1)}, u32[]{:S(2)}, u32[]{:S(2)}) collective-permute-start(bf16[896,256]{1,0:T(8,128)(2,1)S(1)} %broadcast_select_fusion), channel_id=1, source_target_pairs={{0,48},{16,0},{32,16},{48,32},{1,49},{17,1},{33,17},{49,33},{2,50}... | collective-permute-start | bytes 1376264 | tf_op jit(solution)/shard_map/token_features/ppermute | solution.py:52
  32.7 1.7 %collective-permute-start.4 = (bf16[896,256]{1,0:T(8,128)(2,1)S(1)}, bf16[896,256]{1,0:T(8,128)(2,1)}, u32[]{:S(2)}, u32[]{:S(2)}) collective-permute-start(bf16[896,256]{1,0:T(8,128)(2,1)S(1)} %broadcast_select_fusion), channel_id=1, source_target_pairs={{0,32},{16,48},{32,0},{48,16},{1,33},{17,49},{33,1},{49,17},{2,34}... | collective-permute-start | bytes 1376264 | tf_op jit(solution)/shard_map/token_features/ppermute | solution.py:52
  34.4 0.9 slice.19
  35.3 2.9 %collective-permute-start.9 = (bf16[3,112,896]{2,1,0:T(8,128)(2,1)}, bf16[3,112,896]{2,1,0:T(8,128)(2,1)}, u32[]{:S(2)}, u32[]{:S(2)}) collective-permute-start(bf16[3,112,896]{2,1,0:T(8,128)(2,1)} %slice.19), channel_id=1, source_target_pairs={{0,192},{64,0},{128,64},{192,128},{1,193},{65,1},{129,65},{193,129... | collective-permute-start | bytes 1806344 | tf_op jit(solution)/shard_map/weight_rows/ppermute | solution.py:52
  38.2 1.9 %slice.18 = bf16[3,112,896]{2,1,0:T(8,128)(2,1)} slice(bf16[3,224,896]{2,1,0:T(8,128)(2,1)} %collective-permute-done.6.w1), slice={[0:3], [0:112], [0:896]} | slice | bytes 1204224 | tf_op jit(solution)/shard_map/weight_rows/slice | solution.py:345
  40.2 11.9 %collective-permute-done.1.a2 = bf16[896,256]{1,0:T(8,128)(2,1)} collective-permute-done((bf16[896,256]{1,0:T(8,128)(2,1)S(1)}, bf16[896,256]{1,0:T(8,128)(2,1)}, u32[]{:S(2)}, u32[]{:S(2)}) %collective-permute-start.1) | collective-permute-done | bytes 458784 | tf_op jit(solution)/shard_map/token_features/ppermute | solution.py:52
  52.1 1.1 collective-permute-start.3
  53.3 3.5 %collective-permute-start.2 = (bf16[896,256]{1,0:T(8,128)(2,1)}, bf16[896,256]{1,0:T(8,128)(2,1)}, u32[]{:S(2)}, u32[]{:S(2)}) collective-permute-start(bf16[896,256]{1,0:T(8,128)(2,1)} %collective-permute-done.a1), channel_id=1, source_target_pairs={{0,1},{1,0},{2,3},{3,2},{4,5},{5,4},{6,7},{7,6},{8,9},{9,8},{10,11... | collective-permute-start | bytes 1376264 | tf_op jit(solution)/shard_map/token_features/ppermute | solution.py:56
  56.8 1.7 %collective-permute-done.2.b1 = bf16[896,256]{1,0:T(8,128)(2,1)} collective-permute-done((bf16[896,256]{1,0:T(8,128)(2,1)}, bf16[896,256]{1,0:T(8,128)(2,1)}, u32[]{:S(2)}, u32[]{:S(2)}) %collective-permute-start.2) | collective-permute-done | bytes 458784 | tf_op jit(solution)/shard_map/token_features/ppermute | solution.py:56
  58.5 1.6 %early.1 = (bf16[3584,256]{1,0:T(8,128)(2,1)S(1)}, bf16[3584,256]{1,0:T(8,128)(2,1)S(1)}, f32[8,256]{1,0:T(8,128)S(1)}) custom-call(s32[4]{0:T(128)S(1)} %pad_add_fusion.idx, bf16[896,256]{1,0:T(8,128)(2,1)S(1)} %bitcast.27, bf16[896,256]{1,0:T(8,128)(2,1)S(1)} %bitcast.25, bf16[896,256]{1,0:T(8,128)(2,1)} %collective-permute-done.a1, ...), custom_call_target="tpu_custom_call" | custom-call | tf_op jit(solution)/shard_map/mlp/early/pallas_call | solution.py:359
  60.3 6.5 %mlp.1 = (f32[4,224,256]{2,1,0:T(8,128)S(1)}, f32[4,224,256]{2,1,0:T(8,128)S(1)}, bf16[4,240,256]{2,1,0:T(8,128)(2,1)S(1)}, bf16[4,224,256]{2,1,0:T(8,128)(2,1)S...) custom-call(s32[4]{0:T(128)S(1)} %pad_add_fusion.idx, bf16[3584,256]{1,0:T(8,128)(2,1)S(1)} %get-tuple-element.35.x_in, ...), custom_call_target="tpu_custom_call" | custom-call | tf_op jit(solution)/shard_map/mlp/mlp/pallas_call | solution.py:366
  66.8 0.5 collective-permute-start.11
  67.7 1.0 collective-permute-done.11.got2
  68.7 0.7 collective-permute-done.10.got1
  69.4 0.7 core_sum.1
  70.2 1.8 %collective-permute-start.16 = (bf16[240,256]{1,0:T(8,128)(2,1)S(1)}, bf16[240,256]{1,0:T(8,128)(2,1)S(1)}, u32[]{:S(2)}, u32[]{:S(2)}) collective-permute-start(bf16[240,256]{1,0:T(8,128)(2,1)S(1)} %get-tuple-element.49), channel_id=1, source_target_pairs={{0,32},{16,48},{32,0},{48,16},{1,33},{17,49},{33,1},{49,17},{2,34}... | collective-permute-start | bytes 368648 | tf_op jit(solution)/shard_map/hidden_sums/ppermute | solution.py:52
  72.1 0.8 collective-permute-start.17
  72.9 0.7 collective-permute-start.12
  73.6 1.8 %collective-permute-start.13 = (bf16[224,256]{1,0:T(8,128)(2,1)S(1)}, bf16[224,256]{1,0:T(8,128)(2,1)S(1)}, u32[]{:S(2)}, u32[]{:S(2)}) collective-permute-start(bf16[224,256]{1,0:T(8,128)(2,1)S(1)} %get-tuple-element.45), channel_id=1, source_target_pairs={{0,32},{16,48},{32,0},{48,16},{1,33},{17,49},{33,1},{49,17},{2,34}... | collective-permute-start | bytes 344072 | tf_op jit(solution)/shard_map/hidden_sums/ppermute | solution.py:52
  75.4 1.4 %collective-permute-done.15.r1 = bf16[240,256]{1,0:T(8,128)(2,1)S(1)} collective-permute-done((bf16[240,256]{1,0:T(8,128)(2,1)S(1)}, bf16[240,256]{1,0:T(8,128)(2,1)S(1)}, u32[]{:S(2)}, u32[]{:S(2)}) %collective-permute-start.15) | collective-permute-done | bytes 122912 | tf_op jit(solution)/shard_map/hidden_sums/ppermute | solution.py:52
  76.8 0.6 collective-permute-start.14
  77.8 1.1 collective-permute-done.17.r3
  79.5 4.2 %collective-permute-done.12.r1 = bf16[224,256]{1,0:T(8,128)(2,1)S(1)} collective-permute-done((bf16[224,256]{1,0:T(8,128)(2,1)S(1)}, bf16[224,256]{1,0:T(8,128)(2,1)S(1)}, u32[]{:S(2)}, u32[]{:S(2)}) %collective-permute-start.12) | collective-permute-done | bytes 114720 | tf_op jit(solution)/shard_map/hidden_sums/ppermute | solution.py:52
  83.8 2.2 %collective-permute-start.21 = (bf16[240,256]{1,0:T(8,128)(2,1)S(1)}, bf16[240,256]{1,0:T(8,128)(2,1)S(1)}, u32[]{:S(2)}, u32[]{:S(2)}) collective-permute-start(bf16[240,256]{1,0:T(8,128)(2,1)S(1)} %get-tuple-element.56), channel_id=1, source_target_pairs={{0,12},{1,13},{2,14},{3,15},{4,0},{5,1},{6,2},{7,3},{8,4},{9,5},{1... | collective-permute-start | bytes 368648 | tf_op jit(solution)/shard_map/hidden_sums/ppermute | solution.py:52
  86.0 1.2 collective-permute-start.20
  87.2 2.0 %collective-permute-start.19 = (bf16[240,256]{1,0:T(8,128)(2,1)S(1)}, bf16[240,256]{1,0:T(8,128)(2,1)S(1)}, u32[]{:S(2)}, u32[]{:S(2)}) collective-permute-start(bf16[240,256]{1,0:T(8,128)(2,1)S(1)} %get-tuple-element.56), channel_id=1, source_target_pairs={{0,4},{1,5},{2,6},{3,7},{4,8},{5,9},{6,10},{7,11},{8,12},{9,13},{1... | collective-permute-start | bytes 368648 | tf_op jit(solution)/shard_map/hidden_sums/ppermute | solution.py:52
  89.3 0.8 dynamic_slice.26
  90.6 3.1 %copy-done = bf16[4096,896]{1,0:T(8,128)(2,1)S(1)} copy-done((bf16[4096,896]{1,0:T(8,128)(2,1)S(1)}, bf16[4096,896]{1,0:T(8,128)(2,1)}, u32[]{:S(2)}) %copy-start) | copy-done | bytes 7340056
  93.7 3.3 %fetch.1 = (bf16[2,1024,896]{2,1,0:T(8,128)(2,1)S(1)}, f32[224,256]{1,0:T(8,128)S(1)}) custom-call(s32[2,8]{1,0:T(2,128)S(1)} %broadcast_add_fusion.ids, bf16[4096,896]{1,0:T(8,128)(2,1)S(1)} %copy-done, f32[224,256]{1,0:T(8,128)S(1)} %get-tuple-element.54._), custom_call_target="tpu_custom_call", output_to_operand_aliasing={{1}: (2, {})} | custom-call | tf_op jit(solution)/shard_map/hidden_sums/fetch/pallas_call | solution.py:427
  97.0 0.7 grad.1
  97.7 5.0 %collective-permute-start.22 = (bf16[224,256]{1,0:T(8,128)(2,1)S(1)}, bf16[224,256]{1,0:T(8,128)(2,1)S(1)}, u32[]{:S(2)}, u32[]{:S(2)}) collective-permute-start(bf16[224,256]{1,0:T(8,128)(2,1)S(1)} %get-tuple-element.59.g0), channel_id=1, source_target_pairs={{0,2},{1,3},{2,0},{3,1},{4,6},{5,7},{6,4},{7,5},{8,10},{9,11},{10,... | collective-permute-start | bytes 344072 | tf_op jit(solution)/shard_map/decode/ppermute | solution.py:455
  102.7 1.3 collective-permute-start.23
  104.0 1.2 collective-permute-done.22.g1
  105.2 1.6 %collective-permute-start.24 = (bf16[224,256]{1,0:T(8,128)(2,1)S(1)}, bf16[224,256]{1,0:T(8,128)(2,1)S(1)}, u32[]{:S(2)}, u32[]{:S(2)}) collective-permute-start(bf16[224,256]{1,0:T(8,128)(2,1)S(1)} %collective-permute-done.22.g1), channel_id=1, source_target_pairs={{0,1},{1,0},{2,3},{3,2},{4,5},{5,4},{6,7},{7,6},{8,9},{9,8},{10,11... | collective-permute-start | bytes 344072 | tf_op jit(solution)/shard_map/decode/ppermute | solution.py:56
  106.8 1.0 collective-permute-done.24.g3
  107.8 2.0 %decode.1 = (f32[64,1152]{1,0:T(8,128)S(1)}, bf16[64,1152]{1,0:T(8,128)(2,1)S(1)}, bf16[64,1152]{1,0:T(8,128)(2,1)S(1)}, bf16[64,1152]{1,0:T(8,128)(2,1)S(1)}) custom-call(s32[4]{0:T(128)S(1)} %pad_add_fusion.idx, bf16[224,256]{1,0:T(8,128)(2,1)S(1)} %get-tuple-element.59.g0, bf16[224,256]{1,0:T(8,128)(2,1)S(1)} %collective-permute-done.22.g1, ...), custom_call_target="tpu_custom_call" | custom-call | tf_op jit(solution)/shard_map/decode/decode/pallas_call | solution.py:456
  109.8 2.4 %collective-permute-start.25 = (bf16[64,1152]{1,0:T(8,128)(2,1)S(1)}, bf16[64,1152]{1,0:T(8,128)(2,1)S(1)}, u32[]{:S(2)}, u32[]{:S(2)}) collective-permute-start(bf16[64,1152]{1,0:T(8,128)(2,1)S(1)} %get-tuple-element.63), channel_id=1, source_target_pairs={{0,16},{16,32},{32,48},{48,0},{1,17},{17,33},{33,49},{49,1},{2,18}... | collective-permute-start | bytes 442376 | tf_op jit(solution)/shard_map/decode/ppermute | solution.py:52
  112.2 1.7 %collective-permute-start.26 = (bf16[64,1152]{1,0:T(8,128)(2,1)S(1)}, bf16[64,1152]{1,0:T(8,128)(2,1)S(1)}, u32[]{:S(2)}, u32[]{:S(2)}) collective-permute-start(bf16[64,1152]{1,0:T(8,128)(2,1)S(1)} %get-tuple-element.64), channel_id=1, source_target_pairs={{0,32},{16,48},{32,0},{48,16},{1,33},{17,49},{33,1},{49,17},{2,34}... | collective-permute-start | bytes 442376 | tf_op jit(solution)/shard_map/decode/ppermute | solution.py:52
  113.9 0.8 collective-permute-start.27
  114.7 1.7 %collective-permute-done.25.r1 = bf16[64,1152]{1,0:T(8,128)(2,1)S(1)} collective-permute-done((bf16[64,1152]{1,0:T(8,128)(2,1)S(1)}, bf16[64,1152]{1,0:T(8,128)(2,1)S(1)}, u32[]{:S(2)}, u32[]{:S(2)}) %collective-permute-start.25) | collective-permute-done | bytes 147488 | tf_op jit(solution)/shard_map/decode/ppermute | solution.py:52
  116.4 4.2 %collective-permute-done.26.r2 = bf16[64,1152]{1,0:T(8,128)(2,1)S(1)} collective-permute-done((bf16[64,1152]{1,0:T(8,128)(2,1)S(1)}, bf16[64,1152]{1,0:T(8,128)(2,1)S(1)}, u32[]{:S(2)}, u32[]{:S(2)}) %collective-permute-start.26) | collective-permute-done | bytes 147488 | tf_op jit(solution)/shard_map/decode/ppermute | solution.py:52
  120.9 0.7 reshape.108
  121.6 5.9 %all-to-all-start = ((bf16[16,4,1152]{2,1,0:T(4,128)(2,1)}), bf16[16,4,1152]{2,1,0:T(4,128)(2,1)S(1)}, u32[]{:S(2)}, u32[]{:S(2)}) async-start(bf16[16,4,1152]{2,1,0:T(4,128)(2,1)} %reshape.108), calls=%async_computation | async-start | bytes 294912 | tf_op jit(solution)/shard_map/scores/all_to_all | solution.py:475
  127.5 9.2 %all-to-all-done.got = bf16[16,4,1152]{2,1,0:T(4,128)(2,1)S(1)} async-done(((bf16[16,4,1152]{2,1,0:T(4,128)(2,1)}), bf16[16,4,1152]{2,1,0:T(4,128)(2,1)S(1)}, u32[]{:S(2)}, u32[]{:S(2)}) %all-to-all-start) | async-done | bytes 147488 | tf_op jit(solution)/shard_map/scores/all_to_all | solution.py:475
  136.7 1.3 score.1
  (63 shorter events, 2.9 us)
Async XLA Ops:
  0.6 6.0 %copy-start.4 = (bf16[256,56]{0,1:T(8,128)(2,1)S(1)}, bf16[256,56]{0,1:T(8,128)(2,1)}, u32[]{:S(2)}) copy-start(bf16[256,56]{0,1:T(8,128)(2,1)} %param.12) | copy-start | bytes 86020
  0.6 6.0 %copy-start.5 = (bf16[256,56]{0,1:T(8,128)(2,1)S(1)}, bf16[256,56]{0,1:T(8,128)(2,1)}, u32[]{:S(2)}) copy-start(bf16[256,56]{0,1:T(8,128)(2,1)} %param.11) | copy-start | bytes 86020
  3.0 31.4 %collective-permute-start.7 = (bf16[3,224,896]{2,1,0:T(8,128)(2,1)}, bf16[3,224,896]{2,1,0:T(8,128)(2,1)S(1)}, u32[]{:S(2)}, u32[]{:S(2)}) collective-permute-start(bf16[3,224,896]{2,1,0:T(8,128)(2,1)} %stack.34.w0), channel_id=1, source_target_pairs={{0,192},{64,0},{128,64},{192,128},{1,193},{65,1},{129,65},{193,129... | collective-permute-start | bytes 3612680 | tf_op jit(solution)/shard_map/weight_rows/ppermute | solution.py:52
  6.6 31.6 %collective-permute-start.6 = (bf16[3,224,896]{2,1,0:T(8,128)(2,1)}, bf16[3,224,896]{2,1,0:T(8,128)(2,1)}, u32[]{:S(2)}, u32[]{:S(2)}) collective-permute-start(bf16[3,224,896]{2,1,0:T(8,128)(2,1)} %stack.34.w0), channel_id=1, source_target_pairs={{0,64},{64,128},{128,192},{192,0},{1,65},{65,129},{129,193},{193,1... | collective-permute-start | bytes 3612680 | tf_op jit(solution)/shard_map/weight_rows/ppermute | solution.py:52
  30.1 22.0 %collective-permute-start.1 = (bf16[896,256]{1,0:T(8,128)(2,1)S(1)}, bf16[896,256]{1,0:T(8,128)(2,1)}, u32[]{:S(2)}, u32[]{:S(2)}) collective-permute-start(bf16[896,256]{1,0:T(8,128)(2,1)S(1)} %broadcast_select_fusion), channel_id=1, source_target_pairs={{0,48},{16,0},{32,16},{48,32},{1,49},{17,1},{33,17},{49,33},{2,50}... | collective-permute-start | bytes 1376264 | tf_op jit(solution)/shard_map/token_features/ppermute | solution.py:52
  32.7 20.6 %collective-permute-start = (bf16[896,256]{1,0:T(8,128)(2,1)S(1)}, bf16[896,256]{1,0:T(8,128)(2,1)}, u32[]{:S(2)}, u32[]{:S(2)}) collective-permute-start(bf16[896,256]{1,0:T(8,128)(2,1)S(1)} %broadcast_select_fusion), channel_id=1, source_target_pairs={{0,16},{16,32},{32,48},{48,0},{1,17},{17,33},{33,49},{49,1},{2,18}... | collective-permute-start | bytes 1376264 | tf_op jit(solution)/shard_map/token_features/ppermute | solution.py:52
  32.7 24.1 %collective-permute-start.4 = (bf16[896,256]{1,0:T(8,128)(2,1)S(1)}, bf16[896,256]{1,0:T(8,128)(2,1)}, u32[]{:S(2)}, u32[]{:S(2)}) collective-permute-start(bf16[896,256]{1,0:T(8,128)(2,1)S(1)} %broadcast_select_fusion), channel_id=1, source_target_pairs={{0,32},{16,48},{32,0},{48,16},{1,33},{17,49},{33,1},{49,17},{2,34}... | collective-permute-start | bytes 1376264 | tf_op jit(solution)/shard_map/token_features/ppermute | solution.py:52
  35.3 24.9 %copy-start.1 = (bf16[3,224,896]{2,1,0:T(8,128)(2,1)S(1)}, bf16[3,224,896]{2,1,0:T(8,128)(2,1)}, u32[]{:S(2)}) copy-start(bf16[3,224,896]{2,1,0:T(8,128)(2,1)} %stack.34.w0) | copy-start | bytes 3612676
  35.3 24.9 %copy-start.3 = (f32[3584]{0:T(1024)S(1)}, f32[3584]{0:T(1024)}, u32[]{:S(2)}) copy-start(f32[3584]{0:T(1024)} %param.13) | copy-start | bytes 43012
  35.3 24.9 %collective-permute-start.9 = (bf16[3,112,896]{2,1,0:T(8,128)(2,1)}, bf16[3,112,896]{2,1,0:T(8,128)(2,1)}, u32[]{:S(2)}, u32[]{:S(2)}) collective-permute-start(bf16[3,112,896]{2,1,0:T(8,128)(2,1)} %slice.19), channel_id=1, source_target_pairs={{0,192},{64,0},{128,64},{192,128},{1,193},{65,1},{129,65},{193,129... | collective-permute-start | bytes 1806344 | tf_op jit(solution)/shard_map/weight_rows/ppermute | solution.py:52
  40.2 20.0 %collective-permute-start.8 = (bf16[3,112,896]{2,1,0:T(8,128)(2,1)}, bf16[3,112,896]{2,1,0:T(8,128)(2,1)}, u32[]{:S(2)}, u32[]{:S(2)}) collective-permute-start(bf16[3,112,896]{2,1,0:T(8,128)(2,1)} %slice.18), channel_id=1, source_target_pairs={{0,64},{64,128},{128,192},{192,0},{1,65},{65,129},{129,193},{193,1... | collective-permute-start | bytes 1806344 | tf_op jit(solution)/shard_map/weight_rows/ppermute | solution.py:52
  52.1 4.7 %collective-permute-start.3 = (bf16[896,256]{1,0:T(8,128)(2,1)}, bf16[896,256]{1,0:T(8,128)(2,1)}, u32[]{:S(2)}, u32[]{:S(2)}) collective-permute-start(bf16[896,256]{1,0:T(8,128)(2,1)} %collective-permute-done.1.a2), channel_id=1, source_target_pairs={{0,1},{1,0},{2,3},{3,2},{4,5},{5,4},{6,7},{7,6},{8,9},{9,8},{10,11... | collective-permute-start | bytes 1376264 | tf_op jit(solution)/shard_map/token_features/ppermute | solution.py:56
  53.3 5.3 %collective-permute-start.2 = (bf16[896,256]{1,0:T(8,128)(2,1)}, bf16[896,256]{1,0:T(8,128)(2,1)}, u32[]{:S(2)}, u32[]{:S(2)}) collective-permute-start(bf16[896,256]{1,0:T(8,128)(2,1)} %collective-permute-done.a1), channel_id=1, source_target_pairs={{0,1},{1,0},{2,3},{3,2},{4,5},{5,4},{6,7},{7,6},{8,9},{9,8},{10,11... | collective-permute-start | bytes 1376264 | tf_op jit(solution)/shard_map/token_features/ppermute | solution.py:56
  56.8 3.4 %collective-permute-start.5 = (bf16[896,256]{1,0:T(8,128)(2,1)}, bf16[896,256]{1,0:T(8,128)(2,1)}, u32[]{:S(2)}, u32[]{:S(2)}) collective-permute-start(bf16[896,256]{1,0:T(8,128)(2,1)} %collective-permute-done.4.a3), channel_id=1, source_target_pairs={{0,1},{1,0},{2,3},{3,2},{4,5},{5,4},{6,7},{7,6},{8,9},{9,8},{10,11... | collective-permute-start | bytes 1376264 | tf_op jit(solution)/shard_map/token_features/ppermute | solution.py:56
  60.2 7.3 %copy-start.6 = (s32[2,32]{1,0:T(2,128)S(1)}, s32[2,32]{1,0:T(2,128)}, u32[]{:S(2)}) copy-start(s32[2,32]{1,0:T(2,128)} %param.19) | copy-start | bytes 772
  60.2 7.3 %copy-start.7 = (s32[2]{0:T(128)S(1)}, s32[2]{0:T(128)}, u32[]{:S(2)}) copy-start(s32[2]{0:T(128)} %param.20) | copy-start | bytes 28
  66.8 1.9 %collective-permute-start.11 = (bf16[4,224,256]{2,1,0:T(8,128)(2,1)S(1)}, bf16[4,224,256]{2,1,0:T(8,128)(2,1)S(1)}, u32[]{:S(2)}, u32[]{:S(2)}) collective-permute-start(bf16[4,224,256]{2,1,0:T(8,128)(2,1)S(1)} %get-tuple-element.41), channel_id=1, source_target_pairs={{0,1},{1,0},{2,3},{3,2},{4,5},{5,4},{6,7},{7,6},{8,9},{9,8},{10,11... | collective-permute-start | bytes 1376264 | tf_op jit(solution)/shard_map/hidden_sums/ppermute | solution.py:56
  67.3 2.1 %collective-permute-start.10 = (bf16[4,240,256]{2,1,0:T(8,128)(2,1)S(1)}, bf16[4,240,256]{2,1,0:T(8,128)(2,1)S(1)}, u32[]{:S(2)}, u32[]{:S(2)}) collective-permute-start(bf16[4,240,256]{2,1,0:T(8,128)(2,1)S(1)} %get-tuple-element.40), channel_id=1, source_target_pairs={{0,1},{1,0},{2,3},{3,2},{4,5},{5,4},{6,7},{7,6},{8,9},{9,8},{10,11... | collective-permute-start | bytes 1474568 | tf_op jit(solution)/shard_map/hidden_sums/ppermute | solution.py:56
  70.2 6.6 %collective-permute-start.15 = (bf16[240,256]{1,0:T(8,128)(2,1)S(1)}, bf16[240,256]{1,0:T(8,128)(2,1)S(1)}, u32[]{:S(2)}, u32[]{:S(2)}) collective-permute-start(bf16[240,256]{1,0:T(8,128)(2,1)S(1)} %get-tuple-element.48), channel_id=1, source_target_pairs={{0,16},{16,32},{32,48},{48,0},{1,17},{17,33},{33,49},{49,1},{2,18}... | collective-permute-start | bytes 368648 | tf_op jit(solution)/shard_map/hidden_sums/ppermute | solution.py:52
  70.2 7.6 %collective-permute-start.16 = (bf16[240,256]{1,0:T(8,128)(2,1)S(1)}, bf16[240,256]{1,0:T(8,128)(2,1)S(1)}, u32[]{:S(2)}, u32[]{:S(2)}) collective-permute-start(bf16[240,256]{1,0:T(8,128)(2,1)S(1)} %get-tuple-element.49), channel_id=1, source_target_pairs={{0,32},{16,48},{32,0},{48,16},{1,33},{17,49},{33,1},{49,17},{2,34}... | collective-permute-start | bytes 368648 | tf_op jit(solution)/shard_map/hidden_sums/ppermute | solution.py:52
  72.1 6.9 %collective-permute-start.17 = (bf16[240,256]{1,0:T(8,128)(2,1)S(1)}, bf16[240,256]{1,0:T(8,128)(2,1)S(1)}, u32[]{:S(2)}, u32[]{:S(2)}) collective-permute-start(bf16[240,256]{1,0:T(8,128)(2,1)S(1)} %get-tuple-element.50), channel_id=1, source_target_pairs={{0,48},{16,0},{32,16},{48,32},{1,49},{17,1},{33,17},{49,33},{2,50}... | collective-permute-start | bytes 368648 | tf_op jit(solution)/shard_map/hidden_sums/ppermute | solution.py:52
  72.9 10.7 %collective-permute-start.12 = (bf16[224,256]{1,0:T(8,128)(2,1)S(1)}, bf16[224,256]{1,0:T(8,128)(2,1)S(1)}, u32[]{:S(2)}, u32[]{:S(2)}) collective-permute-start(bf16[224,256]{1,0:T(8,128)(2,1)S(1)} %get-tuple-element.44), channel_id=1, source_target_pairs={{0,16},{16,32},{32,48},{48,0},{1,17},{17,33},{33,49},{49,1},{2,18}... | collective-permute-start | bytes 344072 | tf_op jit(solution)/shard_map/hidden_sums/ppermute | solution.py:52
  73.6 10.0 %collective-permute-start.13 = (bf16[224,256]{1,0:T(8,128)(2,1)S(1)}, bf16[224,256]{1,0:T(8,128)(2,1)S(1)}, u32[]{:S(2)}, u32[]{:S(2)}) collective-permute-start(bf16[224,256]{1,0:T(8,128)(2,1)S(1)} %get-tuple-element.45), channel_id=1, source_target_pairs={{0,32},{16,48},{32,0},{48,16},{1,33},{17,49},{33,1},{49,17},{2,34}... | collective-permute-start | bytes 344072 | tf_op jit(solution)/shard_map/hidden_sums/ppermute | solution.py:52
  76.8 6.9 %collective-permute-start.14 = (bf16[224,256]{1,0:T(8,128)(2,1)S(1)}, bf16[224,256]{1,0:T(8,128)(2,1)S(1)}, u32[]{:S(2)}, u32[]{:S(2)}) collective-permute-start(bf16[224,256]{1,0:T(8,128)(2,1)S(1)} %get-tuple-element.46), channel_id=1, source_target_pairs={{0,48},{16,0},{32,16},{48,32},{1,49},{17,1},{33,17},{49,33},{2,50}... | collective-permute-start | bytes 344072 | tf_op jit(solution)/shard_map/hidden_sums/ppermute | solution.py:52
  79.0 4.7 %collective-permute-start.18 = (bf16[240,256]{1,0:T(8,128)(2,1)S(1)}, bf16[240,256]{1,0:T(8,128)(2,1)S(1)}, u32[]{:S(2)}, u32[]{:S(2)}) collective-permute-start(bf16[240,256]{1,0:T(8,128)(2,1)S(1)} %get-tuple-element.52), channel_id=1, source_target_pairs={{0,2},{1,3},{2,0},{3,1},{4,6},{5,7},{6,4},{7,5},{8,10},{9,11},{10,... | collective-permute-start | bytes 368648 | tf_op jit(solution)/shard_map/hidden_sums/ppermute | solution.py:416
  83.8 13.1 %collective-permute-start.21 = (bf16[240,256]{1,0:T(8,128)(2,1)S(1)}, bf16[240,256]{1,0:T(8,128)(2,1)S(1)}, u32[]{:S(2)}, u32[]{:S(2)}) collective-permute-start(bf16[240,256]{1,0:T(8,128)(2,1)S(1)} %get-tuple-element.56), channel_id=1, source_target_pairs={{0,12},{1,13},{2,14},{3,15},{4,0},{5,1},{6,2},{7,3},{8,4},{9,5},{1... | collective-permute-start | bytes 368648 | tf_op jit(solution)/shard_map/hidden_sums/ppermute | solution.py:52
  86.0 11.0 %collective-permute-start.20 = (bf16[240,256]{1,0:T(8,128)(2,1)S(1)}, bf16[240,256]{1,0:T(8,128)(2,1)S(1)}, u32[]{:S(2)}, u32[]{:S(2)}) collective-permute-start(bf16[240,256]{1,0:T(8,128)(2,1)S(1)} %get-tuple-element.56), channel_id=1, source_target_pairs={{0,8},{1,9},{2,10},{3,11},{4,12},{5,13},{6,14},{7,15},{8,0},{9,1},... | collective-permute-start | bytes 368648 | tf_op jit(solution)/shard_map/hidden_sums/ppermute | solution.py:52
  87.2 9.8 %collective-permute-start.19 = (bf16[240,256]{1,0:T(8,128)(2,1)S(1)}, bf16[240,256]{1,0:T(8,128)(2,1)S(1)}, u32[]{:S(2)}, u32[]{:S(2)}) collective-permute-start(bf16[240,256]{1,0:T(8,128)(2,1)S(1)} %get-tuple-element.56), channel_id=1, source_target_pairs={{0,4},{1,5},{2,6},{3,7},{4,8},{5,9},{6,10},{7,11},{8,12},{9,13},{1... | collective-permute-start | bytes 368648 | tf_op jit(solution)/shard_map/hidden_sums/ppermute | solution.py:52
  90.6 3.1 %copy-start = (bf16[4096,896]{1,0:T(8,128)(2,1)S(1)}, bf16[4096,896]{1,0:T(8,128)(2,1)}, u32[]{:S(2)}) copy-start(bf16[4096,896]{1,0:T(8,128)(2,1)} %decoder.1) | copy-start | bytes 22020100
  97.7 7.5 %collective-permute-start.22 = (bf16[224,256]{1,0:T(8,128)(2,1)S(1)}, bf16[224,256]{1,0:T(8,128)(2,1)S(1)}, u32[]{:S(2)}, u32[]{:S(2)}) collective-permute-start(bf16[224,256]{1,0:T(8,128)(2,1)S(1)} %get-tuple-element.59.g0), channel_id=1, source_target_pairs={{0,2},{1,3},{2,0},{3,1},{4,6},{5,7},{6,4},{7,5},{8,10},{9,11},{10,... | collective-permute-start | bytes 344072 | tf_op jit(solution)/shard_map/decode/ppermute | solution.py:455
  102.7 4.1 %collective-permute-start.23 = (bf16[224,256]{1,0:T(8,128)(2,1)S(1)}, bf16[224,256]{1,0:T(8,128)(2,1)S(1)}, u32[]{:S(2)}, u32[]{:S(2)}) collective-permute-start(bf16[224,256]{1,0:T(8,128)(2,1)S(1)} %get-tuple-element.59.g0), channel_id=1, source_target_pairs={{0,1},{1,0},{2,3},{3,2},{4,5},{5,4},{6,7},{7,6},{8,9},{9,8},{10,11... | collective-permute-start | bytes 344072 | tf_op jit(solution)/shard_map/decode/ppermute | solution.py:56
  105.2 2.6 %collective-permute-start.24 = (bf16[224,256]{1,0:T(8,128)(2,1)S(1)}, bf16[224,256]{1,0:T(8,128)(2,1)S(1)}, u32[]{:S(2)}, u32[]{:S(2)}) collective-permute-start(bf16[224,256]{1,0:T(8,128)(2,1)S(1)} %collective-permute-done.22.g1), channel_id=1, source_target_pairs={{0,1},{1,0},{2,3},{3,2},{4,5},{5,4},{6,7},{7,6},{8,9},{9,8},{10,11... | collective-permute-start | bytes 344072 | tf_op jit(solution)/shard_map/decode/ppermute | solution.py:56
  107.8 29.0 %copy-start.2 = (bf16[4,4096]{1,0:T(4,128)(2,1)S(1)}, bf16[4,4096]{1,0:T(4,128)(2,1)}, u32[]{:S(2)}) copy-start(bf16[4,4096]{1,0:T(4,128)(2,1)} %acts.1) | copy-start | bytes 98308
  109.8 6.6 %collective-permute-start.25 = (bf16[64,1152]{1,0:T(8,128)(2,1)S(1)}, bf16[64,1152]{1,0:T(8,128)(2,1)S(1)}, u32[]{:S(2)}, u32[]{:S(2)}) collective-permute-start(bf16[64,1152]{1,0:T(8,128)(2,1)S(1)} %get-tuple-element.63), channel_id=1, source_target_pairs={{0,16},{16,32},{32,48},{48,0},{1,17},{17,33},{33,49},{49,1},{2,18}... | collective-permute-start | bytes 442376 | tf_op jit(solution)/shard_map/decode/ppermute | solution.py:52
  112.2 8.4 %collective-permute-start.26 = (bf16[64,1152]{1,0:T(8,128)(2,1)S(1)}, bf16[64,1152]{1,0:T(8,128)(2,1)S(1)}, u32[]{:S(2)}, u32[]{:S(2)}) collective-permute-start(bf16[64,1152]{1,0:T(8,128)(2,1)S(1)} %get-tuple-element.64), channel_id=1, source_target_pairs={{0,32},{16,48},{32,0},{48,16},{1,33},{17,49},{33,1},{49,17},{2,34}... | collective-permute-start | bytes 442376 | tf_op jit(solution)/shard_map/decode/ppermute | solution.py:52
  113.9 6.8 %collective-permute-start.27 = (bf16[64,1152]{1,0:T(8,128)(2,1)S(1)}, bf16[64,1152]{1,0:T(8,128)(2,1)S(1)}, u32[]{:S(2)}, u32[]{:S(2)}) collective-permute-start(bf16[64,1152]{1,0:T(8,128)(2,1)S(1)} %get-tuple-element.65), channel_id=1, source_target_pairs={{0,48},{16,0},{32,16},{48,32},{1,49},{17,1},{33,17},{49,33},{2,50}... | collective-permute-start | bytes 442376 | tf_op jit(solution)/shard_map/decode/ppermute | solution.py:52
  121.6 15.2 %all-to-all-start = ((bf16[16,4,1152]{2,1,0:T(4,128)(2,1)}), bf16[16,4,1152]{2,1,0:T(4,128)(2,1)S(1)}, u32[]{:S(2)}, u32[]{:S(2)}) async-start(bf16[16,4,1152]{2,1,0:T(4,128)(2,1)} %reshape.108), calls=%async_computation | async-start | bytes 294912 | tf_op jit(solution)/shard_map/scores/all_to_all | solution.py:475
